TPU v7x, 32 devices: a whole 2x2x4 slice. The times are simulated.
32 devices in a mesh: ctx: 8 (over z, x), head: 4 (over y, core).
Axes of the slice: x: 2, y: 2, z: 4, core: 2. Of those that a mesh axis runs over, the one named last changes fastest.
Arguments:
- query_proj: bfloat16 [1024, 4096], P('ctx', 'head'), may hold values from -6 to 6
- key_proj: bfloat16 [1024, 4096], P('ctx', 'head'), may hold values from -0.375 to 0.375
- value_proj: bfloat16 [1024, 8192], P('ctx', 'head'), may hold values from -6 to 6
- gate_proj: bfloat16 [1024, 8192], P('ctx', 'head'), may hold values from -6 to 6
- decay_log: float32 [16, 1024], P('head', 'ctx'), may hold values from -1 to 0
- out_weight: bfloat16 [8192, 4096], P('head'), may hold values from -0.0625 to 0.0625
Outputs:
- layer_out: bfloat16 [1024, 4096], P(('ctx', 'head'))
All inputs are finite; a program needn't handle non-finite values.
Results may differ from a plain program's by a relative error of at most 0.023.
Values may be sent and summed in bfloat16 or wider, within the bound.
No kernel may reach another device: no remote copies, remote signals or barrier semaphores. Data moves between devices by JAX's collectives and lax.ppermute only.
A program may use at most 128 MiB of HBM per device.

v0:
```python
import jax
import jax.numpy as jnp
from jax import lax
from jax.sharding import PartitionSpec as P


def carried_in(value, axis, join, neutral):
    count, mine = (lax.axis_size(axis), lax.axis_index(axis))
    pieces = jax.tree.map(lambda part: lax.all_gather(part, axis), value)
    total = jax.tree.map(
        lambda part, zero: jnp.full_like(part, 0) + jnp.asarray(zero, part.dtype), value, neutral
    )

    def lap(position, total):
        longer = join(total, jax.tree.map(lambda part: part[position], pieces))
        return jax.tree.map(lambda new, old: jnp.where(position < mine, new, old), longer, total)

    return lax.fori_loop(0, count - 1, lap, total)


def combine(earlier_part, later_part):
    return (
        earlier_part[0] * later_part[1][:, None, None] + later_part[0],
        earlier_part[1] * later_part[1],
    )


def local(query_proj, key_proj, value_proj, gate_proj, decay_log, out_weight):
    row_count = query_proj.shape[0]
    heads_here = decay_log.shape[0]
    key_dim = query_proj.shape[1] // heads_here
    value_dim = value_proj.shape[1] // heads_here
    local_sum = jnp.cumsum(decay_log, axis=1)
    token_positions = jnp.arange(row_count)
    causal = token_positions[:, None] >= token_positions[None, :]
    state_list = []
    for which in range(heads_here):
        key_rows = key_proj[:, which * key_dim : (which + 1) * key_dim]
        value_rows = value_proj[:, which * value_dim : (which + 1) * value_dim]
        head_sum = local_sum[which]
        key_scale = jnp.exp(head_sum[-1] - head_sum)[:, None]
        keyed_rows = (key_rows.astype(jnp.float32) * key_scale).astype(jnp.bfloat16)
        state_list.append(
            jnp.einsum("ct,cd->td", keyed_rows, value_rows, preferred_element_type=jnp.float32)
        )
    running_block_state = jnp.stack(state_list, axis=0)
    block_decay = jnp.exp(local_sum[:, -1])
    empty_state = jnp.zeros_like(running_block_state)
    unit_decay = jnp.ones_like(block_decay)
    carried_over_state, _ = carried_in(
        (running_block_state, block_decay), "ctx", combine, (empty_state, unit_decay)
    )
    mixed_list = []
    for which in range(heads_here):
        query_rows = query_proj[:, which * key_dim : (which + 1) * key_dim]
        key_rows = key_proj[:, which * key_dim : (which + 1) * key_dim]
        value_rows = value_proj[:, which * value_dim : (which + 1) * value_dim]
        gate_rows = gate_proj[:, which * value_dim : (which + 1) * value_dim]
        head_sum = local_sum[which]
        gap_matrix = head_sum[:, None] - head_sum[None, :]
        decay_table = jnp.where(causal, jnp.exp(jnp.where(causal, gap_matrix, 0.0)), 0.0)
        scores = jnp.einsum("tk,sk->ts", query_rows, key_rows, preferred_element_type=jnp.float32)
        weights = (scores * decay_table).astype(jnp.bfloat16)
        inner_part = jnp.dot(weights, value_rows, preferred_element_type=jnp.float32)
        scaled_query_rows = query_rows.astype(jnp.float32) * jnp.exp(head_sum)[:, None]
        carried_term = jnp.dot(
            scaled_query_rows, carried_over_state[which], precision=lax.Precision.HIGHEST
        )
        retained = inner_part + carried_term
        row_mean = jnp.mean(retained, axis=1, keepdims=True)
        centered = retained - row_mean
        row_var = jnp.mean(centered * centered, axis=1, keepdims=True)
        normed = centered * lax.rsqrt(row_var + 1e-05)
        mixed_list.append(
            (normed * jax.nn.silu(gate_rows.astype(jnp.float32))).astype(jnp.bfloat16)
        )
    if heads_here == 1:
        mixed_rows = mixed_list[0]
    else:
        mixed_rows = jnp.concatenate(mixed_list, axis=1)
    partial_value = jnp.dot(mixed_rows, out_weight, preferred_element_type=jnp.float32)
    return lax.psum_scatter(
        partial_value.astype(jnp.bfloat16), "head", scatter_dimension=0, tiled=True
    )


def solution(mesh):
    in_specs = (
        P("ctx", "head"),
        P("ctx", "head"),
        P("ctx", "head"),
        P("ctx", "head"),
        P("head", "ctx"),
        P("head", None),
    )
    out_specs = P(("ctx", "head"), None)
    return jax.shard_map(local, mesh=mesh, in_specs=in_specs, out_specs=out_specs, check_vma=False)
```

profile of v0, /device:TPU:0, one launch (start us, length us, event | category | flops | bytes accessed | tf_op | source)
XLA Modules:
  0.0 310.5 jit_solution(4118211647126247913)
XLA Ops:
  6.5 1.1 reduce_window_sum.11
  7.6 0.7 fusion.129
  8.3 2.5 fusion.125
  10.8 1.3 convolution_bitcast_fusion
  12.1 1.3 convolution_bitcast_fusion.1
  13.3 1.3 convolution_bitcast_fusion.2
  15.0 1.5 pad_maximum_fusion
  18.8 23.4 %all-reduce = f32[32]{0:T(128)S(1)} all-reduce(f32[32]{0:T(128)S(1)} %dynamic-update-slice), channel_id=2, replica_groups=mesh['ctx'=8,'head'=4] {'ctx'}, use_global_device_ids=true, to_apply=%add | all-reduce | flops 32 | bytes 256
  42.3 1.0 fusion.6
  43.7 1.2 fusion.8
  44.9 1.2 fusion.7
  46.1 201.1 %all-gather.4.cloned.1.call-done = f32[32,256,512]{2,1,0:T(8,128)} async-done(((f32[4,256,512]{2,1,0:T(8,128)}), f32[32,256,512]{2,1,0:T(8,128)}) %all-gather.4.cloned.1.call-update) | async-done | bytes 16777232 | tf_op jit(solution)/shard_map/all_gather | solution.py:9
  247.1 18.7 %while.14 = (s32[]{:T(128)}, f32[4,256,512]{2,1,0:T(8,128)S(1)}, s32[]{:T(128)}, f32[8,4]{1,0:T(8,128)S(1)}, f32[8,4,256,512]{3,2,1,0:T(8,128)}, /*index=5*/s32[]{:T(128)}, s32[]{:T(128)}) while((s32[]{:T(128)}, f32[4,256,512]{2,1,0:T(8,128)S(1)}, s32[]{:T(128)}, f32[8,4]{1,0:T(8,128)S(1)}, f32[8,4,256,512]{3,2,1,0:T(8,128)}, ...), condition=%wide.region_2.3_spmd.clone, body=%wide.region_1.2_spmd.clone.sunk | while | flops 2097156 | bytes 6291609 | solution.py:18
  247.1 2.7 fusion.136
  249.8 2.6 fusion.136
  252.5 2.6 fusion.136
  255.2 2.6 fusion.136
  257.8 2.6 fusion.136
  260.5 2.6 fusion.136
  263.2 2.6 fusion.136
  265.8 1.4 fusion.133
  267.3 1.4 fusion.132
  271.0 9.4 %convolution_convert_fusion = bf16[128,4096]{1,0:T(8,128)(2,1)} fusion(bf16[2048,4096]{1,0:T(8,128)(2,1)} %param.13, bf16[128,512]{1,0:T(8,128)(2,1)S(1)} %get-tuple-element.130, bf16[128,512]{1,0:T(8,128)(2,1)S(1)} %get-tuple-element.131, bf16[128,512]{1,0:T(8,128)(2,1)S(1)} %get-tuple-element.129, bf16[128,512]{1,0:T(8,128)(2,1)S(1)} %get-tuple-element.128), kind=kOutput, calls=%fused_computation.3 | convolution fusion | flops 2150105088 | bytes 18350080 | tf_op jit(solution)/shard_map/dot_general | solution.py:81
  280.4 23.2 %reduce-scatter.2.cloned.1.call-done = bf16[32,4096]{1,0:T(8,128)(2,1)} async-done(((bf16[128,4096]{1,0:T(8,128)(2,1)}), bf16[32,4096]{1,0:T(8,128)(2,1)}) %reduce-scatter.2.cloned.1.call-update) | async-done | bytes 262160 | tf_op jit(solution)/shard_map/reduce_scatter | solution.py:82
  (47 shorter events, 4.7 us)
Async XLA Ops:
  6.5 8.1 %copy-start = (bf16[128,2048]{1,0:T(8,128)(2,1)S(1)}, bf16[128,2048]{1,0:T(8,128)(2,1)}, u32[]{:S(2)}) copy-start(bf16[128,2048]{1,0:T(8,128)(2,1)} %param.10) | copy-start | bytes 1572868
  6.5 8.1 %copy-start.2 = (bf16[128,1024]{1,0:T(8,128)(2,1)S(1)}, bf16[128,1024]{1,0:T(8,128)(2,1)}, u32[]{:S(2)}) copy-start(bf16[128,1024]{1,0:T(8,128)(2,1)} %param.9) | copy-start | bytes 786436
  6.5 240.6 %all-gather.4.cloned.1.call-start = ((), (), s32[]{:S(2)}) async-start(), calls=%async_computation.2 | async-start | bytes 18874368 | tf_op jit(solution)/shard_map/all_gather | solution.py:9
  16.5 0.7 copy-start.6
  16.5 25.8 %copy-start.3 = (bf16[128,1024]{1,0:T(8,128)(2,1)S(1)}, bf16[128,1024]{1,0:T(8,128)(2,1)}, u32[]{:S(2)}) copy-start(bf16[128,1024]{1,0:T(8,128)(2,1)} %param.8) | copy-start | bytes 786436
  16.5 287.1 %reduce-scatter.2.cloned.1.call-start = ((), (), s32[]{:S(2)}) async-start(), calls=%async_computation.1 | async-start | bytes 1310720 | tf_op jit(solution)/shard_map/reduce_scatter | solution.py:82
  247.1 18.7 %copy-start.1 = (f32[128,512]{1,0:T(8,128)S(1)}, f32[128,512]{1,0:T(8,128)}, u32[]{:S(2)}) copy-start(f32[128,512]{1,0:T(8,128)} %fusion.6) | copy-start | bytes 786436
  265.8 2.9 copy-start.4
  267.3 3.3 %copy-start.5 = (bf16[128,2048]{1,0:T(8,128)(2,1)S(1)}, bf16[128,2048]{1,0:T(8,128)(2,1)}, u32[]{:S(2)}) copy-start(bf16[128,2048]{1,0:T(8,128)(2,1)} %param.11) | copy-start | bytes 1572868
Sparse Core Ops, SparseCore 0:
  16.6 230.4 all-gather.3
  280.5 23.0 reduce-scatter.1
where the time goes:
time: 311 us; the launch traced here: 310 us
  waiting for transfers between devices  224 us (72%)
  other arithmetic  24.7 us (8%)
  blocking collectives  23.4 us (8%)
  matrix products  21.1 us (7%)
  between operations  14.3 us (5%)
    all_gather x1, waiting for transfers between devices, carried_in(): pieces = jax.tree.map(lambda part: lax.all_gather(part, axis), value)  201 us
    unnamed x1, blocking collectives  23.4 us
    reduce_scatter x1, waiting for transfers between devices, local(): lax.psum_scatter(partial_value.astype(jnp.bfloat16), 'head', scatter_dime...  23.2 us
    select_n x7, other arithmetic, lap(): jnp.where(position < mine, new, old)  18.4 us
    dot_general x1, matrix products, local(): jnp.dot(mixed_rows, out_weight, preferred_element_type=jnp.float32)  9.43 us
  transfers between devices with their start and end apart: 2, of which 2 were waited for; matrix products, arithmetic and copies ran while one was open for 2% of the time, Pallas kernels for 0%

commit v1 on v0

v1 whole, which is shorter than its diff:
```python
import functools
import jax
import jax.numpy as jnp
from jax import lax
from jax.experimental import pallas as pl
from jax.experimental.pallas import tpu as pltpu
from jax.sharding import PartitionSpec as P

F32 = jnp.float32
BF16 = jnp.bfloat16
TAIL = 16
SMEM = pl.BlockSpec(memory_space=pltpu.SMEM)
VMEM = pl.BlockSpec(memory_space=pltpu.VMEM)


def params(mib):
    return pltpu.CompilerParams(vmem_limit_bytes=mib * 2**20)


def cost(flops, bytes_accessed):
    return pl.CostEstimate(flops=flops, bytes_accessed=bytes_accessed, transcendentals=0)


def iotas(rows):
    down = lax.broadcasted_iota(jnp.int32, (rows, rows), 0)
    across = lax.broadcasted_iota(jnp.int32, (rows, rows), 1)
    return down, across


def lanes(ref, index, width):
    return ref[:, pl.ds(pl.multiple_of(index * width, width), width)]


def pack_kernel(place_ref, decay_ref, key_ref, value_ref, *out_refs, key_dim, value_dim):
    rows = key_ref.shape[0]
    down, across = iotas(rows)
    for hop, out_ref in enumerate(out_refs):
        head = place_ref[0] ^ hop
        decay = decay_ref[pl.ds(head, 1), :]
        after = jnp.sum(jnp.where(across > down, decay, 0.0), axis=1, keepdims=True)
        keyed = lanes(key_ref, head, key_dim).astype(F32) * jnp.exp(after)
        out_ref[0:rows, :] = keyed.astype(BF16)
        values = lanes(value_ref, head, value_dim)
        for piece in range(value_dim // key_dim):
            out_ref[(piece + 1) * rows : (piece + 2) * rows, :] = values[
                :, piece * key_dim : (piece + 1) * key_dim
            ]
        whole = jnp.exp(jnp.sum(decay, axis=1, keepdims=True))
        whole = jnp.broadcast_to(whole, (TAIL, key_dim))
        high = whole.astype(BF16).astype(F32)
        middle = (whole - high).astype(BF16).astype(F32)
        low = whole - high - middle
        row = lax.broadcasted_iota(jnp.int32, (TAIL, key_dim), 0)
        tail = jnp.where(row == 0, high, jnp.where(row == 1, middle, jnp.where(row == 2, low, 0.0)))
        out_ref[out_ref.shape[0] - TAIL :, :] = tail.astype(BF16)


def query_kernel(place_ref, decay_ref, query_ref, *out_refs, key_dim):
    rows = query_ref.shape[0]
    down, across = iotas(rows)
    for hop, out_ref in enumerate(out_refs):
        head = place_ref[0] ^ hop
        decay = decay_ref[pl.ds(head, 1), :]
        upto = jnp.sum(jnp.where(across <= down, decay, 0.0), axis=1, keepdims=True)
        out_ref[...] = (lanes(query_ref, head, key_dim).astype(F32) * jnp.exp(upto)).astype(BF16)


def block_decay(message_ref):
    tail = message_ref[message_ref.shape[0] - TAIL :, :].astype(F32)
    return tail[0:1] + tail[1:2] + tail[2:3]


def block_state(message_ref, rows, piece):
    return lax.dot_general(
        message_ref[0:rows, :],
        message_ref[(piece + 1) * rows : (piece + 2) * rows, :],
        (((0,), (0,)), ((), ())),
        preferred_element_type=F32,
    )


def state_kernel(place_ref, *refs, rows):
    messages, (state_ref, whole_ref) = refs[:-2], refs[-2:]
    key_dim = messages[0].shape[1]
    place = place_ref[0]
    decays = [block_decay(message) for message in messages]
    scales = []
    for hop in range(len(messages)):
        scale = jnp.ones((1, key_dim), F32)
        for other in range(len(messages)):
            if other != hop:
                scale = scale * jnp.where((place ^ other) > (place ^ hop), decays[other], 1.0)
        scales.append(scale)
    for piece in range(state_ref.shape[1] // key_dim):
        total = None
        for hop, message in enumerate(messages):
            term = block_state(message, rows, piece) * scales[hop]
            total = term if total is None else total + term
        state_ref[:, piece * key_dim : (piece + 1) * key_dim] = total.astype(state_ref.dtype)
    whole = decays[0]
    for decay in decays[1:]:
        whole = whole * decay
    whole_ref[...] = jnp.broadcast_to(whole, whole_ref.shape)


def group_kernel(place_ref, *refs, rows):
    count = (len(refs) - 5) // 2
    messages, queries = refs[:count], refs[count : 2 * count]
    part_ref, scaled_ref, states, earlier, decays = refs[2 * count :]
    key_dim = messages[0].shape[1]
    pieces = part_ref.shape[1] // key_dim
    place = place_ref[0]
    for hop, message in enumerate(messages):
        decays[place ^ hop] = jnp.broadcast_to(block_decay(message), decays.shape[1:])
        for piece in range(pieces):
            states[place ^ hop, :, piece * key_dim : (piece + 1) * key_dim] = block_state(message, rows, piece)
    whole = jnp.ones((1, key_dim), F32)
    for block in range(count):
        if block == 0:
            earlier[0] = jnp.zeros(earlier.shape[1:], BF16)
        elif block == 1:
            total = states[0]
            earlier[1] = total.astype(BF16)
        else:
            total = total * jnp.concatenate([decay] * pieces, axis=1) + states[block - 1]
            earlier[block] = total.astype(BF16)
        decay = decays[block][0:1]
        decays[block] = jnp.broadcast_to(whole, decays.shape[1:])
        whole = whole * decay
    for hop, query in enumerate(queries):
        block = place ^ hop
        part_ref[hop * rows : (hop + 1) * rows, :] = jnp.dot(
            query[...], earlier[block], preferred_element_type=F32
        )
        scaled_ref[hop * rows : (hop + 1) * rows, :] = (query[...].astype(F32) * decays[block][0:1]).astype(BF16)


def cross_kernel(state_ref, scaled_ref, part_ref, *out_refs):
    rows = out_refs[0].shape[0]
    total = part_ref[...] + jnp.dot(scaled_ref[...], state_ref[...], preferred_element_type=F32)
    for hop, out_ref in enumerate(out_refs):
        out_ref[...] = total[hop * rows : (hop + 1) * rows, :].astype(BF16)


def inner_kernel(decay_ref, query_ref, key_ref, value_ref, gate_ref, inner_ref, swish_ref, *, key_dim, value_dim):
    rows = query_ref.shape[0]
    down, across = iotas(rows)
    for head in range(decay_ref.shape[0]):
        decay = decay_ref[head : head + 1, :]
        column = jnp.sum(jnp.where(across <= down, decay, 0.0), axis=1, keepdims=True)
        diagonal = jnp.where(across == down, column, 0.0)
        line = jnp.sum(diagonal, axis=0, keepdims=True)
        causal = across <= down
        table = jnp.where(causal, jnp.exp(jnp.where(causal, column - line, 0.0)), 0.0)
        keys = slice(head * key_dim, (head + 1) * key_dim)
        features = slice(head * value_dim, (head + 1) * value_dim)
        scores = lax.dot_general(
            query_ref[:, keys], key_ref[:, keys], (((1,), (1,)), ((), ())), preferred_element_type=F32
        )
        inner_ref[:, features] = jnp.dot(
            (scores * table).astype(BF16), value_ref[:, features], preferred_element_type=F32
        )
        gate = gate_ref[:, features].astype(F32)
        swish_ref[:, features] = gate / (1.0 + jnp.exp(-gate))


def project_kernel(place_ref, inner_ref, swish_ref, *refs, owners):
    weight_ref, send_ref, keep_ref, mixed, left = refs[-5:]
    parts = refs[:-5]
    rows, value_dim = parts[0].shape
    half = send_ref.shape[0]

    @pl.when(pl.program_id(0) == 0)
    def _():
        place, owner = place_ref[0], place_ref[1]
        for hop, part in enumerate(parts):
            head = place ^ hop
            retained = lanes(inner_ref, head, value_dim) + part[...].astype(F32)
            mean = jnp.mean(retained, axis=1, keepdims=True)
            centered = retained - mean
            variance = jnp.mean(centered * centered, axis=1, keepdims=True)
            mixed[:, pl.ds(pl.multiple_of(head * value_dim, value_dim), value_dim)] = (
                centered * lax.rsqrt(variance + 1e-05) * lanes(swish_ref, head, value_dim)
            )
        share = rows // owners
        bits = owners.bit_length() - 1
        pieces = []
        for position in range(owners):
            flipped = owners - 1 - position
            mask = sum(((flipped >> bit) & 1) << (bits - 1 - bit) for bit in range(bits))
            start = pl.multiple_of((owner ^ mask) * share, share)
            pieces.append(mixed[pl.ds(start, share), :])
        left[...] = jnp.concatenate(pieces, axis=0).astype(BF16)

    out = jnp.dot(left[...], weight_ref[...], preferred_element_type=F32)
    send_ref[...] = out[:half].astype(BF16)
    keep_ref[...] = out[half:].astype(BF16)


def swap(value, axis, size, mask):
    return lax.ppermute(value, axis, [(i, i ^ mask) for i in range(size)])


def carried_into(state, whole, axis, size, group):
    def shift(value, by):
        return lax.ppermute(value, axis, [(i, i + by * group) for i in range(size - by * group)])

    groups = size // group
    if groups == 1:
        return jnp.zeros_like(state)
    got = shift(state, 1)
    if groups == 2:
        return got
    first = lax.axis_index(axis) < group
    total, product = got.astype(F32), jnp.where(first, 1.0, shift(whole, 1))
    by = 1
    pieces = state.shape[1] // whole.shape[1]
    while by < groups - 1:
        none = lax.axis_index(axis) < by * group
        earlier, before = shift(total.astype(BF16), by), jnp.where(none, 1.0, shift(product, by))
        total = total + jnp.tile(product[0:1], (1, pieces)) * earlier.astype(F32)
        product = product * before
        by *= 2
    return total.astype(BF16)


def local(query, key, value, gate, decay, weight, *, ctx, head):
    rows = query.shape[0]
    heads = decay.shape[0]
    key_dim = query.shape[1] // heads
    value_dim = value.shape[1] // heads
    width = weight.shape[1]
    group = heads
    me = lax.axis_index("ctx")
    place = (me % group).astype(jnp.int32).reshape(1)
    both = jnp.stack([me % group, lax.axis_index("head")]).astype(jnp.int32)

    message = jax.ShapeDtypeStruct((rows * (1 + value_dim // key_dim) + TAIL, key_dim), BF16)
    messages = pl.pallas_call(
        functools.partial(pack_kernel, key_dim=key_dim, value_dim=value_dim),
        out_shape=[message] * group,
        in_specs=[SMEM, VMEM, VMEM, VMEM],
        out_specs=[VMEM] * group,
        compiler_params=params(16),
        name="pack_keys_values",
    )(place, decay, key, value)
    messages = [messages[0]] + [swap(messages[hop], "ctx", ctx, hop) for hop in range(1, group)]

    state, whole = pl.pallas_call(
        functools.partial(state_kernel, rows=rows),
        out_shape=[
            jax.ShapeDtypeStruct((key_dim, value_dim), BF16),
            jax.ShapeDtypeStruct((8, key_dim), F32),
        ],
        in_specs=[SMEM] + [VMEM] * group,
        out_specs=[VMEM] * 2,
        compiler_params=params(16),
        name="group_state",
    )(place, *messages)
    carried = carried_into(state, whole, "ctx", ctx, group)

    query_after, _ = lax.optimization_barrier((query, state))
    queries = pl.pallas_call(
        functools.partial(query_kernel, key_dim=key_dim),
        out_shape=[jax.ShapeDtypeStruct((rows, key_dim), BF16)] * group,
        in_specs=[SMEM, VMEM, VMEM],
        out_specs=[VMEM] * group,
        compiler_params=params(16),
        name="pack_queries",
    )(place, decay, query_after)
    queries = [queries[0]] + [swap(queries[hop], "ctx", ctx, hop) for hop in range(1, group)]

    inner, swish = pl.pallas_call(
        functools.partial(inner_kernel, key_dim=key_dim, value_dim=value_dim),
        out_shape=[jax.ShapeDtypeStruct(value.shape, F32)] * 2,
        in_specs=[VMEM] * 5,
        out_specs=[VMEM] * 2,
        compiler_params=params(24),
        cost_estimate=cost(10**9, 4 * 2**20),
        name="block_part",
    )(decay, query_after, key, value, gate)

    part, scaled = pl.pallas_call(
        functools.partial(group_kernel, rows=rows),
        out_shape=[
            jax.ShapeDtypeStruct((group * rows, value_dim), F32),
            jax.ShapeDtypeStruct((group * rows, key_dim), BF16),
        ],
        in_specs=[SMEM] + [VMEM] * (2 * group),
        out_specs=[VMEM] * 2,
        scratch_shapes=[
            pltpu.VMEM((group, key_dim, value_dim), F32),
            pltpu.VMEM((group, key_dim, value_dim), BF16),
            pltpu.VMEM((group, 8, key_dim), F32),
        ],
        compiler_params=params(24),
        cost_estimate=cost(10**9, 4 * 2**20),
        name="group_part",
    )(place, *messages, *queries)

    parts = pl.pallas_call(
        cross_kernel,
        out_shape=[jax.ShapeDtypeStruct((rows, value_dim), BF16)] * group,
        in_specs=[VMEM] * 3,
        out_specs=[VMEM] * group,
        compiler_params=params(16),
        name="carried_part",
    )(carried, scaled, part)
    parts = [parts[0]] + [swap(parts[hop], "ctx", ctx, hop) for hop in range(1, group)]

    tile = 512
    half = rows // 2
    fixed = lambda i: (0, 0)
    send, keep = pl.pallas_call(
        functools.partial(project_kernel, owners=head),
        out_shape=[jax.ShapeDtypeStruct((half, width), BF16)] * 2,
        grid=(width // tile,),
        in_specs=[SMEM]
        + [pl.BlockSpec(value.shape, fixed)] * 2
        + [pl.BlockSpec((rows, value_dim), fixed)] * group
        + [pl.BlockSpec((weight.shape[0], tile), lambda i: (0, i))],
        out_specs=[pl.BlockSpec((half, tile), lambda i: (0, i))] * 2,
        scratch_shapes=[pltpu.VMEM(value.shape, F32), pltpu.VMEM(value.shape, BF16)],
        compiler_params=params(40),
        name="project",
    )(both, inner, swish, *parts, weight)

    mask = 1
    while mask < head:
        total = keep.astype(F32) + swap(send, "head", head, mask).astype(F32)
        half = total.shape[0] // 2
        send, keep = total[:half].astype(BF16), total[half:]
        mask *= 2
        if mask >= head:
            return total.astype(BF16)


def solution(mesh):
    in_specs = (
        P("ctx", "head"),
        P("ctx", "head"),
        P("ctx", "head"),
        P("ctx", "head"),
        P("head", "ctx"),
        P("head", None),
    )
    out_specs = P(("ctx", "head"), None)
    body = functools.partial(local, ctx=mesh.shape["ctx"], head=mesh.shape["head"])
    return jax.shard_map(body, mesh=mesh, in_specs=in_specs, out_specs=out_specs, check_vma=False)
```

time: 311 us -> 64.4 us (0.21)
  waiting for transfers between devices: 224 us -> 22.6 us
  other arithmetic: 24.7 us -> 0.94 us
  blocking collectives: 23.4 us -> 0 us
  matrix products: 21.1 us -> 0 us
  starting transfers between devices: 0.04 us -> 18 us
  between operations: 14.3 us -> 0.13 us
  Pallas kernels: 0 us -> 13.2 us
  local copies, waits for them, and re-layouts: 2.39 us -> 8.99 us
    all_gather x1 -> x0, waiting for transfers between devices: 201 us -> none  [carried_in(): pieces = jax.tree.map(lambda part: lax.all_gather(part, axis), value)]
    unnamed x1 -> x0, blocking collectives: 23.4 us -> none
    reduce_scatter x1 -> x0, waiting for transfers between devices: 23.2 us -> none  [local(): lax.psum_scatter(partial_value.astype(jnp.bfloat16), 'head', scatter_dime...]
    ppermute x0 -> x12, waiting for transfers between devices: none -> 22.6 us  [the longest x11 22.6 us: swap(): return lax.ppermute(value, axis, [(i, i ^ mask) for i in range(size)])]
    dot_general x13 -> x0, matrix products: 21.1 us -> none  [the longest x1 9.43 us: local(): jnp.dot(mixed_rows, out_weight, preferred_element_type=jnp.float32)]
    select_n x7 -> x0, other arithmetic: 18.4 us -> none  [lap(): jnp.where(position < mine, new, old)]
    ppermute x0 -> x12, starting transfers between devices: none -> 18 us  [the longest x11 13.3 us: swap(): return lax.ppermute(value, axis, [(i, i ^ mask) for i in range(size)])]
    pallas_call x0 -> x7, Pallas kernels: none -> 13.2 us  [the longest x1 9.8 us: local(): pl.pallas_call(functools.partial(project_kernel, owners=head), out_shape=...]
  transfers between devices with their start and end apart: 2 -> 12, of which waited for: 2 -> 8; matrix products, arithmetic and copies ran while one was open for 2% -> 0% of each run, Pallas kernels for 0% -> 3%
where the time goes in v1:
time: 64.4 us; the launch traced here: 63.9 us
  waiting for transfers between devices  22.6 us (35%)
  starting transfers between devices  18 us (28%)
  Pallas kernels  13.2 us (20%)
  local copies, waits for them, and re-layouts  8.99 us (14%)
  other arithmetic  0.94 us (1%)
    ppermute x11, waiting for transfers between devices, swap(): return lax.ppermute(value, axis, [(i, i ^ mask) for i in range(size)])  22.6 us
    ppermute x11, starting transfers between devices, swap(): return lax.ppermute(value, axis, [(i, i ^ mask) for i in range(size)])  13.3 us
    pallas_call x1, Pallas kernels, local(): pl.pallas_call(functools.partial(project_kernel, owners=head), out_shape=...  9.8 us
    unnamed x20, local copies, waits for them, and re-layouts  8.96 us
    ppermute x1, starting transfers between devices, shift(): lax.ppermute(value, axis, [(i, i + by * group) for i in range(size - by *...  4.66 us
  transfers between devices with their start and end apart: 12, of which 8 were waited for; matrix products, arithmetic and copies ran while one was open for 0% of the time, Pallas kernels for 3%

profile of v1, /device:TPU:0, one launch (start us, length us, event | category | flops | bytes accessed | tf_op | source)
XLA Modules:
  0.0 63.9 jit_solution(4243650212674748208)
XLA Ops:
  0.0 1.0 %copy-done = bf16[128,2048]{1,0:T(8,128)(2,1)S(1)} copy-done((bf16[128,2048]{1,0:T(8,128)(2,1)S(1)}, bf16[128,2048]{1,0:T(8,128)(2,1)}, u32[]{:S(2)}) %copy-start) | copy-done | bytes 524312
  1.0 0.9 %copy-done.4 = bf16[128,1024]{1,0:T(8,128)(2,1)S(1)} copy-done((bf16[128,1024]{1,0:T(8,128)(2,1)S(1)}, bf16[128,1024]{1,0:T(8,128)(2,1)}, u32[]{:S(2)}) %copy-start.4) | copy-done | bytes 262168
  2.8 3.0 %collective-permute-start = (bf16[400,256]{1,0:T(8,128)(2,1)S(1)}, bf16[400,256]{1,0:T(8,128)(2,1)S(1)}, u32[]{:S(2)}, u32[]{:S(2)}) collective-permute-start(bf16[400,256]{1,0:T(8,128)(2,1)S(1)} %get-tuple-element.26), channel_id=1, source_target_pairs={{0,4},{4,0},{8,12},{12,8},{16,20},{20,16},{24,28},{28,24},{1,5},{5... | collective-permute-start | bytes 614408 | tf_op jit(solution)/shard_map/ppermute | solution.py:201
  5.9 1.6 %collective-permute-start.1 = (bf16[400,256]{1,0:T(8,128)(2,1)S(1)}, bf16[400,256]{1,0:T(8,128)(2,1)S(1)}, u32[]{:S(2)}, u32[]{:S(2)}) collective-permute-start(bf16[400,256]{1,0:T(8,128)(2,1)S(1)} %get-tuple-element.27), channel_id=1, source_target_pairs={{0,8},{4,12},{8,0},{12,4},{16,24},{20,28},{24,16},{28,20},{1,9},{5... | collective-permute-start | bytes 614408 | tf_op jit(solution)/shard_map/ppermute | solution.py:201
  7.4 3.5 %collective-permute-done.refs_1_ = bf16[400,256]{1,0:T(8,128)(2,1)S(1)} collective-permute-done((bf16[400,256]{1,0:T(8,128)(2,1)S(1)}, bf16[400,256]{1,0:T(8,128)(2,1)S(1)}, u32[]{:S(2)}, u32[]{:S(2)}) %collective-permute-start) | collective-permute-done | bytes 204832 | tf_op jit(solution)/shard_map/ppermute | solution.py:201
  10.9 2.9 %collective-permute-done.1.refs_2_ = bf16[400,256]{1,0:T(8,128)(2,1)S(1)} collective-permute-done((bf16[400,256]{1,0:T(8,128)(2,1)S(1)}, bf16[400,256]{1,0:T(8,128)(2,1)S(1)}, u32[]{:S(2)}, u32[]{:S(2)}) %collective-permute-start.1) | collective-permute-done | bytes 204832 | tf_op jit(solution)/shard_map/ppermute | solution.py:201
  13.9 2.7 %collective-permute-done.2.refs_3_ = bf16[400,256]{1,0:T(8,128)(2,1)S(1)} collective-permute-done((bf16[400,256]{1,0:T(8,128)(2,1)S(1)}, bf16[400,256]{1,0:T(8,128)(2,1)S(1)}, u32[]{:S(2)}, u32[]{:S(2)}) %collective-permute-start.2) | collective-permute-done | bytes 204832 | tf_op jit(solution)/shard_map/ppermute | solution.py:201
  16.6 1.0 %group_state.1 = (bf16[256,512]{1,0:T(8,128)(2,1)S(1)}, f32[8,256]{1,0:T(8,128)}) custom-call(s32[1]{0:T(128)} %bitcast.place_ref, bf16[400,256]{1,0:T(8,128)(2,1)S(1)} %get-tuple-element.25.refs_0_, bf16[400,256]{1,0:T(8,128)(2,1)S(1)} %collective-permute-done.refs_1_, bf16[400,256]{1,0:T(8,128)(2,1)S(1)} %collective-permute-done.1.refs_2_, ...), custom_call_target="tpu_custom_call" | custom-call | tf_op jit(solution)/shard_map/group_state/pallas_call | solution.py:249
  17.6 4.7 %collective-permute-start.3 = (bf16[256,512]{1,0:T(8,128)(2,1)S(1)}, bf16[256,512]{1,0:T(8,128)(2,1)S(1)}, u32[]{:S(2)}, u32[]{:S(2)}) collective-permute-start(bf16[256,512]{1,0:T(8,128)(2,1)S(1)} %get-tuple-element.29), channel_id=1, source_target_pairs={{0,16},{4,20},{8,24},{12,28},{1,17},{5,21},{9,25},{13,29},{2,18},{... | collective-permute-start | bytes 786440 | tf_op jit(solution)/shard_map/ppermute | solution.py:206
  24.0 1.6 %collective-permute-start.4 = (bf16[128,256]{1,0:T(8,128)(2,1)S(1)}, bf16[128,256]{1,0:T(8,128)(2,1)S(1)}, u32[]{:S(2)}, u32[]{:S(2)}) collective-permute-start(bf16[128,256]{1,0:T(8,128)(2,1)S(1)} %get-tuple-element.34), channel_id=1, source_target_pairs={{0,4},{4,0},{8,12},{12,8},{16,20},{20,16},{24,28},{28,24},{1,5},{5... | collective-permute-start | bytes 196616 | tf_op jit(solution)/shard_map/ppermute | solution.py:201
  25.6 1.6 %collective-permute-start.5 = (bf16[128,256]{1,0:T(8,128)(2,1)S(1)}, bf16[128,256]{1,0:T(8,128)(2,1)S(1)}, u32[]{:S(2)}, u32[]{:S(2)}) collective-permute-start(bf16[128,256]{1,0:T(8,128)(2,1)S(1)} %get-tuple-element.35), channel_id=1, source_target_pairs={{0,8},{4,12},{8,0},{12,4},{16,24},{20,28},{24,16},{28,20},{1,9},{5... | collective-permute-start | bytes 196616 | tf_op jit(solution)/shard_map/ppermute | solution.py:201
  28.4 1.5 %collective-permute-done.5.refs_6_ = bf16[128,256]{1,0:T(8,128)(2,1)S(1)} collective-permute-done((bf16[128,256]{1,0:T(8,128)(2,1)S(1)}, bf16[128,256]{1,0:T(8,128)(2,1)S(1)}, u32[]{:S(2)}, u32[]{:S(2)}) %collective-permute-start.5) | collective-permute-done | bytes 65568 | tf_op jit(solution)/shard_map/ppermute | solution.py:201
  29.9 2.5 %collective-permute-done.6.refs_7_ = bf16[128,256]{1,0:T(8,128)(2,1)S(1)} collective-permute-done((bf16[128,256]{1,0:T(8,128)(2,1)S(1)}, bf16[128,256]{1,0:T(8,128)(2,1)S(1)}, u32[]{:S(2)}, u32[]{:S(2)}) %collective-permute-start.6) | collective-permute-done | bytes 65568 | tf_op jit(solution)/shard_map/ppermute | solution.py:201
  32.3 1.0 %group_part.1 = (f32[512,512]{1,0:T(8,128)S(1)}, bf16[512,256]{1,0:T(8,128)(2,1)S(1)}) custom-call(s32[1]{0:T(128)} %bitcast.place_ref, bf16[400,256]{1,0:T(8,128)(2,1)S(1)} %get-tuple-element.25.refs_0_, bf16[400,256]{1,0:T(8,128)(2,1)S(1)} %collective-permute-done.refs_1_, bf16[400,256]{1,0:T(8,128)(2,1)S(1)} %collective-permute-done.1.refs_2_, ...), custom_call_target="tpu_custom_call" | custom-call | flops 1000000000 | bytes 4194304 | tf_op jit(solution)/shard_map/group_part/pallas_call | solution.py:283
  34.2 1.3 %collective-permute-start.8 = (bf16[128,512]{1,0:T(8,128)(2,1)S(1)}, bf16[128,512]{1,0:T(8,128)(2,1)S(1)}, u32[]{:S(2)}, u32[]{:S(2)}) collective-permute-start(bf16[128,512]{1,0:T(8,128)(2,1)S(1)} %get-tuple-element.41), channel_id=1, source_target_pairs={{0,8},{4,12},{8,0},{12,4},{16,24},{20,28},{24,16},{28,20},{1,9},{5... | collective-permute-start | bytes 393224 | tf_op jit(solution)/shard_map/ppermute | solution.py:201
  35.5 1.7 %collective-permute-start.9 = (bf16[128,512]{1,0:T(8,128)(2,1)S(1)}, bf16[128,512]{1,0:T(8,128)(2,1)S(1)}, u32[]{:S(2)}, u32[]{:S(2)}) collective-permute-start(bf16[128,512]{1,0:T(8,128)(2,1)S(1)} %get-tuple-element.42), channel_id=1, source_target_pairs={{0,12},{4,8},{8,4},{12,0},{16,28},{20,24},{24,20},{28,16},{1,13},{... | collective-permute-start | bytes 393224 | tf_op jit(solution)/shard_map/ppermute | solution.py:201
  37.3 1.0 %copy-done.1 = bf16[128,2048]{1,0:T(8,128)(2,1)S(1)} copy-done((bf16[128,2048]{1,0:T(8,128)(2,1)S(1)}, bf16[128,2048]{1,0:T(8,128)(2,1)}, u32[]{:S(2)}) %copy-start.1) | copy-done | bytes 524312
  38.3 0.9 %copy-done.3 = bf16[128,1024]{1,0:T(8,128)(2,1)S(1)} copy-done((bf16[128,1024]{1,0:T(8,128)(2,1)S(1)}, bf16[128,1024]{1,0:T(8,128)(2,1)}, u32[]{:S(2)}) %copy-start.3) | copy-done | bytes 262168
  39.3 0.9 %copy-done.5 = bf16[128,1024]{1,0:T(8,128)(2,1)S(1)} copy-done((bf16[128,1024]{1,0:T(8,128)(2,1)S(1)}, bf16[128,1024]{1,0:T(8,128)(2,1)}, u32[]{:S(2)}) %copy-start.5) | copy-done | bytes 262168
  40.9 1.0 %copy-done.9 = bf16[128,2048]{1,0:T(8,128)(2,1)S(1)} copy-done((bf16[128,2048]{1,0:T(8,128)(2,1)S(1)}, bf16[128,2048]{1,0:T(8,128)(2,1)}, u32[]{:S(2)}) %copy-start.9) | copy-done | bytes 524312
  42.8 9.8 %project.1 = (bf16[64,4096]{1,0:T(8,128)(2,1)S(1)}, bf16[64,4096]{1,0:T(8,128)(2,1)S(1)}) custom-call(s32[2]{0:T(128)S(1)} %pad_add_fusion.place_ref, f32[128,2048]{1,0:T(8,128)S(1)} %get-tuple-element.31.inner_ref, f32[128,2048]{1,0:T(8,128)S(1)} %get-tuple-element.32.swish_ref, bf16[128,512]{1,0:T(8,128)(2,1)S(1)} %get-tuple-element.39.refs_0_, ...), custom_call_target="tpu_custom_call" | custom-call | tf_op jit(solution)/shard_map/project/pallas_call | solution.py:314
  52.6 1.9 %collective-permute-done.10 = bf16[64,4096]{1,0:T(8,128)(2,1)S(1)} collective-permute-done((bf16[64,4096]{1,0:T(8,128)(2,1)S(1)}, bf16[64,4096]{1,0:T(8,128)(2,1)S(1)}, u32[]{:S(2)}, u32[]{:S(2)}) %collective-permute-start.10) | collective-permute-done | bytes 524320 | tf_op jit(solution)/shard_map/ppermute | solution.py:201
  54.7 1.6 %collective-permute-start.11 = (bf16[32,4096]{1,0:T(8,128)(2,1)S(1)}, bf16[32,4096]{1,0:T(8,128)(2,1)S(1)}, u32[]{:S(2)}, u32[]{:S(2)}) collective-permute-start(bf16[32,4096]{1,0:T(8,128)(2,1)S(1)} %slice.15), channel_id=1, source_target_pairs={{0,2},{1,3},{2,0},{3,1},{4,6},{5,7},{6,4},{7,5},{8,10},{9,11},{10,... | collective-permute-start | bytes 786440 | tf_op jit(solution)/shard_map/ppermute | solution.py:201
  56.3 6.8 %collective-permute-done.11 = bf16[32,4096]{1,0:T(8,128)(2,1)S(1)} collective-permute-done((bf16[32,4096]{1,0:T(8,128)(2,1)S(1)}, bf16[32,4096]{1,0:T(8,128)(2,1)S(1)}, u32[]{:S(2)}, u32[]{:S(2)}) %collective-permute-start.11) | collective-permute-done | bytes 262176 | tf_op jit(solution)/shard_map/ppermute | solution.py:201
  (31 shorter events, 7.2 us)
Async XLA Ops:
  0.0 1.0 %copy-start = (bf16[128,2048]{1,0:T(8,128)(2,1)S(1)}, bf16[128,2048]{1,0:T(8,128)(2,1)}, u32[]{:S(2)}) copy-start(bf16[128,2048]{1,0:T(8,128)(2,1)} %value_ref.3) | copy-start | bytes 1572868
  1.0 0.9 %copy-start.4 = (bf16[128,1024]{1,0:T(8,128)(2,1)S(1)}, bf16[128,1024]{1,0:T(8,128)(2,1)}, u32[]{:S(2)}) copy-start(bf16[128,1024]{1,0:T(8,128)(2,1)} %key_ref.3) | copy-start | bytes 786436
  2.0 0.7 %copy-start.6 = (f32[4,128]{1,0:T(4,128)S(1)}, f32[4,128]{1,0:T(4,128)}, u32[]{:S(2)}) copy-start(f32[4,128]{1,0:T(4,128)} %decay_ref.5) | copy-start | bytes 6148
  2.8 8.1 %collective-permute-start = (bf16[400,256]{1,0:T(8,128)(2,1)S(1)}, bf16[400,256]{1,0:T(8,128)(2,1)S(1)}, u32[]{:S(2)}, u32[]{:S(2)}) collective-permute-start(bf16[400,256]{1,0:T(8,128)(2,1)S(1)} %get-tuple-element.26), channel_id=1, source_target_pairs={{0,4},{4,0},{8,12},{12,8},{16,20},{20,16},{24,28},{28,24},{1,5},{5... | collective-permute-start | bytes 614408 | tf_op jit(solution)/shard_map/ppermute | solution.py:201
  5.9 8.0 %collective-permute-start.1 = (bf16[400,256]{1,0:T(8,128)(2,1)S(1)}, bf16[400,256]{1,0:T(8,128)(2,1)S(1)}, u32[]{:S(2)}, u32[]{:S(2)}) collective-permute-start(bf16[400,256]{1,0:T(8,128)(2,1)S(1)} %get-tuple-element.27), channel_id=1, source_target_pairs={{0,8},{4,12},{8,0},{12,4},{16,24},{20,28},{24,16},{28,20},{1,9},{5... | collective-permute-start | bytes 614408 | tf_op jit(solution)/shard_map/ppermute | solution.py:201
  7.4 9.2 %collective-permute-start.2 = (bf16[400,256]{1,0:T(8,128)(2,1)S(1)}, bf16[400,256]{1,0:T(8,128)(2,1)S(1)}, u32[]{:S(2)}, u32[]{:S(2)}) collective-permute-start(bf16[400,256]{1,0:T(8,128)(2,1)S(1)} %get-tuple-element.28), channel_id=1, source_target_pairs={{0,12},{4,8},{8,4},{12,0},{16,28},{20,24},{24,20},{28,16},{1,13},{... | collective-permute-start | bytes 614408 | tf_op jit(solution)/shard_map/ppermute | solution.py:201
  17.6 15.7 %collective-permute-start.3 = (bf16[256,512]{1,0:T(8,128)(2,1)S(1)}, bf16[256,512]{1,0:T(8,128)(2,1)S(1)}, u32[]{:S(2)}, u32[]{:S(2)}) collective-permute-start(bf16[256,512]{1,0:T(8,128)(2,1)S(1)} %get-tuple-element.29), channel_id=1, source_target_pairs={{0,16},{4,20},{8,24},{12,28},{1,17},{5,21},{9,25},{13,29},{2,18},{... | collective-permute-start | bytes 786440 | tf_op jit(solution)/shard_map/ppermute | solution.py:206
  22.3 1.0 %copy-start.2 = (bf16[128,1024]{1,0:T(8,128)(2,1)S(1)}, bf16[128,1024]{1,0:T(8,128)(2,1)}, u32[]{:S(2)}) copy-start(bf16[128,1024]{1,0:T(8,128)(2,1)} %query_ref.1) | copy-start | bytes 786436
  23.2 0.7 %copy-start.7 = (f32[4,128]{1,0:T(4,128)S(1)}, f32[4,128]{1,0:T(4,128)}, u32[]{:S(2)}) copy-start(f32[4,128]{1,0:T(4,128)} %decay_ref.5) | copy-start | bytes 6148
  24.0 4.3 %collective-permute-start.4 = (bf16[128,256]{1,0:T(8,128)(2,1)S(1)}, bf16[128,256]{1,0:T(8,128)(2,1)S(1)}, u32[]{:S(2)}, u32[]{:S(2)}) collective-permute-start(bf16[128,256]{1,0:T(8,128)(2,1)S(1)} %get-tuple-element.34), channel_id=1, source_target_pairs={{0,4},{4,0},{8,12},{12,8},{16,20},{20,16},{24,28},{28,24},{1,5},{5... | collective-permute-start | bytes 196616 | tf_op jit(solution)/shard_map/ppermute | solution.py:201
  25.6 4.3 %collective-permute-start.5 = (bf16[128,256]{1,0:T(8,128)(2,1)S(1)}, bf16[128,256]{1,0:T(8,128)(2,1)S(1)}, u32[]{:S(2)}, u32[]{:S(2)}) collective-permute-start(bf16[128,256]{1,0:T(8,128)(2,1)S(1)} %get-tuple-element.35), channel_id=1, source_target_pairs={{0,8},{4,12},{8,0},{12,4},{16,24},{20,28},{24,16},{28,20},{1,9},{5... | collective-permute-start | bytes 196616 | tf_op jit(solution)/shard_map/ppermute | solution.py:201
  27.2 5.2 %collective-permute-start.6 = (bf16[128,256]{1,0:T(8,128)(2,1)S(1)}, bf16[128,256]{1,0:T(8,128)(2,1)S(1)}, u32[]{:S(2)}, u32[]{:S(2)}) collective-permute-start(bf16[128,256]{1,0:T(8,128)(2,1)S(1)} %get-tuple-element.36), channel_id=1, source_target_pairs={{0,12},{4,8},{8,4},{12,0},{16,28},{20,24},{24,20},{28,16},{1,13},{... | collective-permute-start | bytes 196616 | tf_op jit(solution)/shard_map/ppermute | solution.py:201
  33.6 9.1 %collective-permute-start.7 = (bf16[128,512]{1,0:T(8,128)(2,1)S(1)}, bf16[128,512]{1,0:T(8,128)(2,1)S(1)}, u32[]{:S(2)}, u32[]{:S(2)}) collective-permute-start(bf16[128,512]{1,0:T(8,128)(2,1)S(1)} %get-tuple-element.40), channel_id=1, source_target_pairs={{0,4},{4,0},{8,12},{12,8},{16,20},{20,16},{24,28},{28,24},{1,5},{5... | collective-permute-start | bytes 393224 | tf_op jit(solution)/shard_map/ppermute | solution.py:201
  34.2 8.5 %collective-permute-start.8 = (bf16[128,512]{1,0:T(8,128)(2,1)S(1)}, bf16[128,512]{1,0:T(8,128)(2,1)S(1)}, u32[]{:S(2)}, u32[]{:S(2)}) collective-permute-start(bf16[128,512]{1,0:T(8,128)(2,1)S(1)} %get-tuple-element.41), channel_id=1, source_target_pairs={{0,8},{4,12},{8,0},{12,4},{16,24},{20,28},{24,16},{28,20},{1,9},{5... | collective-permute-start | bytes 393224 | tf_op jit(solution)/shard_map/ppermute | solution.py:201
  35.5 7.2 %collective-permute-start.9 = (bf16[128,512]{1,0:T(8,128)(2,1)S(1)}, bf16[128,512]{1,0:T(8,128)(2,1)S(1)}, u32[]{:S(2)}, u32[]{:S(2)}) collective-permute-start(bf16[128,512]{1,0:T(8,128)(2,1)S(1)} %get-tuple-element.42), channel_id=1, source_target_pairs={{0,12},{4,8},{8,4},{12,0},{16,28},{20,24},{24,20},{28,16},{1,13},{... | collective-permute-start | bytes 393224 | tf_op jit(solution)/shard_map/ppermute | solution.py:201
  37.3 1.0 %copy-start.1 = (bf16[128,2048]{1,0:T(8,128)(2,1)S(1)}, bf16[128,2048]{1,0:T(8,128)(2,1)}, u32[]{:S(2)}) copy-start(bf16[128,2048]{1,0:T(8,128)(2,1)} %value_ref.3) | copy-start | bytes 1572868
  38.3 0.9 %copy-start.3 = (bf16[128,1024]{1,0:T(8,128)(2,1)S(1)}, bf16[128,1024]{1,0:T(8,128)(2,1)}, u32[]{:S(2)}) copy-start(bf16[128,1024]{1,0:T(8,128)(2,1)} %query_ref.1) | copy-start | bytes 786436
  39.3 0.9 %copy-start.5 = (bf16[128,1024]{1,0:T(8,128)(2,1)S(1)}, bf16[128,1024]{1,0:T(8,128)(2,1)}, u32[]{:S(2)}) copy-start(bf16[128,1024]{1,0:T(8,128)(2,1)} %key_ref.3) | copy-start | bytes 786436
  40.2 0.7 %copy-start.8 = (f32[4,128]{1,0:T(4,128)S(1)}, f32[4,128]{1,0:T(4,128)}, u32[]{:S(2)}) copy-start(f32[4,128]{1,0:T(4,128)} %decay_ref.5) | copy-start | bytes 6148
  40.9 1.0 %copy-start.9 = (bf16[128,2048]{1,0:T(8,128)(2,1)S(1)}, bf16[128,2048]{1,0:T(8,128)(2,1)}, u32[]{:S(2)}) copy-start(bf16[128,2048]{1,0:T(8,128)(2,1)} %gate_ref.1) | copy-start | bytes 1572868
  52.6 2.0 %collective-permute-start.10 = (bf16[64,4096]{1,0:T(8,128)(2,1)S(1)}, bf16[64,4096]{1,0:T(8,128)(2,1)S(1)}, u32[]{:S(2)}, u32[]{:S(2)}) collective-permute-start(bf16[64,4096]{1,0:T(8,128)(2,1)S(1)} %get-tuple-element.44), channel_id=1, source_target_pairs={{0,1},{1,0},{2,3},{3,2},{4,5},{5,4},{6,7},{7,6},{8,9},{9,8},{10,11... | collective-permute-start | bytes 1572872 | tf_op jit(solution)/shard_map/ppermute | solution.py:201
  54.7 8.4 %collective-permute-start.11 = (bf16[32,4096]{1,0:T(8,128)(2,1)S(1)}, bf16[32,4096]{1,0:T(8,128)(2,1)S(1)}, u32[]{:S(2)}, u32[]{:S(2)}) collective-permute-start(bf16[32,4096]{1,0:T(8,128)(2,1)S(1)} %slice.15), channel_id=1, source_target_pairs={{0,2},{1,3},{2,0},{3,1},{4,6},{5,7},{6,4},{7,5},{8,10},{9,11},{10,... | collective-permute-start | bytes 786440 | tf_op jit(solution)/shard_map/ppermute | solution.py:201

commit v2 on v0

v2 whole, which is shorter than its diff:
```python
import functools
import jax
import jax.numpy as jnp
from jax import lax
from jax.experimental import pallas as pl
from jax.experimental.pallas import tpu as pltpu
from jax.sharding import PartitionSpec as P

F32 = jnp.float32
BF16 = jnp.bfloat16
TAIL = 16
PARTS = 4
SMEM = pl.BlockSpec(memory_space=pltpu.SMEM)
VMEM = pl.BlockSpec(memory_space=pltpu.VMEM)
HBM = pl.BlockSpec(memory_space=pltpu.HBM)


def params(mib):
    return pltpu.CompilerParams(vmem_limit_bytes=mib * 2**20)


def cost(flops, bytes_accessed):
    return pl.CostEstimate(flops=flops, bytes_accessed=bytes_accessed, transcendentals=0)


def in_hbm(*values):
    return [pltpu.with_memory_space_constraint(value, pltpu.HBM) for value in values]


def iotas(rows):
    down = lax.broadcasted_iota(jnp.int32, (rows, rows), 0)
    across = lax.broadcasted_iota(jnp.int32, (rows, rows), 1)
    return down, across


def features(index, width):
    return pl.ds(pl.multiple_of(index * width, width), width)


def fetch(pairs, sems):
    copies = [pltpu.make_async_copy(src, dst, sems.at[i]) for i, (src, dst) in enumerate(pairs)]
    for copy in copies:
        copy.start()
    return copies


def pack_kernel(place_ref, owner_ref, decay_hbm, key_hbm, value_hbm, query_hbm, *refs):
    decay_ref, key_ref, query_ref, sems, value_sems = refs[-5:]
    count = (len(refs) - 5) // 2
    first, second = refs[:count], refs[count : 2 * count]
    rows, width = first[0].shape[0] // 2 - TAIL // 2, first[0].shape[1]
    place = place_ref[0] & (count - 1)
    head_copies = fetch([(decay_hbm, decay_ref), (key_hbm, key_ref), (query_hbm, query_ref)], sems)
    pairs = []
    for hop in range(count):
        head = place ^ hop
        pairs.append((value_hbm.at[:, features(2 * head, width)], first[hop].at[rows : 2 * rows]))
        pairs.append((value_hbm.at[:, features(2 * head + 1, width)], second[hop].at[0:rows]))
    value_copies = fetch(pairs, value_sems)
    down, across = iotas(rows)
    for copy in head_copies:
        copy.wait()
    for hop in range(count):
        head = place ^ hop
        decay = decay_ref[pl.ds(head, 1), :]
        after = jnp.sum(jnp.where(across > down, decay, 0.0), axis=1, keepdims=True)
        upto = jnp.sum(jnp.where(across <= down, decay, 0.0), axis=1, keepdims=True)
        keys = key_ref[:, features(head, width)].astype(F32)
        first[hop][0:rows, :] = (keys * jnp.exp(after)).astype(BF16)
        queries = query_ref[:, features(head, width)].astype(F32)
        second[hop][rows : 2 * rows, :] = (queries * jnp.exp(upto)).astype(BF16)
        whole = jnp.exp(jnp.sum(decay, axis=1, keepdims=True))
        whole = jnp.broadcast_to(whole, (TAIL, width))
        high = whole.astype(BF16).astype(F32)
        middle = (whole - high).astype(BF16).astype(F32)
        low = whole - high - middle
        row = lax.broadcasted_iota(jnp.int32, (TAIL, width), 0)
        tail = jnp.where(row == 0, high, jnp.where(row == 1, middle, jnp.where(row == 2, low, 0.0)))
        first[hop][2 * rows :, :] = tail.astype(BF16)
    for copy in value_copies:
        copy.wait()


def block_decay(message_ref):
    tail = message_ref[message_ref.shape[0] - TAIL :, :].astype(F32)
    return tail[0:1] + tail[1:2] + tail[2:3]


def outer(keys, values):
    return lax.dot_general(keys, values, (((0,), (0,)), ((), ())), preferred_element_type=F32)


def total_state(place, first, values, rows):
    decays = [block_decay(message) for message in first]
    total = None
    for hop, message in enumerate(first):
        scale = None
        for other in range(len(first)):
            if other != hop:
                factor = jnp.where((place ^ other) > (place ^ hop), decays[other], 1.0)
                scale = factor if scale is None else scale * factor
        term = outer(message[0:rows, :], values[hop])
        term = term if scale is None else term * scale
        total = term if total is None else total + term
    return total


def first_state_kernel(place_ref, *refs, rows):
    first, (state_ref, whole_ref) = refs[:-2], refs[-2:]
    values = [message[rows : 2 * rows, :] for message in first]
    state_ref[...] = total_state(place_ref[0] & (len(first) - 1), first, values, rows).astype(BF16)
    whole = block_decay(first[0])
    for message in first[1:]:
        whole = whole * block_decay(message)
    whole_ref[...] = jnp.broadcast_to(whole, whole_ref.shape)


def second_state_kernel(place_ref, *refs, rows):
    count = (len(refs) - 1) // 2
    first, second, state_ref = refs[:count], refs[count : 2 * count], refs[-1]
    values = [message[0:rows, :] for message in second]
    state_ref[...] = total_state(place_ref[0] & (len(first) - 1), first, values, rows).astype(BF16)


def group_kernel(place_ref, *refs, rows):
    count = (len(refs) - 6) // 2
    first, second = refs[:count], refs[count : 2 * count]
    left_ref, right_ref, scaled_ref, states, earlier, decays = refs[2 * count :]
    width = first[0].shape[1]
    place = place_ref[0] & (count - 1)
    for hop in range(count):
        block = place ^ hop
        decays[block] = jnp.broadcast_to(block_decay(first[hop]), decays.shape[1:])
        keys = first[hop][0:rows, :]
        states[block, :, 0:width] = outer(keys, first[hop][rows : 2 * rows, :])
        states[block, :, width : 2 * width] = outer(keys, second[hop][0:rows, :])
    whole = jnp.ones((1, width), F32)
    for block in range(count):
        if block == 0:
            earlier[0] = jnp.zeros(earlier.shape[1:], BF16)
        elif block == 1:
            total = states[0]
            earlier[1] = total.astype(BF16)
        else:
            total = total * jnp.concatenate([decay, decay], axis=1) + states[block - 1]
            earlier[block] = total.astype(BF16)
        decay = decays[block][0:1]
        decays[block] = jnp.broadcast_to(whole, decays.shape[1:])
        whole = whole * decay
    for hop in range(count):
        block = place ^ hop
        queries = second[hop][rows : 2 * rows, :]
        here = slice(hop * rows, (hop + 1) * rows)
        part = jnp.dot(queries, earlier[block], preferred_element_type=F32)
        left_ref[here, :] = part[:, 0:width]
        right_ref[here, :] = part[:, width : 2 * width]
        scaled_ref[here, :] = (queries.astype(F32) * decays[block][0:1]).astype(BF16)


def crossed(place_ref, state_ref, scaled_ref, part_ref, group):
    carried = jnp.dot(scaled_ref[...], state_ref[...], preferred_element_type=F32)
    return (part_ref[...] + jnp.where(place_ref[0] < group, 0.0, carried)).astype(BF16)


def left_cross_kernel(place_ref, state_ref, scaled_ref, part_ref, out_ref, *, group):
    out_ref[...] = crossed(place_ref, state_ref, scaled_ref, part_ref, group)


def right_cross_kernel(place_ref, state_ref, scaled_ref, part_ref, left_ref, *out_refs):
    rows, width = out_refs[0].shape
    right = crossed(place_ref, state_ref, scaled_ref, part_ref, len(out_refs))
    for hop, out_ref in enumerate(out_refs):
        here = slice(hop * rows, (hop + 1) * rows)
        out_ref[:, : width // 2] = left_ref[here, :]
        out_ref[:, width // 2 :] = right[here, :]


def block_kernel(*refs):
    decay_hbm, query_hbm, key_hbm, value_hbm, gate_hbm, inner_ref, swish_ref = refs[:7]
    decay_ref, query_ref, key_ref, value_ref, gate_ref, sems = refs[7:]
    rows = query_ref.shape[0]
    heads = decay_ref.shape[0]
    key_dim, value_dim = query_ref.shape[1] // heads, value_ref.shape[1] // heads
    copies = fetch(
        [
            (decay_hbm, decay_ref),
            (query_hbm, query_ref),
            (key_hbm, key_ref),
            (value_hbm, value_ref),
            (gate_hbm, gate_ref),
        ],
        sems,
    )
    down, across = iotas(rows)
    causal = across <= down
    for copy in copies:
        copy.wait()
    for head in range(heads):
        decay = decay_ref[head : head + 1, :]
        column = jnp.sum(jnp.where(causal, decay, 0.0), axis=1, keepdims=True)
        line = jnp.sum(jnp.where(across == down, column, 0.0), axis=0, keepdims=True)
        table = jnp.where(causal, jnp.exp(jnp.where(causal, column - line, 0.0)), 0.0)
        keys = slice(head * key_dim, (head + 1) * key_dim)
        here = slice(head * value_dim, (head + 1) * value_dim)
        scores = lax.dot_general(
            query_ref[:, keys], key_ref[:, keys], (((1,), (1,)), ((), ())), preferred_element_type=F32
        )
        inner_ref[:, here] = jnp.dot(
            (scores * table).astype(BF16), value_ref[:, here], preferred_element_type=F32
        )
        gate = gate_ref[:, here].astype(F32)
        swish_ref[:, here] = gate / (1.0 + jnp.exp(-gate))


def mix_kernel(place_ref, owner_ref, inner_ref, swish_ref, part_ref, out_ref, mixed, *, hop, group, owners):
    rows, value_dim = out_ref.shape
    here = features((place_ref[0] & (group - 1)) ^ hop, value_dim)
    retained = inner_ref[:, here] + part_ref[...].astype(F32)
    mean = jnp.mean(retained, axis=1, keepdims=True)
    centered = retained - mean
    variance = jnp.mean(centered * centered, axis=1, keepdims=True)
    mixed[...] = centered * lax.rsqrt(variance + 1e-05) * swish_ref[:, here]
    share = rows // owners
    bits = owners.bit_length() - 1
    pieces = []
    for position in range(owners):
        flipped = owners - 1 - position
        mask = sum(((flipped >> bit) & 1) << (bits - 1 - bit) for bit in range(bits))
        start = pl.multiple_of((owner_ref[0] ^ mask) * share, share)
        pieces.append(mixed[pl.ds(start, share), :])
    out_ref[...] = jnp.concatenate(pieces, axis=0).astype(BF16)


def project_kernel(place_ref, *refs, part):
    weight_ref, send_ref, keep_ref = refs[-3:]
    half, width = send_ref.shape
    place = place_ref[0] & (len(refs) - 4)
    tile = min(512, width)
    for start in range(0, width, tile):
        here = slice(start, start + tile)
        out = None
        for hop, rows_ref in enumerate(refs[:-3]):
            depth = rows_ref.shape[1]
            there = pl.ds(pl.multiple_of((place ^ hop) * depth, depth), depth)
            term = jnp.dot(rows_ref[...], weight_ref[there, slice(part * width + start, part * width + start + tile)], preferred_element_type=F32)
            out = term if out is None else out + term
        send_ref[:, here] = out[:half].astype(BF16)
        keep_ref[:, here] = out[half:].astype(BF16)


def swap(value, axis, size, mask):
    return lax.ppermute(value, axis, [(i, i ^ mask) for i in range(size)])


def swaps(values, axis, size):
    return [swap(values[hop], axis, size, hop) for hop in range(1, len(values))]


def carried_into(state, whole, axis, size, group, wrap):
    def shift(value, by):
        count = size if wrap else size - by * group
        return lax.ppermute(value, axis, [(i, (i + by * group) % size) for i in range(count)])

    groups = size // group
    if groups == 1:
        return state
    got = shift(state, 1)
    if groups == 2:
        return got
    first = lax.axis_index(axis) < group
    total, product = jnp.where(first, 0.0, got.astype(F32)), jnp.where(first, 1.0, shift(whole, 1))
    by = 1
    while by < groups - 1:
        none = lax.axis_index(axis) < by * group
        earlier, before = shift(total.astype(BF16), by), shift(product, by)
        total = total + jnp.where(none, 0.0, product[0:1] * earlier.astype(F32))
        product = product * jnp.where(none, 1.0, before)
        by *= 2
    return total.astype(BF16)


def reduce_over(send, keep, axis, size):
    keep = keep.astype(F32)
    mask = 1
    while mask < size:
        keep = keep + swap(send.astype(BF16), axis, size, mask).astype(F32)
        mask *= 2
        if mask < size:
            half = keep.shape[0] // 2
            send, keep = keep[:half], keep[half:]
    return keep.astype(BF16)


def local(query, key, value, gate, decay, weight, *, ctx, head):
    rows = query.shape[0]
    heads = decay.shape[0]
    key_dim = query.shape[1] // heads
    value_dim = value.shape[1] // heads
    depth, width = weight.shape
    group = heads
    me = lax.axis_index("ctx")
    place = me.astype(jnp.int32).reshape(1)
    owner = lax.axis_index("head").astype(jnp.int32).reshape(1)
    shape = jax.ShapeDtypeStruct

    packed = pl.pallas_call(
        pack_kernel,
        out_shape=[shape((2 * rows + TAIL, key_dim), BF16)] * group + [shape((2 * rows, key_dim), BF16)] * group,
        in_specs=[SMEM] * 2 + [HBM] * 4,
        out_specs=[VMEM] * (2 * group),
        scratch_shapes=[
            pltpu.VMEM(decay.shape, F32),
            pltpu.VMEM(key.shape, BF16),
            pltpu.VMEM(query.shape, BF16),
            pltpu.SemaphoreType.DMA((3,)),
            pltpu.SemaphoreType.DMA((2 * group,)),
        ],
        compiler_params=params(8),
        name="pack",
    )(place, owner, *in_hbm(decay, key, value, query))
    def after(value):
        return lax.optimization_barrier((decay, value))[0]

    token = after(packed[0])
    inner, swish = pl.pallas_call(
        block_kernel,
        out_shape=[shape(value.shape, F32)] * 2,
        in_specs=[HBM] * 5,
        out_specs=[VMEM] * 2,
        scratch_shapes=[
            pltpu.VMEM(decay.shape, F32),
            pltpu.VMEM(query.shape, BF16),
            pltpu.VMEM(key.shape, BF16),
            pltpu.VMEM(value.shape, BF16),
            pltpu.VMEM(gate.shape, BF16),
            pltpu.SemaphoreType.DMA((5,)),
        ],
        compiler_params=params(8),
        cost_estimate=cost(10**9, 4 * 2**20),
        name="block_part",
    )(*in_hbm(token, query, key, value, gate))

    first = swaps(packed[:group], "ctx", ctx)
    later, _ = lax.optimization_barrier((packed[group:], inner))
    second = [packed[group]] + swaps(later, "ctx", ctx)
    first = [packed[0]] + first
    left_state, whole = pl.pallas_call(
        functools.partial(first_state_kernel, rows=rows),
        out_shape=[shape((key_dim, key_dim), BF16), shape((8, key_dim), F32)],
        in_specs=[SMEM] + [VMEM] * group,
        out_specs=[VMEM] * 2,
        compiler_params=params(8),
        name="first_state",
    )(place, *first)
    left_carried = carried_into(left_state, whole, "ctx", ctx, group, True)

    right_state = pl.pallas_call(
        functools.partial(second_state_kernel, rows=rows),
        out_shape=shape((key_dim, key_dim), BF16),
        in_specs=[SMEM] + [VMEM] * (2 * group),
        out_specs=VMEM,
        compiler_params=params(8),
        name="second_state",
    )(place, *first, *second)
    right_carried = carried_into(right_state, whole, "ctx", ctx, group, False)

    left_part, right_part, scaled = pl.pallas_call(
        functools.partial(group_kernel, rows=rows),
        out_shape=[shape((group * rows, key_dim), F32)] * 2 + [shape((group * rows, key_dim), BF16)],
        in_specs=[SMEM] + [VMEM] * (2 * group),
        out_specs=[VMEM] * 3,
        scratch_shapes=[
            pltpu.VMEM((group, key_dim, value_dim), F32),
            pltpu.VMEM((group, key_dim, value_dim), BF16),
            pltpu.VMEM((group, 8, key_dim), F32),
        ],
        compiler_params=params(8),
        cost_estimate=cost(10**9, 4 * 2**20),
        name="group_part",
    )(place, *first, *second)

    left_cross = pl.pallas_call(
        functools.partial(left_cross_kernel, group=group),
        out_shape=shape((group * rows, key_dim), BF16),
        in_specs=[SMEM] + [VMEM] * 3,
        out_specs=VMEM,
        compiler_params=params(8),
        name="left_cross",
    )(place, left_carried, scaled, left_part)
    parts = pl.pallas_call(
        right_cross_kernel,
        out_shape=[shape((rows, value_dim), BF16)] * group,
        in_specs=[SMEM] + [VMEM] * 4,
        out_specs=[VMEM] * group,
        compiler_params=params(8),
        name="right_cross",
    )(place, right_carried, scaled, right_part, left_cross)
    parts = [parts[0]] + swaps(parts, "ctx", ctx)

    mixed_rows = [
        pl.pallas_call(
            functools.partial(mix_kernel, hop=hop, group=group, owners=head),
            out_shape=shape((rows, value_dim), BF16),
            in_specs=[SMEM] * 2 + [VMEM] * 3,
            out_specs=VMEM,
            scratch_shapes=[pltpu.VMEM((rows, value_dim), F32)],
            compiler_params=params(4),
            name="mix",
        )(place, owner, inner, swish, parts[hop])
        for hop in range(group)
    ]
    outs = []
    for part in range(PARTS):
        send, keep = pl.pallas_call(
            functools.partial(project_kernel, part=part),
            out_shape=[shape((rows // 2, width // PARTS), BF16)] * 2,
            in_specs=[SMEM] + [VMEM] * (group + 1),
            out_specs=[VMEM] * 2,
            compiler_params=params(4),
            cost_estimate=cost(2**29, 2**22),
            name="project",
        )(place, *mixed_rows, weight)
        outs.append(reduce_over(send, keep, "head", head))
    return jnp.concatenate(outs, axis=1)


def solution(mesh):
    in_specs = (
        P("ctx", "head"),
        P("ctx", "head"),
        P("ctx", "head"),
        P("ctx", "head"),
        P("head", "ctx"),
        P("head", None),
    )
    out_specs = P(("ctx", "head"), None)
    body = functools.partial(local, ctx=mesh.shape["ctx"], head=mesh.shape["head"])
    return jax.shard_map(body, mesh=mesh, in_specs=in_specs, out_specs=out_specs, check_vma=False)
```

time: 311 us -> 51.6 us (0.17)
  waiting for transfers between devices: 224 us -> 15 us
  starting transfers between devices: 0.04 us -> 24.9 us
  other arithmetic: 24.7 us -> 0.9 us
  blocking collectives: 23.4 us -> 0 us
  matrix products: 21.1 us -> 0 us
  between operations: 14.3 us -> 0.2 us
  Pallas kernels: 0 us -> 10.4 us
    all_gather x1 -> x0, waiting for transfers between devices: 201 us -> none  [carried_in(): pieces = jax.tree.map(lambda part: lax.all_gather(part, axis), value)]
    ppermute x0 -> x19, starting transfers between devices: none -> 24.9 us  [the longest x17 18.2 us: swap(): return lax.ppermute(value, axis, [(i, i ^ mask) for i in range(size)])]
    unnamed x1 -> x0, blocking collectives: 23.4 us -> none
    reduce_scatter x1 -> x0, waiting for transfers between devices: 23.2 us -> none  [local(): lax.psum_scatter(partial_value.astype(jnp.bfloat16), 'head', scatter_dime...]
    dot_general x13 -> x0, matrix products: 21.1 us -> none  [the longest x1 9.43 us: local(): jnp.dot(mixed_rows, out_weight, preferred_element_type=jnp.float32)]
    select_n x7 -> x0, other arithmetic: 18.4 us -> none  [lap(): jnp.where(position < mine, new, old)]
    ppermute x0 -> x19, waiting for transfers between devices: none -> 15 us  [the longest x17 13.7 us: swap(): return lax.ppermute(value, axis, [(i, i ^ mask) for i in range(size)])]
    pallas_call x0 -> x15, Pallas kernels: none -> 10.4 us  [the longest x4 2.87 us: local(): pl.pallas_call(functools.partial(project_kernel, part=part), out_shape=[s...]
  transfers between devices with their start and end apart: 2 -> 19, of which waited for: 2 -> 11; matrix products, arithmetic and copies ran while one was open for 2% -> 0% of each run, Pallas kernels for 0% -> 15%
where the time goes in v2:
time: 51.6 us; the launch traced here: 51.4 us
  starting transfers between devices  24.9 us (48%)
  waiting for transfers between devices  15 us (29%)
  Pallas kernels  10.4 us (20%)
  other arithmetic  0.9 us (2%)
    ppermute x17, starting transfers between devices, swap(): return lax.ppermute(value, axis, [(i, i ^ mask) for i in range(size)])  18.2 us
    ppermute x17, waiting for transfers between devices, swap(): return lax.ppermute(value, axis, [(i, i ^ mask) for i in range(size)])  13.7 us
    ppermute x2, starting transfers between devices, shift(): lax.ppermute(value, axis, [(i, (i + by * group) % size) for i in range(co...  6.73 us
    pallas_call x4, Pallas kernels, local(): pl.pallas_call(functools.partial(project_kernel, part=part), out_shape=[s...  2.87 us
    pallas_call x1, Pallas kernels, local(): pl.pallas_call(block_kernel, out_shape=[shape(value.shape, F32)] * 2, in_...  2.31 us
    pallas_call x1, Pallas kernels, local(): pl.pallas_call(pack_kernel, out_shape=[shape((2 * rows + TAIL, key_dim),...  1.75 us
    ppermute x2, waiting for transfers between devices, shift(): lax.ppermute(value, axis, [(i, (i + by * group) % size) for i in range(co...  1.31 us
  transfers between devices with their start and end apart: 19, of which 11 were waited for; matrix products, arithmetic and copies ran while one was open for 0% of the time, Pallas kernels for 15%

profile of v2, /device:TPU:0, one launch (start us, length us, event | category | flops | bytes accessed | tf_op | source)
XLA Modules:
  0.0 51.4 jit_solution(3029499458431878563)
XLA Ops:
  0.0 1.7 %pack.1 = (bf16[272,256]{1,0:T(8,128)(2,1)S(1)}, bf16[272,256]{1,0:T(8,128)(2,1)S(1)}, bf16[272,256]{1,0:T(8,128)(2,1)S(1)}, bf16[272,256]{1,0:T(8,128)(2,1)S(1)...) custom-call(s32[1]{0:T(128)} %bitcast.place_ref, ...), custom_call_target="tpu_custom_call" | custom-call | tf_op jit(solution)/shard_map/pack/pallas_call | solution.py:306
  1.8 3.0 %collective-permute-start = (bf16[272,256]{1,0:T(8,128)(2,1)S(1)}, bf16[272,256]{1,0:T(8,128)(2,1)S(1)}, u32[]{:S(2)}, u32[]{:S(2)}) collective-permute-start(bf16[272,256]{1,0:T(8,128)(2,1)S(1)} %get-tuple-element.39), channel_id=1, source_target_pairs={{0,4},{4,0},{8,12},{12,8},{16,20},{20,16},{24,28},{28,24},{1,5},{5... | collective-permute-start | bytes 417800 | tf_op jit(solution)/shard_map/ppermute | solution.py:252
  4.8 1.6 %collective-permute-start.1 = (bf16[272,256]{1,0:T(8,128)(2,1)S(1)}, bf16[272,256]{1,0:T(8,128)(2,1)S(1)}, u32[]{:S(2)}, u32[]{:S(2)}) collective-permute-start(bf16[272,256]{1,0:T(8,128)(2,1)S(1)} %get-tuple-element.40), channel_id=1, source_target_pairs={{0,8},{4,12},{8,0},{12,4},{16,24},{20,28},{24,16},{28,20},{1,9},{5... | collective-permute-start | bytes 417800 | tf_op jit(solution)/shard_map/ppermute | solution.py:252
  6.3 2.3 %block_part.1 = (f32[128,2048]{1,0:T(8,128)S(1)}, f32[128,2048]{1,0:T(8,128)S(1)}) custom-call(f32[4,128]{1,0:T(4,128)} %refs_0_, bf16[128,1024]{1,0:T(8,128)(2,1)} %refs_1_.1, bf16[128,1024]{1,0:T(8,128)(2,1)} %refs_2_.1, bf16[128,2048]{1,0:T(8,128)(2,1)} %refs_3_.1, bf16[128,2048]{1,0:T(8,128)(2,1)} %refs_4_.5), custom_call_target="tpu_custom_call" | custom-call | flops 1000000000 | bytes 4194304 | tf_op jit(solution)/shard_map/block_part/pallas_call | solution.py:325
  8.7 2.0 %collective-permute-start.3 = (bf16[256,256]{1,0:T(8,128)(2,1)S(1)}, bf16[256,256]{1,0:T(8,128)(2,1)S(1)}, u32[]{:S(2)}, u32[]{:S(2)}) collective-permute-start(bf16[256,256]{1,0:T(8,128)(2,1)S(1)} %get-tuple-element.46), channel_id=1, source_target_pairs={{0,4},{4,0},{8,12},{12,8},{16,20},{20,16},{24,28},{28,24},{1,5},{5... | collective-permute-start | bytes 393224 | tf_op jit(solution)/shard_map/ppermute | solution.py:252
  10.6 1.6 %collective-permute-start.4 = (bf16[256,256]{1,0:T(8,128)(2,1)S(1)}, bf16[256,256]{1,0:T(8,128)(2,1)S(1)}, u32[]{:S(2)}, u32[]{:S(2)}) collective-permute-start(bf16[256,256]{1,0:T(8,128)(2,1)S(1)} %get-tuple-element.47), channel_id=1, source_target_pairs={{0,8},{4,12},{8,0},{12,4},{16,24},{20,28},{24,16},{28,20},{1,9},{5... | collective-permute-start | bytes 393224 | tf_op jit(solution)/shard_map/ppermute | solution.py:252
  12.8 0.9 %first_state.1 = (bf16[256,256]{1,0:T(8,128)(2,1)S(1)}, f32[8,256]{1,0:T(8,128)}) custom-call(s32[1]{0:T(128)} %bitcast.place_ref, bf16[272,256]{1,0:T(8,128)(2,1)S(1)} %get-tuple-element.35.refs_0_, bf16[272,256]{1,0:T(8,128)(2,1)S(1)} %collective-permute-done.refs_1_, bf16[272,256]{1,0:T(8,128)(2,1)S(1)} %collective-permute-done.1.refs_2_, ...), custom_call_target="tpu_custom_call" | custom-call | tf_op jit(solution)/shard_map/first_state/pallas_call | solution.py:347
  13.7 2.8 %collective-permute-start.7 = (bf16[256,256]{1,0:T(8,128)(2,1)S(1)}, bf16[256,256]{1,0:T(8,128)(2,1)S(1)}, u32[]{:S(2)}, u32[]{:S(2)}) collective-permute-start(bf16[256,256]{1,0:T(8,128)(2,1)S(1)} %get-tuple-element.51), channel_id=1, source_target_pairs={{0,16},{4,20},{8,24},{12,28},{16,0},{20,4},{24,8},{28,12},{1,17},{... | collective-permute-start | bytes 393224 | tf_op jit(solution)/shard_map/ppermute | solution.py:262
  16.5 3.3 %collective-permute-done.4.refs_6_ = bf16[256,256]{1,0:T(8,128)(2,1)S(1)} collective-permute-done((bf16[256,256]{1,0:T(8,128)(2,1)S(1)}, bf16[256,256]{1,0:T(8,128)(2,1)S(1)}, u32[]{:S(2)}, u32[]{:S(2)}) %collective-permute-start.4) | collective-permute-done | bytes 131104 | tf_op jit(solution)/shard_map/ppermute | solution.py:252
  20.6 4.0 %collective-permute-start.6 = (bf16[256,256]{1,0:T(8,128)(2,1)S(1)}, bf16[256,256]{1,0:T(8,128)(2,1)S(1)}, u32[]{:S(2)}, u32[]{:S(2)}) collective-permute-start(bf16[256,256]{1,0:T(8,128)(2,1)S(1)} %second_state.1), channel_id=1, source_target_pairs={{0,16},{4,20},{8,24},{12,28},{1,17},{5,21},{9,25},{13,29},{2,18},{... | collective-permute-start | bytes 393224 | tf_op jit(solution)/shard_map/ppermute | solution.py:262
  24.6 0.9 %group_part.1 = (f32[512,256]{1,0:T(8,128)S(1)}, f32[512,256]{1,0:T(8,128)S(1)}, bf16[512,256]{1,0:T(8,128)(2,1)S(1)}) custom-call(s32[1]{0:T(128)} %bitcast.place_ref, bf16[272,256]{1,0:T(8,128)(2,1)S(1)} %get-tuple-element.35.refs_0_, bf16[272,256]{1,0:T(8,128)(2,1)S(1)} %collective-permute-done.refs_1_, ...), custom_call_target="tpu_custom_call" | custom-call | flops 1000000000 | bytes 4194304 | tf_op jit(solution)/shard_map/group_part/pallas_call | solution.py:367
  25.8 1.3 %collective-permute-done.6.state_ref = bf16[256,256]{1,0:T(8,128)(2,1)S(1)} collective-permute-done((bf16[256,256]{1,0:T(8,128)(2,1)S(1)}, bf16[256,256]{1,0:T(8,128)(2,1)S(1)}, u32[]{:S(2)}, u32[]{:S(2)}) %collective-permute-start.6) | collective-permute-done | bytes 131104 | tf_op jit(solution)/shard_map/ppermute | solution.py:262
  27.3 1.7 %collective-permute-start.8 = (bf16[128,512]{1,0:T(8,128)(2,1)S(1)}, bf16[128,512]{1,0:T(8,128)(2,1)S(1)}, u32[]{:S(2)}, u32[]{:S(2)}) collective-permute-start(bf16[128,512]{1,0:T(8,128)(2,1)S(1)} %get-tuple-element.54), channel_id=1, source_target_pairs={{0,4},{4,0},{8,12},{12,8},{16,20},{20,16},{24,28},{28,24},{1,5},{5... | collective-permute-start | bytes 393224 | tf_op jit(solution)/shard_map/ppermute | solution.py:252
  29.0 2.8 %collective-permute-start.9 = (bf16[128,512]{1,0:T(8,128)(2,1)S(1)}, bf16[128,512]{1,0:T(8,128)(2,1)S(1)}, u32[]{:S(2)}, u32[]{:S(2)}) collective-permute-start(bf16[128,512]{1,0:T(8,128)(2,1)S(1)} %get-tuple-element.55), channel_id=1, source_target_pairs={{0,8},{4,12},{8,0},{12,4},{16,24},{20,28},{24,16},{28,20},{1,9},{5... | collective-permute-start | bytes 393224 | tf_op jit(solution)/shard_map/ppermute | solution.py:252
  32.0 1.7 %collective-permute-done.8.part_ref = bf16[128,512]{1,0:T(8,128)(2,1)S(1)} collective-permute-done((bf16[128,512]{1,0:T(8,128)(2,1)S(1)}, bf16[128,512]{1,0:T(8,128)(2,1)S(1)}, u32[]{:S(2)}, u32[]{:S(2)}) %collective-permute-start.8) | collective-permute-done | bytes 131104 | tf_op jit(solution)/shard_map/ppermute | solution.py:252
  34.0 0.8 %collective-permute-done.9.part_ref = bf16[128,512]{1,0:T(8,128)(2,1)S(1)} collective-permute-done((bf16[128,512]{1,0:T(8,128)(2,1)S(1)}, bf16[128,512]{1,0:T(8,128)(2,1)S(1)}, u32[]{:S(2)}, u32[]{:S(2)}) %collective-permute-start.9) | collective-permute-done | bytes 131104 | tf_op jit(solution)/shard_map/ppermute | solution.py:252
  35.0 2.7 %collective-permute-done.10.part_ref = bf16[128,512]{1,0:T(8,128)(2,1)S(1)} collective-permute-done((bf16[128,512]{1,0:T(8,128)(2,1)S(1)}, bf16[128,512]{1,0:T(8,128)(2,1)S(1)}, u32[]{:S(2)}, u32[]{:S(2)}) %collective-permute-start.10) | collective-permute-done | bytes 131104 | tf_op jit(solution)/shard_map/ppermute | solution.py:252
  37.9 0.7 %project.7 = (bf16[64,1024]{1,0:T(8,128)(2,1)S(1)}, bf16[64,1024]{1,0:T(8,128)(2,1)S(1)}) custom-call(s32[1]{0:T(128)} %bitcast.place_ref, bf16[128,512]{1,0:T(8,128)(2,1)S(1)} %mix.4.refs_0_, bf16[128,512]{1,0:T(8,128)(2,1)S(1)} %mix.5.refs_1_, bf16[128,512]{1,0:T(8,128)(2,1)S(1)} %mix.6.refs_2_, bf16[128,512]{1,0:T(8,128)(2,1)S(1)} %mix.7.refs_3_, ...), custom_call_target="tpu_custom_call" | custom-call | flops 536870912 | bytes 4194304 | tf_op jit(solution)/shard_map/project/pallas_call | solution.py:414
  38.7 0.7 %project.6 = (bf16[64,1024]{1,0:T(8,128)(2,1)S(1)}, bf16[64,1024]{1,0:T(8,128)(2,1)S(1)}) custom-call(s32[1]{0:T(128)} %bitcast.place_ref, bf16[128,512]{1,0:T(8,128)(2,1)S(1)} %mix.4.refs_0_, bf16[128,512]{1,0:T(8,128)(2,1)S(1)} %mix.5.refs_1_, bf16[128,512]{1,0:T(8,128)(2,1)S(1)} %mix.6.refs_2_, bf16[128,512]{1,0:T(8,128)(2,1)S(1)} %mix.7.refs_3_, ...), custom_call_target="tpu_custom_call" | custom-call | flops 536870912 | bytes 4194304 | tf_op jit(solution)/shard_map/project/pallas_call | solution.py:414
  42.1 1.6 %collective-permute-start.18 = (bf16[32,1024]{1,0:T(8,128)(2,1)S(1)}, bf16[32,1024]{1,0:T(8,128)(2,1)S(1)}, u32[]{:S(2)}, u32[]{:S(2)}) collective-permute-start(bf16[32,1024]{1,0:T(8,128)(2,1)S(1)} %slice.60), channel_id=1, source_target_pairs={{0,2},{1,3},{2,0},{3,1},{4,6},{5,7},{6,4},{7,5},{8,10},{9,11},{10,... | collective-permute-start | bytes 196616 | tf_op jit(solution)/shard_map/ppermute | solution.py:252
  44.4 1.6 %collective-permute-start.14 = (bf16[32,1024]{1,0:T(8,128)(2,1)S(1)}, bf16[32,1024]{1,0:T(8,128)(2,1)S(1)}, u32[]{:S(2)}, u32[]{:S(2)}) collective-permute-start(bf16[32,1024]{1,0:T(8,128)(2,1)S(1)} %slice.62), channel_id=1, source_target_pairs={{0,2},{1,3},{2,0},{3,1},{4,6},{5,7},{6,4},{7,5},{8,10},{9,11},{10,... | collective-permute-start | bytes 196616 | tf_op jit(solution)/shard_map/ppermute | solution.py:252
  46.9 2.0 %collective-permute-done.16 = bf16[32,1024]{1,0:T(8,128)(2,1)S(1)} collective-permute-done((bf16[32,1024]{1,0:T(8,128)(2,1)S(1)}, bf16[32,1024]{1,0:T(8,128)(2,1)S(1)}, u32[]{:S(2)}, u32[]{:S(2)}) %collective-permute-start.16) | collective-permute-done | bytes 65568 | tf_op jit(solution)/shard_map/ppermute | solution.py:252
  48.9 1.1 %collective-permute-done.14 = bf16[32,1024]{1,0:T(8,128)(2,1)S(1)} collective-permute-done((bf16[32,1024]{1,0:T(8,128)(2,1)S(1)}, bf16[32,1024]{1,0:T(8,128)(2,1)S(1)}, u32[]{:S(2)}, u32[]{:S(2)}) %collective-permute-start.14) | collective-permute-done | bytes 65568 | tf_op jit(solution)/shard_map/ppermute | solution.py:252
  50.7 0.7 %pad_maximum_fusion = bf16[32,4096]{1,0:T(8,128)(2,1)} fusion(bf16[32,1024]{1,0:T(8,128)(2,1)S(1)} %fusion, bf16[32,1024]{1,0:T(8,128)(2,1)S(1)} %fusion.1, bf16[32,1024]{1,0:T(8,128)(2,1)S(1)} %fusion.2, bf16[32,1024]{1,0:T(8,128)(2,1)S(1)} %fusion.3), kind=kLoop, calls=%fused_computation | loop fusion | flops 1048576 | bytes 524288 | tf_op jit(solution)/shard_map/concatenate | solution.py:424
  (44 shorter events, 7.8 us)
Async XLA Ops:
  0.0 37.9 %copy-start = (bf16[2048,4096]{1,0:T(8,128)(2,1)S(1)}, bf16[2048,4096]{1,0:T(8,128)(2,1)}, u32[]{:S(2)}) copy-start(bf16[2048,4096]{1,0:T(8,128)(2,1)} %refs_4_.9) | copy-start | bytes 50331652
  1.8 10.5 %collective-permute-start = (bf16[272,256]{1,0:T(8,128)(2,1)S(1)}, bf16[272,256]{1,0:T(8,128)(2,1)S(1)}, u32[]{:S(2)}, u32[]{:S(2)}) collective-permute-start(bf16[272,256]{1,0:T(8,128)(2,1)S(1)} %get-tuple-element.39), channel_id=1, source_target_pairs={{0,4},{4,0},{8,12},{12,8},{16,20},{20,16},{24,28},{28,24},{1,5},{5... | collective-permute-start | bytes 417800 | tf_op jit(solution)/shard_map/ppermute | solution.py:252
  4.8 7.5 %collective-permute-start.1 = (bf16[272,256]{1,0:T(8,128)(2,1)S(1)}, bf16[272,256]{1,0:T(8,128)(2,1)S(1)}, u32[]{:S(2)}, u32[]{:S(2)}) collective-permute-start(bf16[272,256]{1,0:T(8,128)(2,1)S(1)} %get-tuple-element.40), channel_id=1, source_target_pairs={{0,8},{4,12},{8,0},{12,4},{16,24},{20,28},{24,16},{28,20},{1,9},{5... | collective-permute-start | bytes 417800 | tf_op jit(solution)/shard_map/ppermute | solution.py:252
  6.3 6.5 %collective-permute-start.2 = (bf16[272,256]{1,0:T(8,128)(2,1)S(1)}, bf16[272,256]{1,0:T(8,128)(2,1)S(1)}, u32[]{:S(2)}, u32[]{:S(2)}) collective-permute-start(bf16[272,256]{1,0:T(8,128)(2,1)S(1)} %get-tuple-element.41), channel_id=1, source_target_pairs={{0,12},{4,8},{8,4},{12,0},{16,28},{20,24},{24,20},{28,16},{1,13},{... | collective-permute-start | bytes 417800 | tf_op jit(solution)/shard_map/ppermute | solution.py:252
  8.7 7.8 %collective-permute-start.3 = (bf16[256,256]{1,0:T(8,128)(2,1)S(1)}, bf16[256,256]{1,0:T(8,128)(2,1)S(1)}, u32[]{:S(2)}, u32[]{:S(2)}) collective-permute-start(bf16[256,256]{1,0:T(8,128)(2,1)S(1)} %get-tuple-element.46), channel_id=1, source_target_pairs={{0,4},{4,0},{8,12},{12,8},{16,20},{20,16},{24,28},{28,24},{1,5},{5... | collective-permute-start | bytes 393224 | tf_op jit(solution)/shard_map/ppermute | solution.py:252
  10.6 9.1 %collective-permute-start.4 = (bf16[256,256]{1,0:T(8,128)(2,1)S(1)}, bf16[256,256]{1,0:T(8,128)(2,1)S(1)}, u32[]{:S(2)}, u32[]{:S(2)}) collective-permute-start(bf16[256,256]{1,0:T(8,128)(2,1)S(1)} %get-tuple-element.47), channel_id=1, source_target_pairs={{0,8},{4,12},{8,0},{12,4},{16,24},{20,28},{24,16},{28,20},{1,9},{5... | collective-permute-start | bytes 393224 | tf_op jit(solution)/shard_map/ppermute | solution.py:252
  12.2 8.1 %collective-permute-start.5 = (bf16[256,256]{1,0:T(8,128)(2,1)S(1)}, bf16[256,256]{1,0:T(8,128)(2,1)S(1)}, u32[]{:S(2)}, u32[]{:S(2)}) collective-permute-start(bf16[256,256]{1,0:T(8,128)(2,1)S(1)} %get-tuple-element.48), channel_id=1, source_target_pairs={{0,12},{4,8},{8,4},{12,0},{16,28},{20,24},{24,20},{28,16},{1,13},{... | collective-permute-start | bytes 393224 | tf_op jit(solution)/shard_map/ppermute | solution.py:252
  13.7 11.8 %collective-permute-start.7 = (bf16[256,256]{1,0:T(8,128)(2,1)S(1)}, bf16[256,256]{1,0:T(8,128)(2,1)S(1)}, u32[]{:S(2)}, u32[]{:S(2)}) collective-permute-start(bf16[256,256]{1,0:T(8,128)(2,1)S(1)} %get-tuple-element.51), channel_id=1, source_target_pairs={{0,16},{4,20},{8,24},{12,28},{16,0},{20,4},{24,8},{28,12},{1,17},{... | collective-permute-start | bytes 393224 | tf_op jit(solution)/shard_map/ppermute | solution.py:262
  20.6 6.5 %collective-permute-start.6 = (bf16[256,256]{1,0:T(8,128)(2,1)S(1)}, bf16[256,256]{1,0:T(8,128)(2,1)S(1)}, u32[]{:S(2)}, u32[]{:S(2)}) collective-permute-start(bf16[256,256]{1,0:T(8,128)(2,1)S(1)} %second_state.1), channel_id=1, source_target_pairs={{0,16},{4,20},{8,24},{12,28},{1,17},{5,21},{9,25},{13,29},{2,18},{... | collective-permute-start | bytes 393224 | tf_op jit(solution)/shard_map/ppermute | solution.py:262
  27.3 6.4 %collective-permute-start.8 = (bf16[128,512]{1,0:T(8,128)(2,1)S(1)}, bf16[128,512]{1,0:T(8,128)(2,1)S(1)}, u32[]{:S(2)}, u32[]{:S(2)}) collective-permute-start(bf16[128,512]{1,0:T(8,128)(2,1)S(1)} %get-tuple-element.54), channel_id=1, source_target_pairs={{0,4},{4,0},{8,12},{12,8},{16,20},{20,16},{24,28},{28,24},{1,5},{5... | collective-permute-start | bytes 393224 | tf_op jit(solution)/shard_map/ppermute | solution.py:252
  29.0 5.8 %collective-permute-start.9 = (bf16[128,512]{1,0:T(8,128)(2,1)S(1)}, bf16[128,512]{1,0:T(8,128)(2,1)S(1)}, u32[]{:S(2)}, u32[]{:S(2)}) collective-permute-start(bf16[128,512]{1,0:T(8,128)(2,1)S(1)} %get-tuple-element.55), channel_id=1, source_target_pairs={{0,8},{4,12},{8,0},{12,4},{16,24},{20,28},{24,16},{28,20},{1,9},{5... | collective-permute-start | bytes 393224 | tf_op jit(solution)/shard_map/ppermute | solution.py:252
  31.8 5.9 %collective-permute-start.10 = (bf16[128,512]{1,0:T(8,128)(2,1)S(1)}, bf16[128,512]{1,0:T(8,128)(2,1)S(1)}, u32[]{:S(2)}, u32[]{:S(2)}) collective-permute-start(bf16[128,512]{1,0:T(8,128)(2,1)S(1)} %get-tuple-element.56), channel_id=1, source_target_pairs={{0,12},{4,8},{8,4},{12,0},{16,28},{20,24},{24,20},{28,16},{1,13},{... | collective-permute-start | bytes 393224 | tf_op jit(solution)/shard_map/ppermute | solution.py:252
  38.6 3.4 %collective-permute-start.17 = (bf16[64,1024]{1,0:T(8,128)(2,1)S(1)}, bf16[64,1024]{1,0:T(8,128)(2,1)S(1)}, u32[]{:S(2)}, u32[]{:S(2)}) collective-permute-start(bf16[64,1024]{1,0:T(8,128)(2,1)S(1)} %get-tuple-element.64), channel_id=1, source_target_pairs={{0,1},{1,0},{2,3},{3,2},{4,5},{5,4},{6,7},{7,6},{8,9},{9,8},{10,11... | collective-permute-start | bytes 393224 | tf_op jit(solution)/shard_map/ppermute | solution.py:252
  39.5 4.3 %collective-permute-start.15 = (bf16[64,1024]{1,0:T(8,128)(2,1)S(1)}, bf16[64,1024]{1,0:T(8,128)(2,1)S(1)}, u32[]{:S(2)}, u32[]{:S(2)}) collective-permute-start(bf16[64,1024]{1,0:T(8,128)(2,1)S(1)} %get-tuple-element.62), channel_id=1, source_target_pairs={{0,1},{1,0},{2,3},{3,2},{4,5},{5,4},{6,7},{7,6},{8,9},{9,8},{10,11... | collective-permute-start | bytes 393224 | tf_op jit(solution)/shard_map/ppermute | solution.py:252
  40.7 3.6 %collective-permute-start.13 = (bf16[64,1024]{1,0:T(8,128)(2,1)S(1)}, bf16[64,1024]{1,0:T(8,128)(2,1)S(1)}, u32[]{:S(2)}, u32[]{:S(2)}) collective-permute-start(bf16[64,1024]{1,0:T(8,128)(2,1)S(1)} %get-tuple-element.60), channel_id=1, source_target_pairs={{0,1},{1,0},{2,3},{3,2},{4,5},{5,4},{6,7},{7,6},{8,9},{9,8},{10,11... | collective-permute-start | bytes 393224 | tf_op jit(solution)/shard_map/ppermute | solution.py:252
  41.5 4.5 %collective-permute-start.11 = (bf16[64,1024]{1,0:T(8,128)(2,1)S(1)}, bf16[64,1024]{1,0:T(8,128)(2,1)S(1)}, u32[]{:S(2)}, u32[]{:S(2)}) collective-permute-start(bf16[64,1024]{1,0:T(8,128)(2,1)S(1)} %get-tuple-element.58), channel_id=1, source_target_pairs={{0,1},{1,0},{2,3},{3,2},{4,5},{5,4},{6,7},{7,6},{8,9},{9,8},{10,11... | collective-permute-start | bytes 393224 | tf_op jit(solution)/shard_map/ppermute | solution.py:252
  42.1 4.7 %collective-permute-start.18 = (bf16[32,1024]{1,0:T(8,128)(2,1)S(1)}, bf16[32,1024]{1,0:T(8,128)(2,1)S(1)}, u32[]{:S(2)}, u32[]{:S(2)}) collective-permute-start(bf16[32,1024]{1,0:T(8,128)(2,1)S(1)} %slice.60), channel_id=1, source_target_pairs={{0,2},{1,3},{2,0},{3,1},{4,6},{5,7},{6,4},{7,5},{8,10},{9,11},{10,... | collective-permute-start | bytes 196616 | tf_op jit(solution)/shard_map/ppermute | solution.py:252
  43.8 5.1 %collective-permute-start.16 = (bf16[32,1024]{1,0:T(8,128)(2,1)S(1)}, bf16[32,1024]{1,0:T(8,128)(2,1)S(1)}, u32[]{:S(2)}, u32[]{:S(2)}) collective-permute-start(bf16[32,1024]{1,0:T(8,128)(2,1)S(1)} %slice.61), channel_id=1, source_target_pairs={{0,2},{1,3},{2,0},{3,1},{4,6},{5,7},{6,4},{7,5},{8,10},{9,11},{10,... | collective-permute-start | bytes 196616 | tf_op jit(solution)/shard_map/ppermute | solution.py:252
  44.4 5.6 %collective-permute-start.14 = (bf16[32,1024]{1,0:T(8,128)(2,1)S(1)}, bf16[32,1024]{1,0:T(8,128)(2,1)S(1)}, u32[]{:S(2)}, u32[]{:S(2)}) collective-permute-start(bf16[32,1024]{1,0:T(8,128)(2,1)S(1)} %slice.62), channel_id=1, source_target_pairs={{0,2},{1,3},{2,0},{3,1},{4,6},{5,7},{6,4},{7,5},{8,10},{9,11},{10,... | collective-permute-start | bytes 196616 | tf_op jit(solution)/shard_map/ppermute | solution.py:252
  46.1 4.6 %collective-permute-start.12 = (bf16[32,1024]{1,0:T(8,128)(2,1)S(1)}, bf16[32,1024]{1,0:T(8,128)(2,1)S(1)}, u32[]{:S(2)}, u32[]{:S(2)}) collective-permute-start(bf16[32,1024]{1,0:T(8,128)(2,1)S(1)} %slice.63), channel_id=1, source_target_pairs={{0,2},{1,3},{2,0},{3,1},{4,6},{5,7},{6,4},{7,5},{8,10},{9,11},{10,... | collective-permute-start | bytes 196616 | tf_op jit(solution)/shard_map/ppermute | solution.py:252

commit v3 on v2

--- a/solution.py
+++ b/solution.py
@@ -9,7 +9,7 @@
 F32 = jnp.float32
 BF16 = jnp.bfloat16
 TAIL = 16
-PARTS = 4
+PARTS = 2
 SMEM = pl.BlockSpec(memory_space=pltpu.SMEM)
 VMEM = pl.BlockSpec(memory_space=pltpu.VMEM)
 HBM = pl.BlockSpec(memory_space=pltpu.HBM)
@@ -44,31 +44,25 @@
     return copies
 
 
-def pack_kernel(place_ref, owner_ref, decay_hbm, key_hbm, value_hbm, query_hbm, *refs):
-    decay_ref, key_ref, query_ref, sems, value_sems = refs[-5:]
-    count = (len(refs) - 5) // 2
-    first, second = refs[:count], refs[count : 2 * count]
-    rows, width = first[0].shape[0] // 2 - TAIL // 2, first[0].shape[1]
+def first_pack_kernel(place_ref, owner_ref, decay_hbm, key_hbm, value_hbm, *refs):
+    decay_ref, key_ref, sems = refs[-3:]
+    first = refs[:-3]
+    count = len(first)
+    rows, width = (first[0].shape[0] - TAIL) // 2, first[0].shape[1]
     place = place_ref[0] & (count - 1)
-    head_copies = fetch([(decay_hbm, decay_ref), (key_hbm, key_ref), (query_hbm, query_ref)], sems)
-    pairs = []
+    pairs = [(decay_hbm, decay_ref), (key_hbm, key_ref)]
     for hop in range(count):
-        head = place ^ hop
-        pairs.append((value_hbm.at[:, features(2 * head, width)], first[hop].at[rows : 2 * rows]))
-        pairs.append((value_hbm.at[:, features(2 * head + 1, width)], second[hop].at[0:rows]))
-    value_copies = fetch(pairs, value_sems)
+        pairs.append((value_hbm.at[:, features(2 * (place ^ hop), width)], first[hop].at[rows : 2 * rows]))
+    copies = fetch(pairs, sems)
     down, across = iotas(rows)
-    for copy in head_copies:
+    for copy in copies[:2]:
         copy.wait()
     for hop in range(count):
         head = place ^ hop
         decay = decay_ref[pl.ds(head, 1), :]
         after = jnp.sum(jnp.where(across > down, decay, 0.0), axis=1, keepdims=True)
-        upto = jnp.sum(jnp.where(across <= down, decay, 0.0), axis=1, keepdims=True)
         keys = key_ref[:, features(head, width)].astype(F32)
         first[hop][0:rows, :] = (keys * jnp.exp(after)).astype(BF16)
-        queries = query_ref[:, features(head, width)].astype(F32)
-        second[hop][rows : 2 * rows, :] = (queries * jnp.exp(upto)).astype(BF16)
         whole = jnp.exp(jnp.sum(decay, axis=1, keepdims=True))
         whole = jnp.broadcast_to(whole, (TAIL, width))
         high = whole.astype(BF16).astype(F32)
@@ -77,7 +71,30 @@
         row = lax.broadcasted_iota(jnp.int32, (TAIL, width), 0)
         tail = jnp.where(row == 0, high, jnp.where(row == 1, middle, jnp.where(row == 2, low, 0.0)))
         first[hop][2 * rows :, :] = tail.astype(BF16)
-    for copy in value_copies:
+    for copy in copies[2:]:
+        copy.wait()
+
+
+def second_pack_kernel(place_ref, decay_hbm, query_hbm, value_hbm, *refs):
+    decay_ref, query_ref, sems = refs[-3:]
+    second = refs[:-3]
+    count = len(second)
+    rows, width = second[0].shape[0] // 2, second[0].shape[1]
+    place = place_ref[0] & (count - 1)
+    pairs = [(decay_hbm, decay_ref), (query_hbm, query_ref)]
+    for hop in range(count):
+        pairs.append((value_hbm.at[:, features(2 * (place ^ hop) + 1, width)], second[hop].at[0:rows]))
+    copies = fetch(pairs, sems)
+    down, across = iotas(rows)
+    for copy in copies[:2]:
+        copy.wait()
+    for hop in range(count):
+        head = place ^ hop
+        decay = decay_ref[pl.ds(head, 1), :]
+        upto = jnp.sum(jnp.where(across <= down, decay, 0.0), axis=1, keepdims=True)
+        queries = query_ref[:, features(head, width)].astype(F32)
+        second[hop][rows : 2 * rows, :] = (queries * jnp.exp(upto)).astype(BF16)
+    for copy in copies[2:]:
         copy.wait()
 
 
@@ -157,22 +174,12 @@
         scaled_ref[here, :] = (queries.astype(F32) * decays[block][0:1]).astype(BF16)
 
 
-def crossed(place_ref, state_ref, scaled_ref, part_ref, group):
+def cross_kernel(place_ref, state_ref, scaled_ref, part_ref, *out_refs):
+    rows = out_refs[0].shape[0]
     carried = jnp.dot(scaled_ref[...], state_ref[...], preferred_element_type=F32)
-    return (part_ref[...] + jnp.where(place_ref[0] < group, 0.0, carried)).astype(BF16)
-
-
-def left_cross_kernel(place_ref, state_ref, scaled_ref, part_ref, out_ref, *, group):
-    out_ref[...] = crossed(place_ref, state_ref, scaled_ref, part_ref, group)
-
-
-def right_cross_kernel(place_ref, state_ref, scaled_ref, part_ref, left_ref, *out_refs):
-    rows, width = out_refs[0].shape
-    right = crossed(place_ref, state_ref, scaled_ref, part_ref, len(out_refs))
+    total = part_ref[...] + jnp.where(place_ref[0] < len(out_refs), 0.0, carried)
     for hop, out_ref in enumerate(out_refs):
-        here = slice(hop * rows, (hop + 1) * rows)
-        out_ref[:, : width // 2] = left_ref[here, :]
-        out_ref[:, width // 2 :] = right[here, :]
+        out_ref[...] = total[hop * rows : (hop + 1) * rows, :].astype(BF16)
 
 
 def block_kernel(*refs):
@@ -212,10 +219,11 @@
         swish_ref[:, here] = gate / (1.0 + jnp.exp(-gate))
 
 
-def mix_kernel(place_ref, owner_ref, inner_ref, swish_ref, part_ref, out_ref, mixed, *, hop, group, owners):
-    rows, value_dim = out_ref.shape
+def mix(place_ref, owner_ref, inner_ref, swish_ref, part_refs, mixed, hop, group, owners):
+    rows, value_dim = mixed.shape
     here = features((place_ref[0] & (group - 1)) ^ hop, value_dim)
-    retained = inner_ref[:, here] + part_ref[...].astype(F32)
+    part = jnp.concatenate([part_ref[...] for part_ref in part_refs], axis=1)
+    retained = inner_ref[:, here] + part.astype(F32)
     mean = jnp.mean(retained, axis=1, keepdims=True)
     centered = retained - mean
     variance = jnp.mean(centered * centered, axis=1, keepdims=True)
@@ -228,26 +236,66 @@
         mask = sum(((flipped >> bit) & 1) << (bits - 1 - bit) for bit in range(bits))
         start = pl.multiple_of((owner_ref[0] ^ mask) * share, share)
         pieces.append(mixed[pl.ds(start, share), :])
-    out_ref[...] = jnp.concatenate(pieces, axis=0).astype(BF16)
-
-
-def project_kernel(place_ref, *refs, part):
-    weight_ref, send_ref, keep_ref = refs[-3:]
-    half, width = send_ref.shape
-    place = place_ref[0] & (len(refs) - 4)
+    return jnp.concatenate(pieces, axis=0).astype(BF16)
+
+
+def head_product(place_ref, rows, weight_ref, hop, group, start, tile):
+    depth = rows.shape[1]
+    return jnp.dot(
+        rows,
+        weight_ref[features((place_ref[0] & (group - 1)) ^ hop, depth), start : start + tile],
+        preferred_element_type=F32,
+    )
+
+
+def add_head_kernel(*refs, hop, group, owners):
+    place_ref, owner_ref, inner_ref, swish_ref, weight_ref = refs[:5]
+    before, part_refs = refs[5 : 5 + (hop > 0)], refs[5 + (hop > 0) : -2]
+    total_ref, mixed = refs[-2:]
+    rows = mix(place_ref, owner_ref, inner_ref, swish_ref, part_refs, mixed, hop, group, owners)
+    width = total_ref.shape[1]
     tile = min(512, width)
     for start in range(0, width, tile):
         here = slice(start, start + tile)
-        out = None
-        for hop, rows_ref in enumerate(refs[:-3]):
-            depth = rows_ref.shape[1]
-            there = pl.ds(pl.multiple_of((place ^ hop) * depth, depth), depth)
-            term = jnp.dot(rows_ref[...], weight_ref[there, slice(part * width + start, part * width + start + tile)], preferred_element_type=F32)
-            out = term if out is None else out + term
+        term = head_product(place_ref, rows, weight_ref, hop, group, start, tile)
+        total_ref[:, here] = before[0][:, here] + term if before else term
+
+
+def finish_part(place_ref, rows, weight_ref, totals, send_ref, keep_ref, part, late, group):
+    half, width = send_ref.shape
+    tile = min(512, width)
+    for start in range(0, width, tile):
+        here = slice(start, start + tile)
+        there = part * width + start
+        terms = [
+            head_product(place_ref, rows_ref[...], weight_ref, hop, group, there, tile)
+            for hop, rows_ref in zip(late, rows)
+        ]
+        terms += [total_ref[:, there : there + tile] for total_ref in totals]
+        out = functools.reduce(jnp.add, terms)
         send_ref[:, here] = out[:half].astype(BF16)
         keep_ref[:, here] = out[half:].astype(BF16)
 
 
+def first_part_kernel(*refs, late, group, owners):
+    place_ref, owner_ref, inner_ref, swish_ref, weight_ref = refs[:5]
+    count = len(late)
+    totals, part_refs = refs[5 : 5 + (late[0] > 0)], refs[5 + (late[0] > 0) : -3 - count]
+    send_ref, keep_ref, mixed = refs[-3 - count], refs[-2 - count], refs[-1]
+    rows = refs[-1 - count : -1]
+    each = len(part_refs) // count
+    for at, (hop, rows_ref) in enumerate(zip(late, rows)):
+        mine = part_refs[at * each : (at + 1) * each]
+        rows_ref[...] = mix(place_ref, owner_ref, inner_ref, swish_ref, mine, mixed, hop, group, owners)
+    finish_part(place_ref, rows, weight_ref, totals, send_ref, keep_ref, 0, late, group)
+
+
+def other_part_kernel(place_ref, weight_ref, *refs, part, late, group):
+    count = len(late)
+    send_ref, keep_ref = refs[-2:]
+    finish_part(place_ref, refs[:count], weight_ref, refs[count:-2], send_ref, keep_ref, part, late, group)
+
+
 def swap(value, axis, size, mask):
     return lax.ppermute(value, axis, [(i, i ^ mask) for i in range(size)])
 
@@ -256,10 +304,9 @@
     return [swap(values[hop], axis, size, hop) for hop in range(1, len(values))]
 
 
-def carried_into(state, whole, axis, size, group, wrap):
+def carried_into(state, whole, axis, size, group):
     def shift(value, by):
-        count = size if wrap else size - by * group
-        return lax.ppermute(value, axis, [(i, (i + by * group) % size) for i in range(count)])
+        return lax.ppermute(value, axis, [(i, (i + by * group) % size) for i in range(size)])
 
     groups = size // group
     if groups == 1:
@@ -303,25 +350,39 @@
     owner = lax.axis_index("head").astype(jnp.int32).reshape(1)
     shape = jax.ShapeDtypeStruct
 
-    packed = pl.pallas_call(
-        pack_kernel,
-        out_shape=[shape((2 * rows + TAIL, key_dim), BF16)] * group + [shape((2 * rows, key_dim), BF16)] * group,
-        in_specs=[SMEM] * 2 + [HBM] * 4,
-        out_specs=[VMEM] * (2 * group),
+    def after(value):
+        return lax.optimization_barrier((decay, value))[0]
+
+    first = pl.pallas_call(
+        first_pack_kernel,
+        out_shape=[shape((2 * rows + TAIL, key_dim), BF16)] * group,
+        in_specs=[SMEM] * 2 + [HBM] * 3,
+        out_specs=[VMEM] * group,
         scratch_shapes=[
             pltpu.VMEM(decay.shape, F32),
             pltpu.VMEM(key.shape, BF16),
-            pltpu.VMEM(query.shape, BF16),
-            pltpu.SemaphoreType.DMA((3,)),
-            pltpu.SemaphoreType.DMA((2 * group,)),
+            pltpu.SemaphoreType.DMA((2 + group,)),
         ],
         compiler_params=params(8),
-        name="pack",
-    )(place, owner, *in_hbm(decay, key, value, query))
-    def after(value):
-        return lax.optimization_barrier((decay, value))[0]
-
-    token = after(packed[0])
+        cost_estimate=cost(5 * 10**9, 2**24),
+        name="first_pack",
+    )(place, owner, *in_hbm(decay, key, value))
+    second = pl.pallas_call(
+        second_pack_kernel,
+        out_shape=[shape((2 * rows, key_dim), BF16)] * group,
+        in_specs=[SMEM] + [HBM] * 3,
+        out_specs=[VMEM] * group,
+        scratch_shapes=[
+            pltpu.VMEM(decay.shape, F32),
+            pltpu.VMEM(query.shape, BF16),
+            pltpu.SemaphoreType.DMA((2 + group,)),
+        ],
+        compiler_params=params(8),
+        name="second_pack",
+    )(place, *in_hbm(after(first[0]), query, value))
+    first = [first[0]] + swaps(first, "ctx", ctx)
+    second = [second[0]] + swaps(second, "ctx", ctx)
+    token = after(first[min(1, group - 1)])
     inner, swish = pl.pallas_call(
         block_kernel,
         out_shape=[shape(value.shape, F32)] * 2,
@@ -340,19 +401,17 @@
         name="block_part",
     )(*in_hbm(token, query, key, value, gate))
 
-    first = swaps(packed[:group], "ctx", ctx)
-    later, _ = lax.optimization_barrier((packed[group:], inner))
-    second = [packed[group]] + swaps(later, "ctx", ctx)
-    first = [packed[0]] + first
+    first, inner = lax.optimization_barrier((first, inner))
     left_state, whole = pl.pallas_call(
         functools.partial(first_state_kernel, rows=rows),
         out_shape=[shape((key_dim, key_dim), BF16), shape((8, key_dim), F32)],
         in_specs=[SMEM] + [VMEM] * group,
         out_specs=[VMEM] * 2,
         compiler_params=params(8),
+        cost_estimate=cost(5*10**9, 2**24),
         name="first_state",
     )(place, *first)
-    left_carried = carried_into(left_state, whole, "ctx", ctx, group, True)
+    left_carried = carried_into(left_state, whole, "ctx", ctx, group)
 
     right_state = pl.pallas_call(
         functools.partial(second_state_kernel, rows=rows),
@@ -360,9 +419,10 @@
         in_specs=[SMEM] + [VMEM] * (2 * group),
         out_specs=VMEM,
         compiler_params=params(8),
+        cost_estimate=cost(5*10**9, 2**24),
         name="second_state",
     )(place, *first, *second)
-    right_carried = carried_into(right_state, whole, "ctx", ctx, group, False)
+    right_carried = carried_into(right_state, whole, "ctx", ctx, group)
 
     left_part, right_part, scaled = pl.pallas_call(
         functools.partial(group_kernel, rows=rows),
@@ -379,47 +439,60 @@
         name="group_part",
     )(place, *first, *second)
 
-    left_cross = pl.pallas_call(
-        functools.partial(left_cross_kernel, group=group),
-        out_shape=shape((group * rows, key_dim), BF16),
-        in_specs=[SMEM] + [VMEM] * 3,
-        out_specs=VMEM,
-        compiler_params=params(8),
-        name="left_cross",
-    )(place, left_carried, scaled, left_part)
-    parts = pl.pallas_call(
-        right_cross_kernel,
-        out_shape=[shape((rows, value_dim), BF16)] * group,
-        in_specs=[SMEM] + [VMEM] * 4,
-        out_specs=[VMEM] * group,
-        compiler_params=params(8),
-        name="right_cross",
-    )(place, right_carried, scaled, right_part, left_cross)
-    parts = [parts[0]] + swaps(parts, "ctx", ctx)
-
-    mixed_rows = [
-        pl.pallas_call(
-            functools.partial(mix_kernel, hop=hop, group=group, owners=head),
-            out_shape=shape((rows, value_dim), BF16),
-            in_specs=[SMEM] * 2 + [VMEM] * 3,
-            out_specs=VMEM,
-            scratch_shapes=[pltpu.VMEM((rows, value_dim), F32)],
-            compiler_params=params(4),
-            name="mix",
-        )(place, owner, inner, swish, parts[hop])
-        for hop in range(group)
-    ]
+    def cross(carried, part, name):
+        parts = pl.pallas_call(
+            cross_kernel,
+            out_shape=[shape((rows, key_dim), BF16)] * group,
+            in_specs=[SMEM] + [VMEM] * 3,
+            out_specs=[VMEM] * group,
+            compiler_params=params(8),
+            name=name,
+        )(place, carried, scaled, part)
+        return [parts[0]] + swaps(parts, "ctx", ctx)
+
+    left_parts = cross(left_carried, left_part, "left_cross")
+    right_parts = cross(right_carried, right_part, "right_cross")
+    inner, left_parts = lax.optimization_barrier((inner, left_parts))
+    parts = list(zip(left_parts, right_parts))
+    late = list(range(group))[-2:]
+    total = []
+    for hop in range(late[0]):
+        total = [
+            pl.pallas_call(
+                functools.partial(add_head_kernel, hop=hop, group=group, owners=head),
+                out_shape=shape((rows, width), F32),
+                in_specs=[SMEM] * 2 + [VMEM] * (3 + len(total) + len(parts[hop])),
+                out_specs=VMEM,
+                input_output_aliases={5: 0} if total else {},
+                scratch_shapes=[pltpu.VMEM((rows, value_dim), F32)],
+                compiler_params=params(4),
+                cost_estimate=cost(2**29, 2**22),
+                name="add_head",
+            )(place, owner, inner, swish, weight, *total, *parts[hop])
+        ]
+    late_parts = [piece for hop in late for piece in parts[hop]]
     outs = []
+    halves = [shape((rows // 2, width // PARTS), BF16)] * 2
     for part in range(PARTS):
-        send, keep = pl.pallas_call(
-            functools.partial(project_kernel, part=part),
-            out_shape=[shape((rows // 2, width // PARTS), BF16)] * 2,
-            in_specs=[SMEM] + [VMEM] * (group + 1),
-            out_specs=[VMEM] * 2,
-            compiler_params=params(4),
-            cost_estimate=cost(2**29, 2**22),
-            name="project",
-        )(place, *mixed_rows, weight)
+        if part == 0:
+            send, keep, *last_rows = pl.pallas_call(
+                functools.partial(first_part_kernel, late=late, group=group, owners=head),
+                out_shape=halves + [shape((rows, value_dim), BF16)] * len(late),
+                in_specs=[SMEM] * 2 + [VMEM] * (3 + len(total) + len(late_parts)),
+                out_specs=[VMEM] * (2 + len(late)),
+                scratch_shapes=[pltpu.VMEM((rows, value_dim), F32)],
+                compiler_params=params(4),
+                name="first_part",
+            )(place, owner, inner, swish, weight, *total, *late_parts)
+        else:
+            send, keep = pl.pallas_call(
+                functools.partial(other_part_kernel, part=part, late=late, group=group),
+                out_shape=halves,
+                in_specs=[SMEM] + [VMEM] * (1 + len(late) + len(total)),
+                out_specs=[VMEM] * 2,
+                compiler_params=params(4),
+                name="other_part",
+            )(place, weight, *last_rows, *total)
         outs.append(reduce_over(send, keep, "head", head))
     return jnp.concatenate(outs, axis=1)
 

time: 51.6 us -> 48 us (0.930)
  waiting for transfers between devices: 15 us -> 11.9 us
  starting transfers between devices: 24.9 us -> 23.9 us
    ppermute x17 -> x16, waiting for transfers between devices: 13.7 us -> 10.3 us  [swap(): return lax.ppermute(value, axis, [(i, i ^ mask) for i in range(size)])]
    ppermute x2, starting transfers between devices: 6.73 us -> 5.01 us  [shift(): lax.ppermute(value, axis, [(i, (i + by * group) % size) for i in range(si...]
    ppermute x17 -> x16, starting transfers between devices: 18.2 us -> 18.9 us  [swap(): return lax.ppermute(value, axis, [(i, i ^ mask) for i in range(size)])]
    pallas_call x11 -> x8, Pallas kernels: 5.97 us -> 6.44 us  [the longest x2 1.89 us: local(): pl.pallas_call(functools.partial(add_head_kernel, hop=hop, group=group, o...]
  transfers between devices with their start and end apart: 19 -> 18, of which waited for: 11 -> 10; matrix products, arithmetic and copies ran while one was open for 0% -> 0% of each run, Pallas kernels for 15% -> 18%
where the time goes in v3:
time: 48 us; the launch traced here: 47.8 us
  starting transfers between devices  23.9 us (50%)
  waiting for transfers between devices  11.9 us (25%)
  Pallas kernels  10.9 us (23%)
  other arithmetic  0.89 us (2%)
    ppermute x16, starting transfers between devices, swap(): return lax.ppermute(value, axis, [(i, i ^ mask) for i in range(size)])  18.9 us
    ppermute x16, waiting for transfers between devices, swap(): return lax.ppermute(value, axis, [(i, i ^ mask) for i in range(size)])  10.3 us
    ppermute x2, starting transfers between devices, shift(): lax.ppermute(value, axis, [(i, (i + by * group) % size) for i in range(si...  5.01 us
    pallas_call x1, Pallas kernels, local(): pl.pallas_call(block_kernel, out_shape=[shape(value.shape, F32)] * 2, in_...  2.31 us
    pallas_call x2, Pallas kernels, local(): pl.pallas_call(functools.partial(add_head_kernel, hop=hop, group=group, o...  1.89 us
    ppermute x2, waiting for transfers between devices, shift(): lax.ppermute(value, axis, [(i, (i + by * group) % size) for i in range(si...  1.62 us
    pallas_call x1, Pallas kernels, local(): pl.pallas_call(first_pack_kernel, out_shape=[shape((2 * rows + TAIL, key_...  1.18 us
    pallas_call x1, Pallas kernels, local(): pl.pallas_call(second_pack_kernel, out_shape=[shape((2 * rows, key_dim),...  1.18 us
  transfers between devices with their start and end apart: 18, of which 10 were waited for; matrix products, arithmetic and copies ran while one was open for 0% of the time, Pallas kernels for 18%

profile of v3, /device:TPU:0, one launch (start us, length us, event | category | flops | bytes accessed | tf_op | source)
XLA Modules:
  0.0 47.8 jit_solution(1190211103699771181)
XLA Ops:
  0.0 1.2 %first_pack.1 = (bf16[272,256]{1,0:T(8,128)(2,1)S(1)}, bf16[272,256]{1,0:T(8,128)(2,1)S(1)}, bf16[272,256]{1,0:T(8,128)(2,1)S(1)}, bf16[272,256]{1,0:T(8,128)(2,1)S(1)}) custom-call(s32[1]{0:T(128)} %bitcast.place_ref.refs_0_, s32[1]{0:T(128)} %bitcast.1.owner_ref.refs_1_, f32[4,128]{1,0:T(4,128)} %decay_hbm.2, bf16[128,1024]{1,0:T(8,128)(2,1)} %refs_2_.1, ...), custom_call_target="tpu_custom_call" | custom-call | flops 5000000000 | bytes 16777216 | tf_op jit(solution)/shard_map/first_pack/pallas_call | solution.py:356
  1.2 3.0 %collective-permute-start = (bf16[272,256]{1,0:T(8,128)(2,1)S(1)}, bf16[272,256]{1,0:T(8,128)(2,1)S(1)}, u32[]{:S(2)}, u32[]{:S(2)}) collective-permute-start(bf16[272,256]{1,0:T(8,128)(2,1)S(1)} %get-tuple-element.46), channel_id=1, source_target_pairs={{0,4},{4,0},{8,12},{12,8},{16,20},{20,16},{24,28},{28,24},{1,5},{5... | collective-permute-start | bytes 417800 | tf_op jit(solution)/shard_map/ppermute | solution.py:300
  4.2 1.6 %collective-permute-start.1 = (bf16[272,256]{1,0:T(8,128)(2,1)S(1)}, bf16[272,256]{1,0:T(8,128)(2,1)S(1)}, u32[]{:S(2)}, u32[]{:S(2)}) collective-permute-start(bf16[272,256]{1,0:T(8,128)(2,1)S(1)} %get-tuple-element.47), channel_id=1, source_target_pairs={{0,8},{4,12},{8,0},{12,4},{16,24},{20,28},{24,16},{28,20},{1,9},{5... | collective-permute-start | bytes 417800 | tf_op jit(solution)/shard_map/ppermute | solution.py:300
  5.8 1.2 %second_pack.1 = (bf16[256,256]{1,0:T(8,128)(2,1)S(1)}, bf16[256,256]{1,0:T(8,128)(2,1)S(1)}, bf16[256,256]{1,0:T(8,128)(2,1)S(1)}, bf16[256,256]{1,0:T(8,128)(2,1)S(1)}) custom-call(s32[1]{0:T(128)} %bitcast.place_ref.refs_0_, f32[4,128]{1,0:T(4,128)} %decay_hbm.2, bf16[128,1024]{1,0:T(8,128)(2,1)} %query_hbm.1, bf16[128,2048]{1,0:T(8,128)(2,1)} %value_hbm.3), custom_call_target="tpu_custom_call" | custom-call | tf_op jit(solution)/shard_map/second_pack/pallas_call | solution.py:370
  7.0 2.0 %collective-permute-start.4 = (bf16[256,256]{1,0:T(8,128)(2,1)S(1)}, bf16[256,256]{1,0:T(8,128)(2,1)S(1)}, u32[]{:S(2)}, u32[]{:S(2)}) collective-permute-start(bf16[256,256]{1,0:T(8,128)(2,1)S(1)} %get-tuple-element.59), channel_id=1, source_target_pairs={{0,4},{4,0},{8,12},{12,8},{16,20},{20,16},{24,28},{28,24},{1,5},{5... | collective-permute-start | bytes 393224 | tf_op jit(solution)/shard_map/ppermute | solution.py:300
  8.9 1.6 %collective-permute-start.5 = (bf16[256,256]{1,0:T(8,128)(2,1)S(1)}, bf16[256,256]{1,0:T(8,128)(2,1)S(1)}, u32[]{:S(2)}, u32[]{:S(2)}) collective-permute-start(bf16[256,256]{1,0:T(8,128)(2,1)S(1)} %get-tuple-element.60), channel_id=1, source_target_pairs={{0,8},{4,12},{8,0},{12,4},{16,24},{20,28},{24,16},{28,20},{1,9},{5... | collective-permute-start | bytes 393224 | tf_op jit(solution)/shard_map/ppermute | solution.py:300
  10.9 2.3 %block_part.1 = (f32[128,2048]{1,0:T(8,128)S(1)}, f32[128,2048]{1,0:T(8,128)S(1)}) custom-call(f32[4,128]{1,0:T(4,128)} %decay_hbm.2, bf16[128,1024]{1,0:T(8,128)(2,1)} %query_hbm.1, bf16[128,1024]{1,0:T(8,128)(2,1)} %refs_2_.1, bf16[128,2048]{1,0:T(8,128)(2,1)} %value_hbm.3, bf16[128,2048]{1,0:T(8,128)(2,1)} %refs_4_.4), custom_call_target="tpu_custom_call" | custom-call | flops 1000000000 | bytes 4194304 | tf_op jit(solution)/shard_map/block_part/pallas_call | solution.py:386
  14.2 2.6 %collective-permute-start.3 = (bf16[256,256]{1,0:T(8,128)(2,1)S(1)}, bf16[256,256]{1,0:T(8,128)(2,1)S(1)}, u32[]{:S(2)}, u32[]{:S(2)}) collective-permute-start(bf16[256,256]{1,0:T(8,128)(2,1)S(1)} %get-tuple-element.56), channel_id=1, source_target_pairs={{0,16},{4,20},{8,24},{12,28},{16,0},{20,4},{24,8},{28,12},{1,17},{... | collective-permute-start | bytes 393224 | tf_op jit(solution)/shard_map/ppermute | solution.py:309
  16.8 1.1 %collective-permute-done.5.refs_6_ = bf16[256,256]{1,0:T(8,128)(2,1)S(1)} collective-permute-done((bf16[256,256]{1,0:T(8,128)(2,1)S(1)}, bf16[256,256]{1,0:T(8,128)(2,1)S(1)}, u32[]{:S(2)}, u32[]{:S(2)}) %collective-permute-start.5) | collective-permute-done | bytes 131104 | tf_op jit(solution)/shard_map/ppermute | solution.py:300
  17.9 1.3 %collective-permute-done.6.refs_7_ = bf16[256,256]{1,0:T(8,128)(2,1)S(1)} collective-permute-done((bf16[256,256]{1,0:T(8,128)(2,1)S(1)}, bf16[256,256]{1,0:T(8,128)(2,1)S(1)}, u32[]{:S(2)}, u32[]{:S(2)}) %collective-permute-start.6) | collective-permute-done | bytes 131104 | tf_op jit(solution)/shard_map/ppermute | solution.py:300
  19.5 2.4 %collective-permute-start.10 = (bf16[256,256]{1,0:T(8,128)(2,1)S(1)}, bf16[256,256]{1,0:T(8,128)(2,1)S(1)}, u32[]{:S(2)}, u32[]{:S(2)}) collective-permute-start(bf16[256,256]{1,0:T(8,128)(2,1)S(1)} %second_state.1), channel_id=1, source_target_pairs={{0,16},{4,20},{8,24},{12,28},{16,0},{20,4},{24,8},{28,12},{1,17},{... | collective-permute-start | bytes 393224 | tf_op jit(solution)/shard_map/ppermute | solution.py:309
  21.9 0.9 %group_part.1 = (f32[512,256]{1,0:T(8,128)S(1)}, f32[512,256]{1,0:T(8,128)S(1)}, bf16[512,256]{1,0:T(8,128)(2,1)S(1)}) custom-call(s32[1]{0:T(128)} %bitcast.place_ref.refs_0_, bf16[272,256]{1,0:T(8,128)(2,1)S(1)} %get-tuple-element.52.refs_0_, bf16[272,256]{1,0:T(8,128)(2,1)S(1)} %collective-permute-done.refs_1_, ...), custom_call_target="tpu_custom_call" | custom-call | flops 1000000000 | bytes 4194304 | tf_op jit(solution)/shard_map/group_part/pallas_call | solution.py:427
  22.9 1.5 %collective-permute-done.3.state_ref = bf16[256,256]{1,0:T(8,128)(2,1)S(1)} collective-permute-done((bf16[256,256]{1,0:T(8,128)(2,1)S(1)}, bf16[256,256]{1,0:T(8,128)(2,1)S(1)}, u32[]{:S(2)}, u32[]{:S(2)}) %collective-permute-start.3) | collective-permute-done | bytes 131104 | tf_op jit(solution)/shard_map/ppermute | solution.py:309
  24.6 2.2 %collective-permute-start.7 = (bf16[128,256]{1,0:T(8,128)(2,1)S(1)}, bf16[128,256]{1,0:T(8,128)(2,1)S(1)}, u32[]{:S(2)}, u32[]{:S(2)}) collective-permute-start(bf16[128,256]{1,0:T(8,128)(2,1)S(1)} %get-tuple-element.65), channel_id=1, source_target_pairs={{0,4},{4,0},{8,12},{12,8},{16,20},{20,16},{24,28},{28,24},{1,5},{5... | collective-permute-start | bytes 196616 | tf_op jit(solution)/shard_map/ppermute | solution.py:300
  27.0 1.4 %collective-permute-start.9 = (bf16[128,256]{1,0:T(8,128)(2,1)S(1)}, bf16[128,256]{1,0:T(8,128)(2,1)S(1)}, u32[]{:S(2)}, u32[]{:S(2)}) collective-permute-start(bf16[128,256]{1,0:T(8,128)(2,1)S(1)} %get-tuple-element.67), channel_id=1, source_target_pairs={{0,12},{4,8},{8,4},{12,0},{16,28},{20,24},{24,20},{28,16},{1,13},{... | collective-permute-start | bytes 196616 | tf_op jit(solution)/shard_map/ppermute | solution.py:300
  28.7 1.9 %collective-permute-start.11 = (bf16[128,256]{1,0:T(8,128)(2,1)S(1)}, bf16[128,256]{1,0:T(8,128)(2,1)S(1)}, u32[]{:S(2)}, u32[]{:S(2)}) collective-permute-start(bf16[128,256]{1,0:T(8,128)(2,1)S(1)} %get-tuple-element.74), channel_id=1, source_target_pairs={{0,4},{4,0},{8,12},{12,8},{16,20},{20,16},{24,28},{28,24},{1,5},{5... | collective-permute-start | bytes 196616 | tf_op jit(solution)/shard_map/ppermute | solution.py:300
  30.8 1.5 %collective-permute-start.13 = (bf16[128,256]{1,0:T(8,128)(2,1)S(1)}, bf16[128,256]{1,0:T(8,128)(2,1)S(1)}, u32[]{:S(2)}, u32[]{:S(2)}) collective-permute-start(bf16[128,256]{1,0:T(8,128)(2,1)S(1)} %get-tuple-element.78), channel_id=1, source_target_pairs={{0,12},{4,8},{8,4},{12,0},{16,28},{20,24},{24,20},{28,16},{1,13},{... | collective-permute-start | bytes 196616 | tf_op jit(solution)/shard_map/ppermute | solution.py:300
  32.3 0.9 %add_head.2.refs_5_ = f32[128,4096]{1,0:T(8,128)S(1)} custom-call(s32[1]{0:T(128)} %bitcast.place_ref.refs_0_, s32[1]{0:T(128)} %bitcast.1.owner_ref.refs_1_, f32[128,2048]{1,0:T(8,128)S(1)} %get-tuple-element.68.refs_2_, f32[128,2048]{1,0:T(8,128)S(1)} %get-tuple-element.69.refs_3_, bf16[2048,4096]{1,0:T(8,128)(2,1)S(1)} %bitcast.3, ...), custom_call_target="tpu_custom_call" | custom-call | flops 536870912 | bytes 4194304 | tf_op jit(solution)/shard_map/add_head/pallas_call | solution.py:461
  34.0 1.0 %add_head.3.refs_5_.refs_2_ = f32[128,4096]{1,0:T(8,128)S(1)} custom-call(s32[1]{0:T(128)} %bitcast.place_ref.refs_0_, s32[1]{0:T(128)} %bitcast.1.owner_ref.refs_1_, f32[128,2048]{1,0:T(8,128)S(1)} %get-tuple-element.68.refs_2_, f32[128,2048]{1,0:T(8,128)S(1)} %get-tuple-element.69.refs_3_, ...), custom_call_target="tpu_custom_call", output_to_operand_aliasing={{}: (5, {})} | custom-call | flops 536870912 | bytes 4194304 | tf_op jit(solution)/shard_map/add_head/pallas_call | solution.py:461
  35.1 0.9 %collective-permute-done.13.refs_9_ = bf16[128,256]{1,0:T(8,128)(2,1)S(1)} collective-permute-done((bf16[128,256]{1,0:T(8,128)(2,1)S(1)}, bf16[128,256]{1,0:T(8,128)(2,1)S(1)}, u32[]{:S(2)}, u32[]{:S(2)}) %collective-permute-start.13) | collective-permute-done | bytes 65568 | tf_op jit(solution)/shard_map/ppermute | solution.py:300
  36.0 1.0 %first_part.1 = (bf16[64,2048]{1,0:T(8,128)(2,1)S(1)}, bf16[64,2048]{1,0:T(8,128)(2,1)S(1)}, bf16[128,512]{1,0:T(8,128)(2,1)S(1)}, bf16[128,512]{1,0:T(8,128)(2,1)S(1)}) custom-call(s32[1]{0:T(128)} %bitcast.place_ref.refs_0_, s32[1]{0:T(128)} %bitcast.1.owner_ref.refs_1_, f32[128,2048]{1,0:T(8,128)S(1)} %get-tuple-element.68.refs_2_, ...), custom_call_target="tpu_custom_call" | custom-call | tf_op jit(solution)/shard_map/first_part/pallas_call | solution.py:478
  38.7 1.6 %collective-permute-start.15 = (bf16[32,2048]{1,0:T(8,128)(2,1)S(1)}, bf16[32,2048]{1,0:T(8,128)(2,1)S(1)}, u32[]{:S(2)}, u32[]{:S(2)}) collective-permute-start(bf16[32,2048]{1,0:T(8,128)(2,1)S(1)} %slice.31), channel_id=1, source_target_pairs={{0,2},{1,3},{2,0},{3,1},{4,6},{5,7},{6,4},{7,5},{8,10},{9,11},{10,... | collective-permute-start | bytes 393224 | tf_op jit(solution)/shard_map/ppermute | solution.py:300
  41.2 3.9 %collective-permute-done.15 = bf16[32,2048]{1,0:T(8,128)(2,1)S(1)} collective-permute-done((bf16[32,2048]{1,0:T(8,128)(2,1)S(1)}, bf16[32,2048]{1,0:T(8,128)(2,1)S(1)}, u32[]{:S(2)}, u32[]{:S(2)}) %collective-permute-start.15) | collective-permute-done | bytes 131104 | tf_op jit(solution)/shard_map/ppermute | solution.py:300
  45.1 2.0 %collective-permute-done.17 = bf16[32,2048]{1,0:T(8,128)(2,1)S(1)} collective-permute-done((bf16[32,2048]{1,0:T(8,128)(2,1)S(1)}, bf16[32,2048]{1,0:T(8,128)(2,1)S(1)}, u32[]{:S(2)}, u32[]{:S(2)}) %collective-permute-start.17) | collective-permute-done | bytes 131104 | tf_op jit(solution)/shard_map/ppermute | solution.py:300
  (40 shorter events, 6.8 us)
Async XLA Ops:
  1.2 9.3 %collective-permute-start = (bf16[272,256]{1,0:T(8,128)(2,1)S(1)}, bf16[272,256]{1,0:T(8,128)(2,1)S(1)}, u32[]{:S(2)}, u32[]{:S(2)}) collective-permute-start(bf16[272,256]{1,0:T(8,128)(2,1)S(1)} %get-tuple-element.46), channel_id=1, source_target_pairs={{0,4},{4,0},{8,12},{12,8},{16,20},{20,16},{24,28},{28,24},{1,5},{5... | collective-permute-start | bytes 417800 | tf_op jit(solution)/shard_map/ppermute | solution.py:300
  4.2 9.0 %collective-permute-start.1 = (bf16[272,256]{1,0:T(8,128)(2,1)S(1)}, bf16[272,256]{1,0:T(8,128)(2,1)S(1)}, u32[]{:S(2)}, u32[]{:S(2)}) collective-permute-start(bf16[272,256]{1,0:T(8,128)(2,1)S(1)} %get-tuple-element.47), channel_id=1, source_target_pairs={{0,8},{4,12},{8,0},{12,4},{16,24},{20,28},{24,16},{28,20},{1,9},{5... | collective-permute-start | bytes 417800 | tf_op jit(solution)/shard_map/ppermute | solution.py:300
  5.8 7.6 %collective-permute-start.2 = (bf16[272,256]{1,0:T(8,128)(2,1)S(1)}, bf16[272,256]{1,0:T(8,128)(2,1)S(1)}, u32[]{:S(2)}, u32[]{:S(2)}) collective-permute-start(bf16[272,256]{1,0:T(8,128)(2,1)S(1)} %get-tuple-element.48), channel_id=1, source_target_pairs={{0,12},{4,8},{8,4},{12,0},{16,28},{20,24},{24,20},{28,16},{1,13},{... | collective-permute-start | bytes 417800 | tf_op jit(solution)/shard_map/ppermute | solution.py:300
  7.0 9.8 %collective-permute-start.4 = (bf16[256,256]{1,0:T(8,128)(2,1)S(1)}, bf16[256,256]{1,0:T(8,128)(2,1)S(1)}, u32[]{:S(2)}, u32[]{:S(2)}) collective-permute-start(bf16[256,256]{1,0:T(8,128)(2,1)S(1)} %get-tuple-element.59), channel_id=1, source_target_pairs={{0,4},{4,0},{8,12},{12,8},{16,20},{20,16},{24,28},{28,24},{1,5},{5... | collective-permute-start | bytes 393224 | tf_op jit(solution)/shard_map/ppermute | solution.py:300
  8.9 9.0 %collective-permute-start.5 = (bf16[256,256]{1,0:T(8,128)(2,1)S(1)}, bf16[256,256]{1,0:T(8,128)(2,1)S(1)}, u32[]{:S(2)}, u32[]{:S(2)}) collective-permute-start(bf16[256,256]{1,0:T(8,128)(2,1)S(1)} %get-tuple-element.60), channel_id=1, source_target_pairs={{0,8},{4,12},{8,0},{12,4},{16,24},{20,28},{24,16},{28,20},{1,9},{5... | collective-permute-start | bytes 393224 | tf_op jit(solution)/shard_map/ppermute | solution.py:300
  10.5 8.7 %collective-permute-start.6 = (bf16[256,256]{1,0:T(8,128)(2,1)S(1)}, bf16[256,256]{1,0:T(8,128)(2,1)S(1)}, u32[]{:S(2)}, u32[]{:S(2)}) collective-permute-start(bf16[256,256]{1,0:T(8,128)(2,1)S(1)} %get-tuple-element.61), channel_id=1, source_target_pairs={{0,12},{4,8},{8,4},{12,0},{16,28},{20,24},{24,20},{28,16},{1,13},{... | collective-permute-start | bytes 393224 | tf_op jit(solution)/shard_map/ppermute | solution.py:300
  13.3 19.0 %slice-start = ((s8[16777216]{0:T(1024)(128)(4,1)}), s8[4194304]{0:T(1024)(128)(4,1)S(1)}, s32[]{:S(2)}) async-start(s8[16777216]{0:T(1024)(128)(4,1)} %bitcast.2), calls=%async_computation | async-start | bytes 8388608
  13.3 19.0 %slice-start.1 = ((s8[16777216]{0:T(1024)(128)(4,1)}), s8[4194304]{0:T(1024)(128)(4,1)S(1)}, s32[]{:S(2)}) async-start(s8[16777216]{0:T(1024)(128)(4,1)} %bitcast.2), calls=%async_computation.1 | async-start | bytes 8388608
  14.2 10.2 %collective-permute-start.3 = (bf16[256,256]{1,0:T(8,128)(2,1)S(1)}, bf16[256,256]{1,0:T(8,128)(2,1)S(1)}, u32[]{:S(2)}, u32[]{:S(2)}) collective-permute-start(bf16[256,256]{1,0:T(8,128)(2,1)S(1)} %get-tuple-element.56), channel_id=1, source_target_pairs={{0,16},{4,20},{8,24},{12,28},{16,0},{20,4},{24,8},{28,12},{1,17},{... | collective-permute-start | bytes 393224 | tf_op jit(solution)/shard_map/ppermute | solution.py:309
  19.2 13.1 %slice-start.2 = ((s8[16777216]{0:T(1024)(128)(4,1)}), s8[4194304]{0:T(1024)(128)(4,1)S(1)}, s32[]{:S(2)}) async-start(s8[16777216]{0:T(1024)(128)(4,1)} %bitcast.2), calls=%async_computation.2 | async-start | bytes 8388608
  19.2 13.1 %slice-start.3 = ((s8[16777216]{0:T(1024)(128)(4,1)}), s8[4194304]{0:T(1024)(128)(4,1)S(1)}, s32[]{:S(2)}) async-start(s8[16777216]{0:T(1024)(128)(4,1)} %bitcast.2), calls=%async_computation.3 | async-start | bytes 8388608
  19.5 9.0 %collective-permute-start.10 = (bf16[256,256]{1,0:T(8,128)(2,1)S(1)}, bf16[256,256]{1,0:T(8,128)(2,1)S(1)}, u32[]{:S(2)}, u32[]{:S(2)}) collective-permute-start(bf16[256,256]{1,0:T(8,128)(2,1)S(1)} %second_state.1), channel_id=1, source_target_pairs={{0,16},{4,20},{8,24},{12,28},{16,0},{20,4},{24,8},{28,12},{1,17},{... | collective-permute-start | bytes 393224 | tf_op jit(solution)/shard_map/ppermute | solution.py:309
  24.6 6.2 %collective-permute-start.7 = (bf16[128,256]{1,0:T(8,128)(2,1)S(1)}, bf16[128,256]{1,0:T(8,128)(2,1)S(1)}, u32[]{:S(2)}, u32[]{:S(2)}) collective-permute-start(bf16[128,256]{1,0:T(8,128)(2,1)S(1)} %get-tuple-element.65), channel_id=1, source_target_pairs={{0,4},{4,0},{8,12},{12,8},{16,20},{20,16},{24,28},{28,24},{1,5},{5... | collective-permute-start | bytes 196616 | tf_op jit(solution)/shard_map/ppermute | solution.py:300
  26.8 5.5 %collective-permute-start.8 = (bf16[128,256]{1,0:T(8,128)(2,1)S(1)}, bf16[128,256]{1,0:T(8,128)(2,1)S(1)}, u32[]{:S(2)}, u32[]{:S(2)}) collective-permute-start(bf16[128,256]{1,0:T(8,128)(2,1)S(1)} %get-tuple-element.66), channel_id=1, source_target_pairs={{0,8},{4,12},{8,0},{12,4},{16,24},{20,28},{24,16},{28,20},{1,9},{5... | collective-permute-start | bytes 196616 | tf_op jit(solution)/shard_map/ppermute | solution.py:300
  27.0 5.3 %collective-permute-start.9 = (bf16[128,256]{1,0:T(8,128)(2,1)S(1)}, bf16[128,256]{1,0:T(8,128)(2,1)S(1)}, u32[]{:S(2)}, u32[]{:S(2)}) collective-permute-start(bf16[128,256]{1,0:T(8,128)(2,1)S(1)} %get-tuple-element.67), channel_id=1, source_target_pairs={{0,12},{4,8},{8,4},{12,0},{16,28},{20,24},{24,20},{28,16},{1,13},{... | collective-permute-start | bytes 196616 | tf_op jit(solution)/shard_map/ppermute | solution.py:300
  28.7 5.3 %collective-permute-start.11 = (bf16[128,256]{1,0:T(8,128)(2,1)S(1)}, bf16[128,256]{1,0:T(8,128)(2,1)S(1)}, u32[]{:S(2)}, u32[]{:S(2)}) collective-permute-start(bf16[128,256]{1,0:T(8,128)(2,1)S(1)} %get-tuple-element.74), channel_id=1, source_target_pairs={{0,4},{4,0},{8,12},{12,8},{16,20},{20,16},{24,28},{28,24},{1,5},{5... | collective-permute-start | bytes 196616 | tf_op jit(solution)/shard_map/ppermute | solution.py:300
  30.6 4.4 %collective-permute-start.12 = (bf16[128,256]{1,0:T(8,128)(2,1)S(1)}, bf16[128,256]{1,0:T(8,128)(2,1)S(1)}, u32[]{:S(2)}, u32[]{:S(2)}) collective-permute-start(bf16[128,256]{1,0:T(8,128)(2,1)S(1)} %get-tuple-element.76), channel_id=1, source_target_pairs={{0,8},{4,12},{8,0},{12,4},{16,24},{20,28},{24,16},{28,20},{1,9},{5... | collective-permute-start | bytes 196616 | tf_op jit(solution)/shard_map/ppermute | solution.py:300
  30.8 5.2 %collective-permute-start.13 = (bf16[128,256]{1,0:T(8,128)(2,1)S(1)}, bf16[128,256]{1,0:T(8,128)(2,1)S(1)}, u32[]{:S(2)}, u32[]{:S(2)}) collective-permute-start(bf16[128,256]{1,0:T(8,128)(2,1)S(1)} %get-tuple-element.78), channel_id=1, source_target_pairs={{0,12},{4,8},{8,4},{12,0},{16,28},{20,24},{24,20},{28,16},{1,13},{... | collective-permute-start | bytes 196616 | tf_op jit(solution)/shard_map/ppermute | solution.py:300
  37.0 1.6 %collective-permute-start.14 = (bf16[64,2048]{1,0:T(8,128)(2,1)S(1)}, bf16[64,2048]{1,0:T(8,128)(2,1)S(1)}, u32[]{:S(2)}, u32[]{:S(2)}) collective-permute-start(bf16[64,2048]{1,0:T(8,128)(2,1)S(1)} %get-tuple-element.80), channel_id=1, source_target_pairs={{0,1},{1,0},{2,3},{3,2},{4,5},{5,4},{6,7},{7,6},{8,9},{9,8},{10,11... | collective-permute-start | bytes 786440 | tf_op jit(solution)/shard_map/ppermute | solution.py:300
  37.8 2.4 %collective-permute-start.16 = (bf16[64,2048]{1,0:T(8,128)(2,1)S(1)}, bf16[64,2048]{1,0:T(8,128)(2,1)S(1)}, u32[]{:S(2)}, u32[]{:S(2)}) collective-permute-start(bf16[64,2048]{1,0:T(8,128)(2,1)S(1)} %get-tuple-element.84), channel_id=1, source_target_pairs={{0,1},{1,0},{2,3},{3,2},{4,5},{5,4},{6,7},{7,6},{8,9},{9,8},{10,11... | collective-permute-start | bytes 786440 | tf_op jit(solution)/shard_map/ppermute | solution.py:300
  38.7 6.4 %collective-permute-start.15 = (bf16[32,2048]{1,0:T(8,128)(2,1)S(1)}, bf16[32,2048]{1,0:T(8,128)(2,1)S(1)}, u32[]{:S(2)}, u32[]{:S(2)}) collective-permute-start(bf16[32,2048]{1,0:T(8,128)(2,1)S(1)} %slice.31), channel_id=1, source_target_pairs={{0,2},{1,3},{2,0},{3,1},{4,6},{5,7},{6,4},{7,5},{8,10},{9,11},{10,... | collective-permute-start | bytes 393224 | tf_op jit(solution)/shard_map/ppermute | solution.py:300
  40.3 6.7 %collective-permute-start.17 = (bf16[32,2048]{1,0:T(8,128)(2,1)S(1)}, bf16[32,2048]{1,0:T(8,128)(2,1)S(1)}, u32[]{:S(2)}, u32[]{:S(2)}) collective-permute-start(bf16[32,2048]{1,0:T(8,128)(2,1)S(1)} %slice.30), channel_id=1, source_target_pairs={{0,2},{1,3},{2,0},{3,1},{4,6},{5,7},{6,4},{7,5},{8,10},{9,11},{10,... | collective-permute-start | bytes 393224 | tf_op jit(solution)/shard_map/ppermute | solution.py:300

commit v4 on v3

--- a/solution.py
+++ b/solution.py
@@ -9,7 +9,6 @@
 F32 = jnp.float32
 BF16 = jnp.bfloat16
 TAIL = 16
-PARTS = 2
 SMEM = pl.BlockSpec(memory_space=pltpu.SMEM)
 VMEM = pl.BlockSpec(memory_space=pltpu.VMEM)
 HBM = pl.BlockSpec(memory_space=pltpu.HBM)
@@ -132,7 +131,7 @@
     whole_ref[...] = jnp.broadcast_to(whole, whole_ref.shape)
 
 
-def second_state_kernel(place_ref, *refs, rows):
+def second_state_kernel(place_ref, token_ref, *refs, rows):
     count = (len(refs) - 1) // 2
     first, second, state_ref = refs[:count], refs[count : 2 * count], refs[-1]
     values = [message[0:rows, :] for message in second]
@@ -183,8 +182,8 @@
 
 
 def block_kernel(*refs):
-    decay_hbm, query_hbm, key_hbm, value_hbm, gate_hbm, inner_ref, swish_ref = refs[:7]
-    decay_ref, query_ref, key_ref, value_ref, gate_ref, sems = refs[7:]
+    _, decay_hbm, query_hbm, key_hbm, value_hbm, gate_hbm, inner_ref, swish_ref, token_ref = refs[:9]
+    decay_ref, query_ref, key_ref, value_ref, gate_ref, sems = refs[9:]
     rows = query_ref.shape[0]
     heads = decay_ref.shape[0]
     key_dim, value_dim = query_ref.shape[1] // heads, value_ref.shape[1] // heads
@@ -217,6 +216,7 @@
         )
         gate = gate_ref[:, here].astype(F32)
         swish_ref[:, here] = gate / (1.0 + jnp.exp(-gate))
+    token_ref[...] = jnp.zeros_like(token_ref)
 
 
 def mix(place_ref, owner_ref, inner_ref, swish_ref, part_refs, mixed, hop, group, owners):
@@ -261,12 +261,12 @@
         total_ref[:, here] = before[0][:, here] + term if before else term
 
 
-def finish_part(place_ref, rows, weight_ref, totals, send_ref, keep_ref, part, late, group):
+def finish_part(place_ref, rows, weight_ref, totals, send_ref, keep_ref, offset, late, group):
     half, width = send_ref.shape
     tile = min(512, width)
     for start in range(0, width, tile):
         here = slice(start, start + tile)
-        there = part * width + start
+        there = offset + start
         terms = [
             head_product(place_ref, rows_ref[...], weight_ref, hop, group, there, tile)
             for hop, rows_ref in zip(late, rows)
@@ -290,10 +290,10 @@
     finish_part(place_ref, rows, weight_ref, totals, send_ref, keep_ref, 0, late, group)
 
 
-def other_part_kernel(place_ref, weight_ref, *refs, part, late, group):
+def other_part_kernel(place_ref, weight_ref, *refs, offset, late, group):
     count = len(late)
     send_ref, keep_ref = refs[-2:]
-    finish_part(place_ref, refs[:count], weight_ref, refs[count:-2], send_ref, keep_ref, part, late, group)
+    finish_part(place_ref, refs[:count], weight_ref, refs[count:-2], send_ref, keep_ref, offset, late, group)
 
 
 def swap(value, axis, size, mask):
@@ -382,12 +382,22 @@
     )(place, *in_hbm(after(first[0]), query, value))
     first = [first[0]] + swaps(first, "ctx", ctx)
     second = [second[0]] + swaps(second, "ctx", ctx)
-    token = after(first[min(1, group - 1)])
-    inner, swish = pl.pallas_call(
+    left_state, whole = pl.pallas_call(
+        functools.partial(first_state_kernel, rows=rows),
+        out_shape=[shape((key_dim, key_dim), BF16), shape((8, key_dim), F32)],
+        in_specs=[SMEM] + [VMEM] * group,
+        out_specs=[VMEM] * 2,
+        compiler_params=params(8),
+        cost_estimate=cost(5*10**9, 2**24),
+        name="first_state",
+    )(place, *first)
+    left_carried = carried_into(left_state, whole, "ctx", ctx, group)
+
+    inner, swish, token = pl.pallas_call(
         block_kernel,
-        out_shape=[shape(value.shape, F32)] * 2,
-        in_specs=[HBM] * 5,
-        out_specs=[VMEM] * 2,
+        out_shape=[shape(value.shape, F32)] * 2 + [shape((8, 128), F32)],
+        in_specs=[VMEM] + [HBM] * 5,
+        out_specs=[VMEM] * 3,
         scratch_shapes=[
             pltpu.VMEM(decay.shape, F32),
             pltpu.VMEM(query.shape, BF16),
@@ -399,29 +409,17 @@
         compiler_params=params(8),
         cost_estimate=cost(10**9, 4 * 2**20),
         name="block_part",
-    )(*in_hbm(token, query, key, value, gate))
-
-    first, inner = lax.optimization_barrier((first, inner))
-    left_state, whole = pl.pallas_call(
-        functools.partial(first_state_kernel, rows=rows),
-        out_shape=[shape((key_dim, key_dim), BF16), shape((8, key_dim), F32)],
-        in_specs=[SMEM] + [VMEM] * group,
-        out_specs=[VMEM] * 2,
-        compiler_params=params(8),
-        cost_estimate=cost(5*10**9, 2**24),
-        name="first_state",
-    )(place, *first)
-    left_carried = carried_into(left_state, whole, "ctx", ctx, group)
+    )(whole, *in_hbm(decay, query, key, value, gate))
 
     right_state = pl.pallas_call(
         functools.partial(second_state_kernel, rows=rows),
         out_shape=shape((key_dim, key_dim), BF16),
-        in_specs=[SMEM] + [VMEM] * (2 * group),
+        in_specs=[SMEM] + [VMEM] * (1 + 2 * group),
         out_specs=VMEM,
         compiler_params=params(8),
         cost_estimate=cost(5*10**9, 2**24),
         name="second_state",
-    )(place, *first, *second)
+    )(place, token, *first, *second)
     right_carried = carried_into(right_state, whole, "ctx", ctx, group)
 
     left_part, right_part, scaled = pl.pallas_call(
@@ -454,7 +452,7 @@
     right_parts = cross(right_carried, right_part, "right_cross")
     inner, left_parts = lax.optimization_barrier((inner, left_parts))
     parts = list(zip(left_parts, right_parts))
-    late = list(range(group))[-2:]
+    late = list(range(group))[-1:]
     total = []
     for hop in range(late[0]):
         total = [
@@ -466,14 +464,14 @@
                 input_output_aliases={5: 0} if total else {},
                 scratch_shapes=[pltpu.VMEM((rows, value_dim), F32)],
                 compiler_params=params(4),
-                cost_estimate=cost(2**29, 2**22),
                 name="add_head",
             )(place, owner, inner, swish, weight, *total, *parts[hop])
         ]
     late_parts = [piece for hop in late for piece in parts[hop]]
     outs = []
-    halves = [shape((rows // 2, width // PARTS), BF16)] * 2
-    for part in range(PARTS):
+    offset = 0
+    for part, columns in enumerate((width * 3 // 8, width * 5 // 8)):
+        halves = [shape((rows // 2, columns), BF16)] * 2
         if part == 0:
             send, keep, *last_rows = pl.pallas_call(
                 functools.partial(first_part_kernel, late=late, group=group, owners=head),
@@ -486,7 +484,7 @@
             )(place, owner, inner, swish, weight, *total, *late_parts)
         else:
             send, keep = pl.pallas_call(
-                functools.partial(other_part_kernel, part=part, late=late, group=group),
+                functools.partial(other_part_kernel, offset=offset, late=late, group=group),
                 out_shape=halves,
                 in_specs=[SMEM] + [VMEM] * (1 + len(late) + len(total)),
                 out_specs=[VMEM] * 2,
@@ -494,6 +492,7 @@
                 name="other_part",
             )(place, weight, *last_rows, *total)
         outs.append(reduce_over(send, keep, "head", head))
+        offset += columns
     return jnp.concatenate(outs, axis=1)
 
 

time: 48 us -> 47.6 us (level)
  waiting for transfers between devices: 11.9 us -> 10.7 us
  starting transfers between devices: 23.9 us -> 25 us
    ppermute x2, waiting for transfers between devices: 1.62 us -> 0.57 us  [shift(): lax.ppermute(value, axis, [(i, (i + by * group) % size) for i in range(si...]
    pallas_call x2 -> x3, Pallas kernels: 1.89 us -> 2.88 us  [local(): pl.pallas_call(functools.partial(add_head_kernel, hop=hop, group=group, o...]
    ppermute x16, starting transfers between devices: 18.9 us -> 19.9 us  [swap(): return lax.ppermute(value, axis, [(i, i ^ mask) for i in range(size)])]
    pallas_call x1, Pallas kernels: 0.87 us -> 0.33 us  [local(): pl.pallas_call(functools.partial(first_state_kernel, rows=rows), out_shap...]
  transfers between devices with their start and end apart: 18 -> 18, of which waited for: 10 -> 8; matrix products, arithmetic and copies ran while one was open for 0% -> 0% of each run, Pallas kernels for 18% -> 19%
where the time goes in v4:
time: 47.6 us; the launch traced here: 47.4 us
  starting transfers between devices  25 us (53%)
  Pallas kernels  10.7 us (22%)
  waiting for transfers between devices  10.7 us (22%)
  other arithmetic  0.88 us (2%)
    ppermute x16, starting transfers between devices, swap(): return lax.ppermute(value, axis, [(i, i ^ mask) for i in range(size)])  19.9 us
    ppermute x16, waiting for transfers between devices, swap(): return lax.ppermute(value, axis, [(i, i ^ mask) for i in range(size)])  10.1 us
    ppermute x2, starting transfers between devices, shift(): lax.ppermute(value, axis, [(i, (i + by * group) % size) for i in range(si...  5.07 us
    pallas_call x3, Pallas kernels, local(): pl.pallas_call(functools.partial(add_head_kernel, hop=hop, group=group, o...  2.88 us
    pallas_call x1, Pallas kernels, local(): pl.pallas_call(block_kernel, out_shape=[shape(value.shape, F32)] * 2 + [s...  2.31 us
    pallas_call x1, Pallas kernels, local(): pl.pallas_call(first_pack_kernel, out_shape=[shape((2 * rows + TAIL, key_...  1.18 us
    pallas_call x1, Pallas kernels, local(): pl.pallas_call(second_pack_kernel, out_shape=[shape((2 * rows, key_dim),...  1.18 us
  transfers between devices with their start and end apart: 18, of which 8 were waited for; matrix products, arithmetic and copies ran while one was open for 0% of the time, Pallas kernels for 19%

profile of v4, /device:TPU:0, one launch (start us, length us, event | category | flops | bytes accessed | tf_op | source)
XLA Modules:
  0.0 47.4 jit_solution(5301206262301374537)
XLA Ops:
  0.0 1.2 %first_pack.1 = (bf16[272,256]{1,0:T(8,128)(2,1)S(1)}, bf16[272,256]{1,0:T(8,128)(2,1)S(1)}, bf16[272,256]{1,0:T(8,128)(2,1)S(1)}, bf16[272,256]{1,0:T(8,128)(2,1)S(1)}) custom-call(s32[1]{0:T(128)} %bitcast.place_ref.refs_0_, s32[1]{0:T(128)} %bitcast.1.owner_ref.refs_1_, f32[4,128]{1,0:T(4,128)} %decay_hbm.2, bf16[128,1024]{1,0:T(8,128)(2,1)} %refs_3_.1, ...), custom_call_target="tpu_custom_call" | custom-call | flops 5000000000 | bytes 16777216 | tf_op jit(solution)/shard_map/first_pack/pallas_call | solution.py:356
  1.2 3.0 %collective-permute-start = (bf16[272,256]{1,0:T(8,128)(2,1)S(1)}, bf16[272,256]{1,0:T(8,128)(2,1)S(1)}, u32[]{:S(2)}, u32[]{:S(2)}) collective-permute-start(bf16[272,256]{1,0:T(8,128)(2,1)S(1)} %get-tuple-element.41), channel_id=1, source_target_pairs={{0,4},{4,0},{8,12},{12,8},{16,20},{20,16},{24,28},{28,24},{1,5},{5... | collective-permute-start | bytes 417800 | tf_op jit(solution)/shard_map/ppermute | solution.py:300
  4.2 1.6 %collective-permute-start.1 = (bf16[272,256]{1,0:T(8,128)(2,1)S(1)}, bf16[272,256]{1,0:T(8,128)(2,1)S(1)}, u32[]{:S(2)}, u32[]{:S(2)}) collective-permute-start(bf16[272,256]{1,0:T(8,128)(2,1)S(1)} %get-tuple-element.42), channel_id=1, source_target_pairs={{0,8},{4,12},{8,0},{12,4},{16,24},{20,28},{24,16},{28,20},{1,9},{5... | collective-permute-start | bytes 417800 | tf_op jit(solution)/shard_map/ppermute | solution.py:300
  5.8 1.2 %second_pack.1 = (bf16[256,256]{1,0:T(8,128)(2,1)S(1)}, bf16[256,256]{1,0:T(8,128)(2,1)S(1)}, bf16[256,256]{1,0:T(8,128)(2,1)S(1)}, bf16[256,256]{1,0:T(8,128)(2,1)S(1)}) custom-call(s32[1]{0:T(128)} %bitcast.place_ref.refs_0_, f32[4,128]{1,0:T(4,128)} %decay_hbm.2, bf16[128,1024]{1,0:T(8,128)(2,1)} %query_hbm.1, bf16[128,2048]{1,0:T(8,128)(2,1)} %value_hbm.3), custom_call_target="tpu_custom_call" | custom-call | tf_op jit(solution)/shard_map/second_pack/pallas_call | solution.py:370
  7.0 2.0 %collective-permute-start.4 = (bf16[256,256]{1,0:T(8,128)(2,1)S(1)}, bf16[256,256]{1,0:T(8,128)(2,1)S(1)}, u32[]{:S(2)}, u32[]{:S(2)}) collective-permute-start(bf16[256,256]{1,0:T(8,128)(2,1)S(1)} %get-tuple-element.49), channel_id=1, source_target_pairs={{0,4},{4,0},{8,12},{12,8},{16,20},{20,16},{24,28},{28,24},{1,5},{5... | collective-permute-start | bytes 393224 | tf_op jit(solution)/shard_map/ppermute | solution.py:300
  8.9 1.6 %collective-permute-start.5 = (bf16[256,256]{1,0:T(8,128)(2,1)S(1)}, bf16[256,256]{1,0:T(8,128)(2,1)S(1)}, u32[]{:S(2)}, u32[]{:S(2)}) collective-permute-start(bf16[256,256]{1,0:T(8,128)(2,1)S(1)} %get-tuple-element.50), channel_id=1, source_target_pairs={{0,8},{4,12},{8,0},{12,4},{16,24},{20,28},{24,16},{28,20},{1,9},{5... | collective-permute-start | bytes 393224 | tf_op jit(solution)/shard_map/ppermute | solution.py:300
  10.9 2.4 %collective-permute-done.2.refs_3_ = bf16[272,256]{1,0:T(8,128)(2,1)S(1)} collective-permute-done((bf16[272,256]{1,0:T(8,128)(2,1)S(1)}, bf16[272,256]{1,0:T(8,128)(2,1)S(1)}, u32[]{:S(2)}, u32[]{:S(2)}) %collective-permute-start.2) | collective-permute-done | bytes 139296 | tf_op jit(solution)/shard_map/ppermute | solution.py:300
  13.7 2.7 %collective-permute-start.3 = (bf16[256,256]{1,0:T(8,128)(2,1)S(1)}, bf16[256,256]{1,0:T(8,128)(2,1)S(1)}, u32[]{:S(2)}, u32[]{:S(2)}) collective-permute-start(bf16[256,256]{1,0:T(8,128)(2,1)S(1)} %get-tuple-element.46), channel_id=1, source_target_pairs={{0,16},{4,20},{8,24},{12,28},{16,0},{20,4},{24,8},{28,12},{1,17},{... | collective-permute-start | bytes 393224 | tf_op jit(solution)/shard_map/ppermute | solution.py:309
  16.3 2.3 %block_part.1 = (f32[128,2048]{1,0:T(8,128)S(1)}, f32[128,2048]{1,0:T(8,128)S(1)}, f32[8,128]{1,0:T(8,128)S(1)}) custom-call(f32[8,256]{1,0:T(8,128)S(1)} %get-tuple-element.44.refs_0_, f32[4,128]{1,0:T(4,128)} %decay_hbm.2, bf16[128,1024]{1,0:T(8,128)(2,1)} %query_hbm.1, bf16[128,1024]{1,0:T(8,128)(2,1)} %refs_3_.1, bf16[128,2048]{1,0:T(8,128)(2,1)} %value_hbm.3, ...), custom_call_target="tpu_custom_call" | custom-call | flops 1000000000 | bytes 4194304 | tf_op jit(solution)/shard_map/block_part/pallas_call | solution.py:396
  19.5 2.4 %collective-permute-start.10 = (bf16[256,256]{1,0:T(8,128)(2,1)S(1)}, bf16[256,256]{1,0:T(8,128)(2,1)S(1)}, u32[]{:S(2)}, u32[]{:S(2)}) collective-permute-start(bf16[256,256]{1,0:T(8,128)(2,1)S(1)} %second_state.1), channel_id=1, source_target_pairs={{0,16},{4,20},{8,24},{12,28},{16,0},{20,4},{24,8},{28,12},{1,17},{... | collective-permute-start | bytes 393224 | tf_op jit(solution)/shard_map/ppermute | solution.py:309
  21.9 0.9 %group_part.1 = (f32[512,256]{1,0:T(8,128)S(1)}, f32[512,256]{1,0:T(8,128)S(1)}, bf16[512,256]{1,0:T(8,128)(2,1)S(1)}) custom-call(s32[1]{0:T(128)} %bitcast.place_ref.refs_0_, bf16[272,256]{1,0:T(8,128)(2,1)S(1)} %get-tuple-element.40.refs_0_, bf16[272,256]{1,0:T(8,128)(2,1)S(1)} %collective-permute-done.refs_1_, ...), custom_call_target="tpu_custom_call" | custom-call | flops 1000000000 | bytes 4194304 | tf_op jit(solution)/shard_map/group_part/pallas_call | solution.py:425
  23.1 3.2 %collective-permute-start.7 = (bf16[128,256]{1,0:T(8,128)(2,1)S(1)}, bf16[128,256]{1,0:T(8,128)(2,1)S(1)}, u32[]{:S(2)}, u32[]{:S(2)}) collective-permute-start(bf16[128,256]{1,0:T(8,128)(2,1)S(1)} %get-tuple-element.55), channel_id=1, source_target_pairs={{0,4},{4,0},{8,12},{12,8},{16,20},{20,16},{24,28},{28,24},{1,5},{5... | collective-permute-start | bytes 196616 | tf_op jit(solution)/shard_map/ppermute | solution.py:300
  27.0 0.9 %collective-permute-start.9 = (bf16[128,256]{1,0:T(8,128)(2,1)S(1)}, bf16[128,256]{1,0:T(8,128)(2,1)S(1)}, u32[]{:S(2)}, u32[]{:S(2)}) collective-permute-start(bf16[128,256]{1,0:T(8,128)(2,1)S(1)} %get-tuple-element.57), channel_id=1, source_target_pairs={{0,12},{4,8},{8,4},{12,0},{16,28},{20,24},{24,20},{28,16},{1,13},{... | collective-permute-start | bytes 196616 | tf_op jit(solution)/shard_map/ppermute | solution.py:300
  28.6 1.5 %collective-permute-start.11 = (bf16[128,256]{1,0:T(8,128)(2,1)S(1)}, bf16[128,256]{1,0:T(8,128)(2,1)S(1)}, u32[]{:S(2)}, u32[]{:S(2)}) collective-permute-start(bf16[128,256]{1,0:T(8,128)(2,1)S(1)} %get-tuple-element.65), channel_id=1, source_target_pairs={{0,4},{4,0},{8,12},{12,8},{16,20},{20,16},{24,28},{28,24},{1,5},{5... | collective-permute-start | bytes 196616 | tf_op jit(solution)/shard_map/ppermute | solution.py:300
  30.8 1.4 %collective-permute-start.13 = (bf16[128,256]{1,0:T(8,128)(2,1)S(1)}, bf16[128,256]{1,0:T(8,128)(2,1)S(1)}, u32[]{:S(2)}, u32[]{:S(2)}) collective-permute-start(bf16[128,256]{1,0:T(8,128)(2,1)S(1)} %get-tuple-element.69), channel_id=1, source_target_pairs={{0,12},{4,8},{8,4},{12,0},{16,28},{20,24},{24,20},{28,16},{1,13},{... | collective-permute-start | bytes 196616 | tf_op jit(solution)/shard_map/ppermute | solution.py:300
  32.3 0.9 %add_head.3.refs_5_ = f32[128,4096]{1,0:T(8,128)S(1)} custom-call(s32[1]{0:T(128)} %bitcast.place_ref.refs_0_, s32[1]{0:T(128)} %bitcast.1.owner_ref.refs_1_, f32[128,2048]{1,0:T(8,128)S(1)} %get-tuple-element.58.refs_2_, f32[128,2048]{1,0:T(8,128)S(1)} %get-tuple-element.59.refs_3_, bf16[2048,4096]{1,0:T(8,128)(2,1)S(1)} %bitcast.3, ...), custom_call_target="tpu_custom_call" | custom-call | tf_op jit(solution)/shard_map/add_head/pallas_call | solution.py:459
  33.2 0.9 %collective-permute-done.11.refs_7_ = bf16[128,256]{1,0:T(8,128)(2,1)S(1)} collective-permute-done((bf16[128,256]{1,0:T(8,128)(2,1)S(1)}, bf16[128,256]{1,0:T(8,128)(2,1)S(1)}, u32[]{:S(2)}, u32[]{:S(2)}) %collective-permute-start.11) | collective-permute-done | bytes 65568 | tf_op jit(solution)/shard_map/ppermute | solution.py:300
  34.1 1.0 %add_head.4.refs_5_ = f32[128,4096]{1,0:T(8,128)S(1)} custom-call(s32[1]{0:T(128)} %bitcast.place_ref.refs_0_, s32[1]{0:T(128)} %bitcast.1.owner_ref.refs_1_, f32[128,2048]{1,0:T(8,128)S(1)} %get-tuple-element.58.refs_2_, f32[128,2048]{1,0:T(8,128)S(1)} %get-tuple-element.59.refs_3_, bf16[2048,4096]{1,0:T(8,128)(2,1)S(1)} %bitcast.3, ...), custom_call_target="tpu_custom_call", output_to_operand_aliasing={{}: (5, {})} | custom-call | tf_op jit(solution)/shard_map/add_head/pallas_call | solution.py:459
  35.1 1.0 %add_head.5.refs_5_.refs_1_ = f32[128,4096]{1,0:T(8,128)S(1)} custom-call(s32[1]{0:T(128)} %bitcast.place_ref.refs_0_, s32[1]{0:T(128)} %bitcast.1.owner_ref.refs_1_, f32[128,2048]{1,0:T(8,128)S(1)} %get-tuple-element.58.refs_2_, f32[128,2048]{1,0:T(8,128)S(1)} %get-tuple-element.59.refs_3_, ...), custom_call_target="tpu_custom_call", output_to_operand_aliasing={{}: (5, {})} | custom-call | tf_op jit(solution)/shard_map/add_head/pallas_call | solution.py:459
  38.3 1.6 %collective-permute-start.15 = (bf16[32,1536]{1,0:T(8,128)(2,1)S(1)}, bf16[32,1536]{1,0:T(8,128)(2,1)S(1)}, u32[]{:S(2)}, u32[]{:S(2)}) collective-permute-start(bf16[32,1536]{1,0:T(8,128)(2,1)S(1)} %slice.31), channel_id=1, source_target_pairs={{0,2},{1,3},{2,0},{3,1},{4,6},{5,7},{6,4},{7,5},{8,10},{9,11},{10,... | collective-permute-start | bytes 294920 | tf_op jit(solution)/shard_map/ppermute | solution.py:300
  40.0 0.9 %collective-permute-start.17 = (bf16[32,2560]{1,0:T(8,128)(2,1)S(1)}, bf16[32,2560]{1,0:T(8,128)(2,1)S(1)}, u32[]{:S(2)}, u32[]{:S(2)}) collective-permute-start(bf16[32,2560]{1,0:T(8,128)(2,1)S(1)} %slice.30), channel_id=1, source_target_pairs={{0,2},{1,3},{2,0},{3,1},{4,6},{5,7},{6,4},{7,5},{8,10},{9,11},{10,... | collective-permute-start | bytes 491528 | tf_op jit(solution)/shard_map/ppermute | solution.py:300
  40.8 3.1 %collective-permute-done.15 = bf16[32,1536]{1,0:T(8,128)(2,1)S(1)} collective-permute-done((bf16[32,1536]{1,0:T(8,128)(2,1)S(1)}, bf16[32,1536]{1,0:T(8,128)(2,1)S(1)}, u32[]{:S(2)}, u32[]{:S(2)}) %collective-permute-start.15) | collective-permute-done | bytes 98336 | tf_op jit(solution)/shard_map/ppermute | solution.py:300
  44.0 2.7 %collective-permute-done.17 = bf16[32,2560]{1,0:T(8,128)(2,1)S(1)} collective-permute-done((bf16[32,2560]{1,0:T(8,128)(2,1)S(1)}, bf16[32,2560]{1,0:T(8,128)(2,1)S(1)}, u32[]{:S(2)}, u32[]{:S(2)}) %collective-permute-start.17) | collective-permute-done | bytes 163872 | tf_op jit(solution)/shard_map/ppermute | solution.py:300
  46.7 0.7 %pad_maximum_fusion = bf16[32,4096]{1,0:T(8,128)(2,1)} fusion(bf16[32,2560]{1,0:T(8,128)(2,1)S(1)} %fusion, bf16[32,1536]{1,0:T(8,128)(2,1)S(1)} %fusion.1), kind=kLoop, calls=%fused_computation.5 | loop fusion | flops 524288 | bytes 524288 | tf_op jit(solution)/shard_map/concatenate | solution.py:496
  (41 shorter events, 6.3 us)
Async XLA Ops:
  1.2 9.3 %collective-permute-start = (bf16[272,256]{1,0:T(8,128)(2,1)S(1)}, bf16[272,256]{1,0:T(8,128)(2,1)S(1)}, u32[]{:S(2)}, u32[]{:S(2)}) collective-permute-start(bf16[272,256]{1,0:T(8,128)(2,1)S(1)} %get-tuple-element.41), channel_id=1, source_target_pairs={{0,4},{4,0},{8,12},{12,8},{16,20},{20,16},{24,28},{28,24},{1,5},{5... | collective-permute-start | bytes 417800 | tf_op jit(solution)/shard_map/ppermute | solution.py:300
  4.2 6.7 %collective-permute-start.1 = (bf16[272,256]{1,0:T(8,128)(2,1)S(1)}, bf16[272,256]{1,0:T(8,128)(2,1)S(1)}, u32[]{:S(2)}, u32[]{:S(2)}) collective-permute-start(bf16[272,256]{1,0:T(8,128)(2,1)S(1)} %get-tuple-element.42), channel_id=1, source_target_pairs={{0,8},{4,12},{8,0},{12,4},{16,24},{20,28},{24,16},{28,20},{1,9},{5... | collective-permute-start | bytes 417800 | tf_op jit(solution)/shard_map/ppermute | solution.py:300
  5.8 7.6 %collective-permute-start.2 = (bf16[272,256]{1,0:T(8,128)(2,1)S(1)}, bf16[272,256]{1,0:T(8,128)(2,1)S(1)}, u32[]{:S(2)}, u32[]{:S(2)}) collective-permute-start(bf16[272,256]{1,0:T(8,128)(2,1)S(1)} %get-tuple-element.43), channel_id=1, source_target_pairs={{0,12},{4,8},{8,4},{12,0},{16,28},{20,24},{24,20},{28,16},{1,13},{... | collective-permute-start | bytes 417800 | tf_op jit(solution)/shard_map/ppermute | solution.py:300
  7.0 11.7 %collective-permute-start.4 = (bf16[256,256]{1,0:T(8,128)(2,1)S(1)}, bf16[256,256]{1,0:T(8,128)(2,1)S(1)}, u32[]{:S(2)}, u32[]{:S(2)}) collective-permute-start(bf16[256,256]{1,0:T(8,128)(2,1)S(1)} %get-tuple-element.49), channel_id=1, source_target_pairs={{0,4},{4,0},{8,12},{12,8},{16,20},{20,16},{24,28},{28,24},{1,5},{5... | collective-permute-start | bytes 393224 | tf_op jit(solution)/shard_map/ppermute | solution.py:300
  8.9 9.7 %collective-permute-start.5 = (bf16[256,256]{1,0:T(8,128)(2,1)S(1)}, bf16[256,256]{1,0:T(8,128)(2,1)S(1)}, u32[]{:S(2)}, u32[]{:S(2)}) collective-permute-start(bf16[256,256]{1,0:T(8,128)(2,1)S(1)} %get-tuple-element.50), channel_id=1, source_target_pairs={{0,8},{4,12},{8,0},{12,4},{16,24},{20,28},{24,16},{28,20},{1,9},{5... | collective-permute-start | bytes 393224 | tf_op jit(solution)/shard_map/ppermute | solution.py:300
  10.5 8.7 %collective-permute-start.6 = (bf16[256,256]{1,0:T(8,128)(2,1)S(1)}, bf16[256,256]{1,0:T(8,128)(2,1)S(1)}, u32[]{:S(2)}, u32[]{:S(2)}) collective-permute-start(bf16[256,256]{1,0:T(8,128)(2,1)S(1)} %get-tuple-element.51), channel_id=1, source_target_pairs={{0,12},{4,8},{8,4},{12,0},{16,28},{20,24},{24,20},{28,16},{1,13},{... | collective-permute-start | bytes 393224 | tf_op jit(solution)/shard_map/ppermute | solution.py:300
  13.3 18.9 %slice-start = ((s8[16777216]{0:T(1024)(128)(4,1)}), s8[4194304]{0:T(1024)(128)(4,1)S(1)}, s32[]{:S(2)}) async-start(s8[16777216]{0:T(1024)(128)(4,1)} %bitcast.2), calls=%async_computation | async-start | bytes 8388608
  13.3 18.9 %slice-start.1 = ((s8[16777216]{0:T(1024)(128)(4,1)}), s8[4194304]{0:T(1024)(128)(4,1)S(1)}, s32[]{:S(2)}) async-start(s8[16777216]{0:T(1024)(128)(4,1)} %bitcast.2), calls=%async_computation.1 | async-start | bytes 8388608
  13.7 9.2 %collective-permute-start.3 = (bf16[256,256]{1,0:T(8,128)(2,1)S(1)}, bf16[256,256]{1,0:T(8,128)(2,1)S(1)}, u32[]{:S(2)}, u32[]{:S(2)}) collective-permute-start(bf16[256,256]{1,0:T(8,128)(2,1)S(1)} %get-tuple-element.46), channel_id=1, source_target_pairs={{0,16},{4,20},{8,24},{12,28},{16,0},{20,4},{24,8},{28,12},{1,17},{... | collective-permute-start | bytes 393224 | tf_op jit(solution)/shard_map/ppermute | solution.py:309
  19.2 13.1 %slice-start.2 = ((s8[16777216]{0:T(1024)(128)(4,1)}), s8[4194304]{0:T(1024)(128)(4,1)S(1)}, s32[]{:S(2)}) async-start(s8[16777216]{0:T(1024)(128)(4,1)} %bitcast.2), calls=%async_computation.2 | async-start | bytes 8388608
  19.2 13.1 %slice-start.3 = ((s8[16777216]{0:T(1024)(128)(4,1)}), s8[4194304]{0:T(1024)(128)(4,1)S(1)}, s32[]{:S(2)}) async-start(s8[16777216]{0:T(1024)(128)(4,1)} %bitcast.2), calls=%async_computation.3 | async-start | bytes 8388608
  19.5 8.9 %collective-permute-start.10 = (bf16[256,256]{1,0:T(8,128)(2,1)S(1)}, bf16[256,256]{1,0:T(8,128)(2,1)S(1)}, u32[]{:S(2)}, u32[]{:S(2)}) collective-permute-start(bf16[256,256]{1,0:T(8,128)(2,1)S(1)} %second_state.1), channel_id=1, source_target_pairs={{0,16},{4,20},{8,24},{12,28},{16,0},{20,4},{24,8},{28,12},{1,17},{... | collective-permute-start | bytes 393224 | tf_op jit(solution)/shard_map/ppermute | solution.py:309
  23.1 7.7 %collective-permute-start.7 = (bf16[128,256]{1,0:T(8,128)(2,1)S(1)}, bf16[128,256]{1,0:T(8,128)(2,1)S(1)}, u32[]{:S(2)}, u32[]{:S(2)}) collective-permute-start(bf16[128,256]{1,0:T(8,128)(2,1)S(1)} %get-tuple-element.55), channel_id=1, source_target_pairs={{0,4},{4,0},{8,12},{12,8},{16,20},{20,16},{24,28},{28,24},{1,5},{5... | collective-permute-start | bytes 196616 | tf_op jit(solution)/shard_map/ppermute | solution.py:300
  26.3 5.9 %collective-permute-start.8 = (bf16[128,256]{1,0:T(8,128)(2,1)S(1)}, bf16[128,256]{1,0:T(8,128)(2,1)S(1)}, u32[]{:S(2)}, u32[]{:S(2)}) collective-permute-start(bf16[128,256]{1,0:T(8,128)(2,1)S(1)} %get-tuple-element.56), channel_id=1, source_target_pairs={{0,8},{4,12},{8,0},{12,4},{16,24},{20,28},{24,16},{28,20},{1,9},{5... | collective-permute-start | bytes 196616 | tf_op jit(solution)/shard_map/ppermute | solution.py:300
  27.0 5.3 %collective-permute-start.9 = (bf16[128,256]{1,0:T(8,128)(2,1)S(1)}, bf16[128,256]{1,0:T(8,128)(2,1)S(1)}, u32[]{:S(2)}, u32[]{:S(2)}) collective-permute-start(bf16[128,256]{1,0:T(8,128)(2,1)S(1)} %get-tuple-element.57), channel_id=1, source_target_pairs={{0,12},{4,8},{8,4},{12,0},{16,28},{20,24},{24,20},{28,16},{1,13},{... | collective-permute-start | bytes 196616 | tf_op jit(solution)/shard_map/ppermute | solution.py:300
  28.6 5.4 %collective-permute-start.11 = (bf16[128,256]{1,0:T(8,128)(2,1)S(1)}, bf16[128,256]{1,0:T(8,128)(2,1)S(1)}, u32[]{:S(2)}, u32[]{:S(2)}) collective-permute-start(bf16[128,256]{1,0:T(8,128)(2,1)S(1)} %get-tuple-element.65), channel_id=1, source_target_pairs={{0,4},{4,0},{8,12},{12,8},{16,20},{20,16},{24,28},{28,24},{1,5},{5... | collective-permute-start | bytes 196616 | tf_op jit(solution)/shard_map/ppermute | solution.py:300
  30.1 5.0 %collective-permute-start.12 = (bf16[128,256]{1,0:T(8,128)(2,1)S(1)}, bf16[128,256]{1,0:T(8,128)(2,1)S(1)}, u32[]{:S(2)}, u32[]{:S(2)}) collective-permute-start(bf16[128,256]{1,0:T(8,128)(2,1)S(1)} %get-tuple-element.67), channel_id=1, source_target_pairs={{0,8},{4,12},{8,0},{12,4},{16,24},{20,28},{24,16},{28,20},{1,9},{5... | collective-permute-start | bytes 196616 | tf_op jit(solution)/shard_map/ppermute | solution.py:300
  30.8 5.3 %collective-permute-start.13 = (bf16[128,256]{1,0:T(8,128)(2,1)S(1)}, bf16[128,256]{1,0:T(8,128)(2,1)S(1)}, u32[]{:S(2)}, u32[]{:S(2)}) collective-permute-start(bf16[128,256]{1,0:T(8,128)(2,1)S(1)} %get-tuple-element.69), channel_id=1, source_target_pairs={{0,12},{4,8},{8,4},{12,0},{16,28},{20,24},{24,20},{28,16},{1,13},{... | collective-permute-start | bytes 196616 | tf_op jit(solution)/shard_map/ppermute | solution.py:300
  36.7 1.5 %collective-permute-start.14 = (bf16[64,1536]{1,0:T(8,128)(2,1)S(1)}, bf16[64,1536]{1,0:T(8,128)(2,1)S(1)}, u32[]{:S(2)}, u32[]{:S(2)}) collective-permute-start(bf16[64,1536]{1,0:T(8,128)(2,1)S(1)} %get-tuple-element.71), channel_id=1, source_target_pairs={{0,1},{1,0},{2,3},{3,2},{4,5},{5,4},{6,7},{7,6},{8,9},{9,8},{10,11... | collective-permute-start | bytes 589832 | tf_op jit(solution)/shard_map/ppermute | solution.py:300
  37.3 2.6 %collective-permute-start.16 = (bf16[64,2560]{1,0:T(8,128)(2,1)S(1)}, bf16[64,2560]{1,0:T(8,128)(2,1)S(1)}, u32[]{:S(2)}, u32[]{:S(2)}) collective-permute-start(bf16[64,2560]{1,0:T(8,128)(2,1)S(1)} %get-tuple-element.74), channel_id=1, source_target_pairs={{0,1},{1,0},{2,3},{3,2},{4,5},{5,4},{6,7},{7,6},{8,9},{9,8},{10,11... | collective-permute-start | bytes 983048 | tf_op jit(solution)/shard_map/ppermute | solution.py:300
  38.3 5.7 %collective-permute-start.15 = (bf16[32,1536]{1,0:T(8,128)(2,1)S(1)}, bf16[32,1536]{1,0:T(8,128)(2,1)S(1)}, u32[]{:S(2)}, u32[]{:S(2)}) collective-permute-start(bf16[32,1536]{1,0:T(8,128)(2,1)S(1)} %slice.31), channel_id=1, source_target_pairs={{0,2},{1,3},{2,0},{3,1},{4,6},{5,7},{6,4},{7,5},{8,10},{9,11},{10,... | collective-permute-start | bytes 294920 | tf_op jit(solution)/shard_map/ppermute | solution.py:300
  40.0 6.7 %collective-permute-start.17 = (bf16[32,2560]{1,0:T(8,128)(2,1)S(1)}, bf16[32,2560]{1,0:T(8,128)(2,1)S(1)}, u32[]{:S(2)}, u32[]{:S(2)}) collective-permute-start(bf16[32,2560]{1,0:T(8,128)(2,1)S(1)} %slice.30), channel_id=1, source_target_pairs={{0,2},{1,3},{2,0},{3,1},{4,6},{5,7},{6,4},{7,5},{8,10},{9,11},{10,... | collective-permute-start | bytes 491528 | tf_op jit(solution)/shard_map/ppermute | solution.py:300

commit v5 on v4

--- a/solution.py
+++ b/solution.py
@@ -36,6 +36,18 @@
     return pl.ds(pl.multiple_of(index * width, width), width)
 
 
+def by_owner(scratch, value, owner, owners):
+    scratch[...] = value
+    share = value.shape[0] // owners
+    bits = owners.bit_length() - 1
+    pieces = []
+    for position in range(owners):
+        flipped = owners - 1 - position
+        mask = sum(((flipped >> bit) & 1) << (bits - 1 - bit) for bit in range(bits))
+        pieces.append(scratch[pl.ds(pl.multiple_of((owner ^ mask) * share, share), share), :])
+    return jnp.concatenate(pieces, axis=0)
+
+
 def fetch(pairs, sems):
     copies = [pltpu.make_async_copy(src, dst, sems.at[i]) for i, (src, dst) in enumerate(pairs)]
     for copy in copies:
@@ -54,14 +66,12 @@
         pairs.append((value_hbm.at[:, features(2 * (place ^ hop), width)], first[hop].at[rows : 2 * rows]))
     copies = fetch(pairs, sems)
     down, across = iotas(rows)
-    for copy in copies[:2]:
-        copy.wait()
-    for hop in range(count):
-        head = place ^ hop
-        decay = decay_ref[pl.ds(head, 1), :]
+    copies[0].wait()
+    scales = []
+    for hop in range(count):
+        decay = decay_ref[pl.ds(place ^ hop, 1), :]
         after = jnp.sum(jnp.where(across > down, decay, 0.0), axis=1, keepdims=True)
-        keys = key_ref[:, features(head, width)].astype(F32)
-        first[hop][0:rows, :] = (keys * jnp.exp(after)).astype(BF16)
+        scales.append(jnp.exp(after))
         whole = jnp.exp(jnp.sum(decay, axis=1, keepdims=True))
         whole = jnp.broadcast_to(whole, (TAIL, width))
         high = whole.astype(BF16).astype(F32)
@@ -70,13 +80,17 @@
         row = lax.broadcasted_iota(jnp.int32, (TAIL, width), 0)
         tail = jnp.where(row == 0, high, jnp.where(row == 1, middle, jnp.where(row == 2, low, 0.0)))
         first[hop][2 * rows :, :] = tail.astype(BF16)
+    copies[1].wait()
+    for hop in range(count):
+        keys = key_ref[:, features(place ^ hop, width)].astype(F32)
+        first[hop][0:rows, :] = (keys * scales[hop]).astype(BF16)
     for copy in copies[2:]:
         copy.wait()
 
 
-def second_pack_kernel(place_ref, decay_hbm, query_hbm, value_hbm, *refs):
-    decay_ref, query_ref, sems = refs[-3:]
-    second = refs[:-3]
+def second_pack_kernel(place_ref, owner_ref, decay_hbm, query_hbm, value_hbm, *refs, owners):
+    decay_ref, query_ref, ordered, sems = refs[-4:]
+    second = refs[:-4]
     count = len(second)
     rows, width = second[0].shape[0] // 2, second[0].shape[1]
     place = place_ref[0] & (count - 1)
@@ -92,7 +106,8 @@
         decay = decay_ref[pl.ds(head, 1), :]
         upto = jnp.sum(jnp.where(across <= down, decay, 0.0), axis=1, keepdims=True)
         queries = query_ref[:, features(head, width)].astype(F32)
-        second[hop][rows : 2 * rows, :] = (queries * jnp.exp(upto)).astype(BF16)
+        queries = by_owner(ordered, queries * jnp.exp(upto), owner_ref[0], owners)
+        second[hop][rows : 2 * rows, :] = queries.astype(BF16)
     for copy in copies[2:]:
         copy.wait()
 
@@ -181,9 +196,9 @@
         out_ref[...] = total[hop * rows : (hop + 1) * rows, :].astype(BF16)
 
 
-def block_kernel(*refs):
+def block_kernel(owner_ref, *refs, owners):
     _, decay_hbm, query_hbm, key_hbm, value_hbm, gate_hbm, inner_ref, swish_ref, token_ref = refs[:9]
-    decay_ref, query_ref, key_ref, value_ref, gate_ref, sems = refs[9:]
+    decay_ref, query_ref, key_ref, value_ref, gate_ref, ordered, sems = refs[9:]
     rows = query_ref.shape[0]
     heads = decay_ref.shape[0]
     key_dim, value_dim = query_ref.shape[1] // heads, value_ref.shape[1] // heads
@@ -211,32 +226,22 @@
         scores = lax.dot_general(
             query_ref[:, keys], key_ref[:, keys], (((1,), (1,)), ((), ())), preferred_element_type=F32
         )
-        inner_ref[:, here] = jnp.dot(
-            (scores * table).astype(BF16), value_ref[:, here], preferred_element_type=F32
-        )
+        inner = jnp.dot((scores * table).astype(BF16), value_ref[:, here], preferred_element_type=F32)
+        inner_ref[:, here] = by_owner(ordered.at[0], inner, owner_ref[0], owners)
         gate = gate_ref[:, here].astype(F32)
-        swish_ref[:, here] = gate / (1.0 + jnp.exp(-gate))
+        swish_ref[:, here] = by_owner(ordered.at[1], gate / (1.0 + jnp.exp(-gate)), owner_ref[0], owners)
     token_ref[...] = jnp.zeros_like(token_ref)
 
 
-def mix(place_ref, owner_ref, inner_ref, swish_ref, part_refs, mixed, hop, group, owners):
-    rows, value_dim = mixed.shape
+def mix(place_ref, inner_ref, swish_ref, part_refs, hop, group):
+    value_dim = sum(part_ref.shape[1] for part_ref in part_refs)
     here = features((place_ref[0] & (group - 1)) ^ hop, value_dim)
     part = jnp.concatenate([part_ref[...] for part_ref in part_refs], axis=1)
     retained = inner_ref[:, here] + part.astype(F32)
     mean = jnp.mean(retained, axis=1, keepdims=True)
     centered = retained - mean
     variance = jnp.mean(centered * centered, axis=1, keepdims=True)
-    mixed[...] = centered * lax.rsqrt(variance + 1e-05) * swish_ref[:, here]
-    share = rows // owners
-    bits = owners.bit_length() - 1
-    pieces = []
-    for position in range(owners):
-        flipped = owners - 1 - position
-        mask = sum(((flipped >> bit) & 1) << (bits - 1 - bit) for bit in range(bits))
-        start = pl.multiple_of((owner_ref[0] ^ mask) * share, share)
-        pieces.append(mixed[pl.ds(start, share), :])
-    return jnp.concatenate(pieces, axis=0).astype(BF16)
+    return centered * lax.rsqrt(variance + 1e-05) * swish_ref[:, here]
 
 
 def head_product(place_ref, rows, weight_ref, hop, group, start, tile):
@@ -248,11 +253,12 @@
     )
 
 
-def add_head_kernel(*refs, hop, group, owners):
-    place_ref, owner_ref, inner_ref, swish_ref, weight_ref = refs[:5]
-    before, part_refs = refs[5 : 5 + (hop > 0)], refs[5 + (hop > 0) : -2]
+def add_head_kernel(*refs, hop, group, summed):
+    place_ref, inner_ref, swish_ref, weight_ref = refs[:4]
+    before, part_refs = refs[4 : 4 + summed], refs[4 + summed : -2]
     total_ref, mixed = refs[-2:]
-    rows = mix(place_ref, owner_ref, inner_ref, swish_ref, part_refs, mixed, hop, group, owners)
+    mixed[...] = mix(place_ref, inner_ref, swish_ref, part_refs, hop, group)
+    rows = mixed[...].astype(BF16)
     width = total_ref.shape[1]
     tile = min(512, width)
     for start in range(0, width, tile):
@@ -277,16 +283,15 @@
         keep_ref[:, here] = out[half:].astype(BF16)
 
 
-def first_part_kernel(*refs, late, group, owners):
-    place_ref, owner_ref, inner_ref, swish_ref, weight_ref = refs[:5]
+def first_part_kernel(*refs, late, group, summed):
+    place_ref, inner_ref, swish_ref, weight_ref = refs[:4]
     count = len(late)
-    totals, part_refs = refs[5 : 5 + (late[0] > 0)], refs[5 + (late[0] > 0) : -3 - count]
-    send_ref, keep_ref, mixed = refs[-3 - count], refs[-2 - count], refs[-1]
-    rows = refs[-1 - count : -1]
+    totals, part_refs = refs[4 : 4 + summed], refs[4 + summed : -2 - count]
+    send_ref, keep_ref = refs[-2 - count], refs[-1 - count]
+    rows = refs[-count:]
     each = len(part_refs) // count
     for at, (hop, rows_ref) in enumerate(zip(late, rows)):
-        mine = part_refs[at * each : (at + 1) * each]
-        rows_ref[...] = mix(place_ref, owner_ref, inner_ref, swish_ref, mine, mixed, hop, group, owners)
+        rows_ref[...] = mix(place_ref, inner_ref, swish_ref, part_refs[at * each : (at + 1) * each], hop, group).astype(BF16)
     finish_part(place_ref, rows, weight_ref, totals, send_ref, keep_ref, 0, late, group)
 
 
@@ -368,18 +373,19 @@
         name="first_pack",
     )(place, owner, *in_hbm(decay, key, value))
     second = pl.pallas_call(
-        second_pack_kernel,
+        functools.partial(second_pack_kernel, owners=head),
         out_shape=[shape((2 * rows, key_dim), BF16)] * group,
-        in_specs=[SMEM] + [HBM] * 3,
+        in_specs=[SMEM] * 2 + [HBM] * 3,
         out_specs=[VMEM] * group,
         scratch_shapes=[
             pltpu.VMEM(decay.shape, F32),
             pltpu.VMEM(query.shape, BF16),
+            pltpu.VMEM((rows, key_dim), F32),
             pltpu.SemaphoreType.DMA((2 + group,)),
         ],
         compiler_params=params(8),
         name="second_pack",
-    )(place, *in_hbm(after(first[0]), query, value))
+    )(place, owner, *in_hbm(after(first[0]), query, value))
     first = [first[0]] + swaps(first, "ctx", ctx)
     second = [second[0]] + swaps(second, "ctx", ctx)
     left_state, whole = pl.pallas_call(
@@ -394,9 +400,9 @@
     left_carried = carried_into(left_state, whole, "ctx", ctx, group)
 
     inner, swish, token = pl.pallas_call(
-        block_kernel,
+        functools.partial(block_kernel, owners=head),
         out_shape=[shape(value.shape, F32)] * 2 + [shape((8, 128), F32)],
-        in_specs=[VMEM] + [HBM] * 5,
+        in_specs=[SMEM, VMEM] + [HBM] * 5,
         out_specs=[VMEM] * 3,
         scratch_shapes=[
             pltpu.VMEM(decay.shape, F32),
@@ -404,12 +410,13 @@
             pltpu.VMEM(key.shape, BF16),
             pltpu.VMEM(value.shape, BF16),
             pltpu.VMEM(gate.shape, BF16),
+            pltpu.VMEM((2, rows, value_dim), F32),
             pltpu.SemaphoreType.DMA((5,)),
         ],
         compiler_params=params(8),
         cost_estimate=cost(10**9, 4 * 2**20),
         name="block_part",
-    )(whole, *in_hbm(decay, query, key, value, gate))
+    )(owner, whole, *in_hbm(decay, query, key, value, gate))
 
     right_state = pl.pallas_call(
         functools.partial(second_state_kernel, rows=rows),
@@ -452,20 +459,21 @@
     right_parts = cross(right_carried, right_part, "right_cross")
     inner, left_parts = lax.optimization_barrier((inner, left_parts))
     parts = list(zip(left_parts, right_parts))
-    late = list(range(group))[-1:]
+    hops = [0, *range(2, group), *range(1, min(2, group))]
+    late = hops[-1:]
     total = []
-    for hop in range(late[0]):
+    for hop in hops[:-1]:
         total = [
             pl.pallas_call(
-                functools.partial(add_head_kernel, hop=hop, group=group, owners=head),
+                functools.partial(add_head_kernel, hop=hop, group=group, summed=len(total)),
                 out_shape=shape((rows, width), F32),
-                in_specs=[SMEM] * 2 + [VMEM] * (3 + len(total) + len(parts[hop])),
+                in_specs=[SMEM] + [VMEM] * (3 + len(total) + len(parts[hop])),
                 out_specs=VMEM,
-                input_output_aliases={5: 0} if total else {},
+
                 scratch_shapes=[pltpu.VMEM((rows, value_dim), F32)],
                 compiler_params=params(4),
                 name="add_head",
-            )(place, owner, inner, swish, weight, *total, *parts[hop])
+            )(place, inner, swish, weight, *total, *parts[hop])
         ]
     late_parts = [piece for hop in late for piece in parts[hop]]
     outs = []
@@ -474,14 +482,13 @@
         halves = [shape((rows // 2, columns), BF16)] * 2
         if part == 0:
             send, keep, *last_rows = pl.pallas_call(
-                functools.partial(first_part_kernel, late=late, group=group, owners=head),
+                functools.partial(first_part_kernel, late=late, group=group, summed=len(total)),
                 out_shape=halves + [shape((rows, value_dim), BF16)] * len(late),
-                in_specs=[SMEM] * 2 + [VMEM] * (3 + len(total) + len(late_parts)),
+                in_specs=[SMEM] + [VMEM] * (3 + len(total) + len(late_parts)),
                 out_specs=[VMEM] * (2 + len(late)),
-                scratch_shapes=[pltpu.VMEM((rows, value_dim), F32)],
                 compiler_params=params(4),
                 name="first_part",
-            )(place, owner, inner, swish, weight, *total, *late_parts)
+            )(place, inner, swish, weight, *total, *late_parts)
         else:
             send, keep = pl.pallas_call(
                 functools.partial(other_part_kernel, offset=offset, late=late, group=group),

time: 47.6 us -> 47.3 us (level)
  transfers between devices with their start and end apart: 18 -> 18, of which waited for: 8 -> 9; matrix products, arithmetic and copies ran while one was open for 0% -> 0% of each run, Pallas kernels for 19% -> 19%
where the time goes in v5:
time: 47.3 us; the launch traced here: 47.1 us
  starting transfers between devices  24.9 us (53%)
  waiting for transfers between devices  10.6 us (22%)
  Pallas kernels  10.5 us (22%)
  other arithmetic  0.88 us (2%)
    ppermute x16, starting transfers between devices, swap(): return lax.ppermute(value, axis, [(i, i ^ mask) for i in range(size)])  19.8 us
    ppermute x16, waiting for transfers between devices, swap(): return lax.ppermute(value, axis, [(i, i ^ mask) for i in range(size)])  10 us
    ppermute x2, starting transfers between devices, shift(): lax.ppermute(value, axis, [(i, (i + by * group) % size) for i in range(si...  5.07 us
    pallas_call x3, Pallas kernels, local(): pl.pallas_call(functools.partial(add_head_kernel, hop=hop, group=group, s...  2.57 us
    pallas_call x1, Pallas kernels, local(): pl.pallas_call(functools.partial(block_kernel, owners=head), out_shape=[s...  2.4 us
    pallas_call x1, Pallas kernels, local(): pl.pallas_call(functools.partial(second_pack_kernel, owners=head), out_sh...  1.2 us
    pallas_call x1, Pallas kernels, local(): pl.pallas_call(first_pack_kernel, out_shape=[shape((2 * rows + TAIL, key_...  1.17 us
  transfers between devices with their start and end apart: 18, of which 9 were waited for; matrix products, arithmetic and copies ran while one was open for 0% of the time, Pallas kernels for 19%

profile of v5, /device:TPU:0, one launch (start us, length us, event | category | flops | bytes accessed | tf_op | source)
XLA Modules:
  0.0 47.1 jit_solution(2724888799424025230)
XLA Ops:
  0.0 1.2 %first_pack.1 = (bf16[272,256]{1,0:T(8,128)(2,1)S(1)}, bf16[272,256]{1,0:T(8,128)(2,1)S(1)}, bf16[272,256]{1,0:T(8,128)(2,1)S(1)}, bf16[272,256]{1,0:T(8,128)(2,1)S(1)}) custom-call(s32[1]{0:T(128)} %bitcast.place_ref.refs_0_, s32[1]{0:T(128)} %bitcast.1.owner_ref, f32[4,128]{1,0:T(4,128)} %decay_hbm.2, bf16[128,1024]{1,0:T(8,128)(2,1)} %refs_3_.5, ...), custom_call_target="tpu_custom_call" | custom-call | flops 5000000000 | bytes 16777216 | tf_op jit(solution)/shard_map/first_pack/pallas_call | solution.py:361
  1.2 3.0 %collective-permute-start = (bf16[272,256]{1,0:T(8,128)(2,1)S(1)}, bf16[272,256]{1,0:T(8,128)(2,1)S(1)}, u32[]{:S(2)}, u32[]{:S(2)}) collective-permute-start(bf16[272,256]{1,0:T(8,128)(2,1)S(1)} %get-tuple-element.41), channel_id=1, source_target_pairs={{0,4},{4,0},{8,12},{12,8},{16,20},{20,16},{24,28},{28,24},{1,5},{5... | collective-permute-start | bytes 417800 | tf_op jit(solution)/shard_map/ppermute | solution.py:305
  4.2 1.6 %collective-permute-start.1 = (bf16[272,256]{1,0:T(8,128)(2,1)S(1)}, bf16[272,256]{1,0:T(8,128)(2,1)S(1)}, u32[]{:S(2)}, u32[]{:S(2)}) collective-permute-start(bf16[272,256]{1,0:T(8,128)(2,1)S(1)} %get-tuple-element.42), channel_id=1, source_target_pairs={{0,8},{4,12},{8,0},{12,4},{16,24},{20,28},{24,16},{28,20},{1,9},{5... | collective-permute-start | bytes 417800 | tf_op jit(solution)/shard_map/ppermute | solution.py:305
  5.8 1.2 %second_pack.1 = (bf16[256,256]{1,0:T(8,128)(2,1)S(1)}, bf16[256,256]{1,0:T(8,128)(2,1)S(1)}, bf16[256,256]{1,0:T(8,128)(2,1)S(1)}, bf16[256,256]{1,0:T(8,128)(2,1)S(1)}) custom-call(s32[1]{0:T(128)} %bitcast.place_ref.refs_0_, s32[1]{0:T(128)} %bitcast.1.owner_ref, f32[4,128]{1,0:T(4,128)} %decay_hbm.2, bf16[128,1024]{1,0:T(8,128)(2,1)} %query_hbm.1, ...), custom_call_target="tpu_custom_call" | custom-call | tf_op jit(solution)/shard_map/second_pack/pallas_call | solution.py:375
  7.0 2.0 %collective-permute-start.4 = (bf16[256,256]{1,0:T(8,128)(2,1)S(1)}, bf16[256,256]{1,0:T(8,128)(2,1)S(1)}, u32[]{:S(2)}, u32[]{:S(2)}) collective-permute-start(bf16[256,256]{1,0:T(8,128)(2,1)S(1)} %get-tuple-element.49), channel_id=1, source_target_pairs={{0,4},{4,0},{8,12},{12,8},{16,20},{20,16},{24,28},{28,24},{1,5},{5... | collective-permute-start | bytes 393224 | tf_op jit(solution)/shard_map/ppermute | solution.py:305
  8.9 1.6 %collective-permute-start.5 = (bf16[256,256]{1,0:T(8,128)(2,1)S(1)}, bf16[256,256]{1,0:T(8,128)(2,1)S(1)}, u32[]{:S(2)}, u32[]{:S(2)}) collective-permute-start(bf16[256,256]{1,0:T(8,128)(2,1)S(1)} %get-tuple-element.50), channel_id=1, source_target_pairs={{0,8},{4,12},{8,0},{12,4},{16,24},{20,28},{24,16},{28,20},{1,9},{5... | collective-permute-start | bytes 393224 | tf_op jit(solution)/shard_map/ppermute | solution.py:305
  10.9 2.4 %collective-permute-done.2.refs_3_ = bf16[272,256]{1,0:T(8,128)(2,1)S(1)} collective-permute-done((bf16[272,256]{1,0:T(8,128)(2,1)S(1)}, bf16[272,256]{1,0:T(8,128)(2,1)S(1)}, u32[]{:S(2)}, u32[]{:S(2)}) %collective-permute-start.2) | collective-permute-done | bytes 139296 | tf_op jit(solution)/shard_map/ppermute | solution.py:305
  13.7 2.7 %collective-permute-start.3 = (bf16[256,256]{1,0:T(8,128)(2,1)S(1)}, bf16[256,256]{1,0:T(8,128)(2,1)S(1)}, u32[]{:S(2)}, u32[]{:S(2)}) collective-permute-start(bf16[256,256]{1,0:T(8,128)(2,1)S(1)} %get-tuple-element.46), channel_id=1, source_target_pairs={{0,16},{4,20},{8,24},{12,28},{16,0},{20,4},{24,8},{28,12},{1,17},{... | collective-permute-start | bytes 393224 | tf_op jit(solution)/shard_map/ppermute | solution.py:314
  16.3 2.4 %block_part.1 = (f32[128,2048]{1,0:T(8,128)S(1)}, f32[128,2048]{1,0:T(8,128)S(1)}, f32[8,128]{1,0:T(8,128)S(1)}) custom-call(s32[1]{0:T(128)} %bitcast.1.owner_ref, f32[8,256]{1,0:T(8,128)S(1)} %get-tuple-element.44.refs_0_, f32[4,128]{1,0:T(4,128)} %decay_hbm.2, bf16[128,1024]{1,0:T(8,128)(2,1)} %query_hbm.1, bf16[128,1024]{1,0:T(8,128)(2,1)} %refs_3_.5, ...), custom_call_target="tpu_custom_call" | custom-call | flops 1000000000 | bytes 4194304 | tf_op jit(solution)/shard_map/block_part/pallas_call | solution.py:402
  19.5 2.4 %collective-permute-start.10 = (bf16[256,256]{1,0:T(8,128)(2,1)S(1)}, bf16[256,256]{1,0:T(8,128)(2,1)S(1)}, u32[]{:S(2)}, u32[]{:S(2)}) collective-permute-start(bf16[256,256]{1,0:T(8,128)(2,1)S(1)} %second_state.1), channel_id=1, source_target_pairs={{0,16},{4,20},{8,24},{12,28},{16,0},{20,4},{24,8},{28,12},{1,17},{... | collective-permute-start | bytes 393224 | tf_op jit(solution)/shard_map/ppermute | solution.py:314
  21.9 0.9 %group_part.1 = (f32[512,256]{1,0:T(8,128)S(1)}, f32[512,256]{1,0:T(8,128)S(1)}, bf16[512,256]{1,0:T(8,128)(2,1)S(1)}) custom-call(s32[1]{0:T(128)} %bitcast.place_ref.refs_0_, bf16[272,256]{1,0:T(8,128)(2,1)S(1)} %get-tuple-element.40.refs_0_, bf16[272,256]{1,0:T(8,128)(2,1)S(1)} %collective-permute-done.refs_1_, ...), custom_call_target="tpu_custom_call" | custom-call | flops 1000000000 | bytes 4194304 | tf_op jit(solution)/shard_map/group_part/pallas_call | solution.py:432
  23.1 3.2 %collective-permute-start.7 = (bf16[128,256]{1,0:T(8,128)(2,1)S(1)}, bf16[128,256]{1,0:T(8,128)(2,1)S(1)}, u32[]{:S(2)}, u32[]{:S(2)}) collective-permute-start(bf16[128,256]{1,0:T(8,128)(2,1)S(1)} %get-tuple-element.55), channel_id=1, source_target_pairs={{0,4},{4,0},{8,12},{12,8},{16,20},{20,16},{24,28},{28,24},{1,5},{5... | collective-permute-start | bytes 196616 | tf_op jit(solution)/shard_map/ppermute | solution.py:305
  26.3 0.7 %collective-permute-start.8 = (bf16[128,256]{1,0:T(8,128)(2,1)S(1)}, bf16[128,256]{1,0:T(8,128)(2,1)S(1)}, u32[]{:S(2)}, u32[]{:S(2)}) collective-permute-start(bf16[128,256]{1,0:T(8,128)(2,1)S(1)} %get-tuple-element.56), channel_id=1, source_target_pairs={{0,8},{4,12},{8,0},{12,4},{16,24},{20,28},{24,16},{28,20},{1,9},{5... | collective-permute-start | bytes 196616 | tf_op jit(solution)/shard_map/ppermute | solution.py:305
  27.0 0.9 %collective-permute-start.9 = (bf16[128,256]{1,0:T(8,128)(2,1)S(1)}, bf16[128,256]{1,0:T(8,128)(2,1)S(1)}, u32[]{:S(2)}, u32[]{:S(2)}) collective-permute-start(bf16[128,256]{1,0:T(8,128)(2,1)S(1)} %get-tuple-element.57), channel_id=1, source_target_pairs={{0,12},{4,8},{8,4},{12,0},{16,28},{20,24},{24,20},{28,16},{1,13},{... | collective-permute-start | bytes 196616 | tf_op jit(solution)/shard_map/ppermute | solution.py:305
  28.9 2.7 %collective-permute-start.12 = (bf16[128,256]{1,0:T(8,128)(2,1)S(1)}, bf16[128,256]{1,0:T(8,128)(2,1)S(1)}, u32[]{:S(2)}, u32[]{:S(2)}) collective-permute-start(bf16[128,256]{1,0:T(8,128)(2,1)S(1)} %get-tuple-element.67), channel_id=1, source_target_pairs={{0,12},{4,8},{8,4},{12,0},{16,28},{20,24},{24,20},{28,16},{1,13},{... | collective-permute-start | bytes 196616 | tf_op jit(solution)/shard_map/ppermute | solution.py:305
  31.6 0.6 %collective-permute-start.13 = (bf16[128,256]{1,0:T(8,128)(2,1)S(1)}, bf16[128,256]{1,0:T(8,128)(2,1)S(1)}, u32[]{:S(2)}, u32[]{:S(2)}) collective-permute-start(bf16[128,256]{1,0:T(8,128)(2,1)S(1)} %get-tuple-element.69), channel_id=1, source_target_pairs={{0,4},{4,0},{8,12},{12,8},{16,20},{20,16},{24,28},{28,24},{1,5},{5... | collective-permute-start | bytes 196616 | tf_op jit(solution)/shard_map/ppermute | solution.py:305
  32.3 0.9 %add_head.3.refs_4_ = f32[128,4096]{1,0:T(8,128)S(1)} custom-call(s32[1]{0:T(128)} %bitcast.place_ref.refs_0_, f32[128,2048]{1,0:T(8,128)S(1)} %get-tuple-element.58.refs_1_, f32[128,2048]{1,0:T(8,128)S(1)} %get-tuple-element.59.refs_2_, bf16[2048,4096]{1,0:T(8,128)(2,1)S(1)} %bitcast.3, bf16[128,256]{1,0:T(8,128)(2,1)S(1)} %get-tuple-element.60.refs_4_, ...), custom_call_target="tpu_custom_call" | custom-call | tf_op jit(solution)/shard_map/add_head/pallas_call | solution.py:467
  33.4 0.9 %add_head.4.refs_4_ = f32[128,4096]{1,0:T(8,128)S(1)} custom-call(s32[1]{0:T(128)} %bitcast.place_ref.refs_0_, f32[128,2048]{1,0:T(8,128)S(1)} %get-tuple-element.58.refs_1_, f32[128,2048]{1,0:T(8,128)S(1)} %get-tuple-element.59.refs_2_, bf16[2048,4096]{1,0:T(8,128)(2,1)S(1)} %bitcast.3, f32[128,4096]{1,0:T(8,128)S(1)} %add_head.3.refs_4_, ...), custom_call_target="tpu_custom_call" | custom-call | tf_op jit(solution)/shard_map/add_head/pallas_call | solution.py:467
  34.5 0.9 %add_head.5.refs_4_.refs_1_ = f32[128,4096]{1,0:T(8,128)S(1)} custom-call(s32[1]{0:T(128)} %bitcast.place_ref.refs_0_, f32[128,2048]{1,0:T(8,128)S(1)} %get-tuple-element.58.refs_1_, f32[128,2048]{1,0:T(8,128)S(1)} %get-tuple-element.59.refs_2_, bf16[2048,4096]{1,0:T(8,128)(2,1)S(1)} %bitcast.3, f32[128,4096]{1,0:T(8,128)S(1)} %add_head.4.refs_4_, ...), custom_call_target="tpu_custom_call" | custom-call | tf_op jit(solution)/shard_map/add_head/pallas_call | solution.py:467
  38.0 1.6 %collective-permute-start.15 = (bf16[32,1536]{1,0:T(8,128)(2,1)S(1)}, bf16[32,1536]{1,0:T(8,128)(2,1)S(1)}, u32[]{:S(2)}, u32[]{:S(2)}) collective-permute-start(bf16[32,1536]{1,0:T(8,128)(2,1)S(1)} %slice.31), channel_id=1, source_target_pairs={{0,2},{1,3},{2,0},{3,1},{4,6},{5,7},{6,4},{7,5},{8,10},{9,11},{10,... | collective-permute-start | bytes 294920 | tf_op jit(solution)/shard_map/ppermute | solution.py:305
  39.6 0.9 %collective-permute-start.17 = (bf16[32,2560]{1,0:T(8,128)(2,1)S(1)}, bf16[32,2560]{1,0:T(8,128)(2,1)S(1)}, u32[]{:S(2)}, u32[]{:S(2)}) collective-permute-start(bf16[32,2560]{1,0:T(8,128)(2,1)S(1)} %slice.30), channel_id=1, source_target_pairs={{0,2},{1,3},{2,0},{3,1},{4,6},{5,7},{6,4},{7,5},{8,10},{9,11},{10,... | collective-permute-start | bytes 491528 | tf_op jit(solution)/shard_map/ppermute | solution.py:305
  40.5 3.1 %collective-permute-done.15 = bf16[32,1536]{1,0:T(8,128)(2,1)S(1)} collective-permute-done((bf16[32,1536]{1,0:T(8,128)(2,1)S(1)}, bf16[32,1536]{1,0:T(8,128)(2,1)S(1)}, u32[]{:S(2)}, u32[]{:S(2)}) %collective-permute-start.15) | collective-permute-done | bytes 98336 | tf_op jit(solution)/shard_map/ppermute | solution.py:305
  43.6 2.8 %collective-permute-done.17 = bf16[32,2560]{1,0:T(8,128)(2,1)S(1)} collective-permute-done((bf16[32,2560]{1,0:T(8,128)(2,1)S(1)}, bf16[32,2560]{1,0:T(8,128)(2,1)S(1)}, u32[]{:S(2)}, u32[]{:S(2)}) %collective-permute-start.17) | collective-permute-done | bytes 163872 | tf_op jit(solution)/shard_map/ppermute | solution.py:305
  46.4 0.7 %pad_maximum_fusion = bf16[32,4096]{1,0:T(8,128)(2,1)} fusion(bf16[32,2560]{1,0:T(8,128)(2,1)S(1)} %fusion, bf16[32,1536]{1,0:T(8,128)(2,1)S(1)} %fusion.1), kind=kLoop, calls=%fused_computation.5 | loop fusion | flops 524288 | bytes 524288 | tf_op jit(solution)/shard_map/concatenate | solution.py:503
  (41 shorter events, 6.0 us)
Async XLA Ops:
  1.2 9.3 %collective-permute-start = (bf16[272,256]{1,0:T(8,128)(2,1)S(1)}, bf16[272,256]{1,0:T(8,128)(2,1)S(1)}, u32[]{:S(2)}, u32[]{:S(2)}) collective-permute-start(bf16[272,256]{1,0:T(8,128)(2,1)S(1)} %get-tuple-element.41), channel_id=1, source_target_pairs={{0,4},{4,0},{8,12},{12,8},{16,20},{20,16},{24,28},{28,24},{1,5},{5... | collective-permute-start | bytes 417800 | tf_op jit(solution)/shard_map/ppermute | solution.py:305
  4.2 6.7 %collective-permute-start.1 = (bf16[272,256]{1,0:T(8,128)(2,1)S(1)}, bf16[272,256]{1,0:T(8,128)(2,1)S(1)}, u32[]{:S(2)}, u32[]{:S(2)}) collective-permute-start(bf16[272,256]{1,0:T(8,128)(2,1)S(1)} %get-tuple-element.42), channel_id=1, source_target_pairs={{0,8},{4,12},{8,0},{12,4},{16,24},{20,28},{24,16},{28,20},{1,9},{5... | collective-permute-start | bytes 417800 | tf_op jit(solution)/shard_map/ppermute | solution.py:305
  5.8 7.6 %collective-permute-start.2 = (bf16[272,256]{1,0:T(8,128)(2,1)S(1)}, bf16[272,256]{1,0:T(8,128)(2,1)S(1)}, u32[]{:S(2)}, u32[]{:S(2)}) collective-permute-start(bf16[272,256]{1,0:T(8,128)(2,1)S(1)} %get-tuple-element.43), channel_id=1, source_target_pairs={{0,12},{4,8},{8,4},{12,0},{16,28},{20,24},{24,20},{28,16},{1,13},{... | collective-permute-start | bytes 417800 | tf_op jit(solution)/shard_map/ppermute | solution.py:305
  7.0 11.8 %collective-permute-start.4 = (bf16[256,256]{1,0:T(8,128)(2,1)S(1)}, bf16[256,256]{1,0:T(8,128)(2,1)S(1)}, u32[]{:S(2)}, u32[]{:S(2)}) collective-permute-start(bf16[256,256]{1,0:T(8,128)(2,1)S(1)} %get-tuple-element.49), channel_id=1, source_target_pairs={{0,4},{4,0},{8,12},{12,8},{16,20},{20,16},{24,28},{28,24},{1,5},{5... | collective-permute-start | bytes 393224 | tf_op jit(solution)/shard_map/ppermute | solution.py:305
  8.9 9.8 %collective-permute-start.5 = (bf16[256,256]{1,0:T(8,128)(2,1)S(1)}, bf16[256,256]{1,0:T(8,128)(2,1)S(1)}, u32[]{:S(2)}, u32[]{:S(2)}) collective-permute-start(bf16[256,256]{1,0:T(8,128)(2,1)S(1)} %get-tuple-element.50), channel_id=1, source_target_pairs={{0,8},{4,12},{8,0},{12,4},{16,24},{20,28},{24,16},{28,20},{1,9},{5... | collective-permute-start | bytes 393224 | tf_op jit(solution)/shard_map/ppermute | solution.py:305
  10.5 8.6 %collective-permute-start.6 = (bf16[256,256]{1,0:T(8,128)(2,1)S(1)}, bf16[256,256]{1,0:T(8,128)(2,1)S(1)}, u32[]{:S(2)}, u32[]{:S(2)}) collective-permute-start(bf16[256,256]{1,0:T(8,128)(2,1)S(1)} %get-tuple-element.51), channel_id=1, source_target_pairs={{0,12},{4,8},{8,4},{12,0},{16,28},{20,24},{24,20},{28,16},{1,13},{... | collective-permute-start | bytes 393224 | tf_op jit(solution)/shard_map/ppermute | solution.py:305
  13.3 18.9 %slice-start = ((s8[16777216]{0:T(1024)(128)(4,1)}), s8[4194304]{0:T(1024)(128)(4,1)S(1)}, s32[]{:S(2)}) async-start(s8[16777216]{0:T(1024)(128)(4,1)} %bitcast.2), calls=%async_computation | async-start | bytes 8388608
  13.3 18.9 %slice-start.1 = ((s8[16777216]{0:T(1024)(128)(4,1)}), s8[4194304]{0:T(1024)(128)(4,1)S(1)}, s32[]{:S(2)}) async-start(s8[16777216]{0:T(1024)(128)(4,1)} %bitcast.2), calls=%async_computation.1 | async-start | bytes 8388608
  13.7 9.2 %collective-permute-start.3 = (bf16[256,256]{1,0:T(8,128)(2,1)S(1)}, bf16[256,256]{1,0:T(8,128)(2,1)S(1)}, u32[]{:S(2)}, u32[]{:S(2)}) collective-permute-start(bf16[256,256]{1,0:T(8,128)(2,1)S(1)} %get-tuple-element.46), channel_id=1, source_target_pairs={{0,16},{4,20},{8,24},{12,28},{16,0},{20,4},{24,8},{28,12},{1,17},{... | collective-permute-start | bytes 393224 | tf_op jit(solution)/shard_map/ppermute | solution.py:314
  19.2 13.1 %slice-start.2 = ((s8[16777216]{0:T(1024)(128)(4,1)}), s8[4194304]{0:T(1024)(128)(4,1)S(1)}, s32[]{:S(2)}) async-start(s8[16777216]{0:T(1024)(128)(4,1)} %bitcast.2), calls=%async_computation.2 | async-start | bytes 8388608
  19.2 13.1 %slice-start.3 = ((s8[16777216]{0:T(1024)(128)(4,1)}), s8[4194304]{0:T(1024)(128)(4,1)S(1)}, s32[]{:S(2)}) async-start(s8[16777216]{0:T(1024)(128)(4,1)} %bitcast.2), calls=%async_computation.3 | async-start | bytes 8388608
  19.5 8.9 %collective-permute-start.10 = (bf16[256,256]{1,0:T(8,128)(2,1)S(1)}, bf16[256,256]{1,0:T(8,128)(2,1)S(1)}, u32[]{:S(2)}, u32[]{:S(2)}) collective-permute-start(bf16[256,256]{1,0:T(8,128)(2,1)S(1)} %second_state.1), channel_id=1, source_target_pairs={{0,16},{4,20},{8,24},{12,28},{16,0},{20,4},{24,8},{28,12},{1,17},{... | collective-permute-start | bytes 393224 | tf_op jit(solution)/shard_map/ppermute | solution.py:314
  23.1 8.4 %collective-permute-start.7 = (bf16[128,256]{1,0:T(8,128)(2,1)S(1)}, bf16[128,256]{1,0:T(8,128)(2,1)S(1)}, u32[]{:S(2)}, u32[]{:S(2)}) collective-permute-start(bf16[128,256]{1,0:T(8,128)(2,1)S(1)} %get-tuple-element.55), channel_id=1, source_target_pairs={{0,4},{4,0},{8,12},{12,8},{16,20},{20,16},{24,28},{28,24},{1,5},{5... | collective-permute-start | bytes 196616 | tf_op jit(solution)/shard_map/ppermute | solution.py:305
  26.3 5.9 %collective-permute-start.8 = (bf16[128,256]{1,0:T(8,128)(2,1)S(1)}, bf16[128,256]{1,0:T(8,128)(2,1)S(1)}, u32[]{:S(2)}, u32[]{:S(2)}) collective-permute-start(bf16[128,256]{1,0:T(8,128)(2,1)S(1)} %get-tuple-element.56), channel_id=1, source_target_pairs={{0,8},{4,12},{8,0},{12,4},{16,24},{20,28},{24,16},{28,20},{1,9},{5... | collective-permute-start | bytes 196616 | tf_op jit(solution)/shard_map/ppermute | solution.py:305
  27.0 5.2 %collective-permute-start.9 = (bf16[128,256]{1,0:T(8,128)(2,1)S(1)}, bf16[128,256]{1,0:T(8,128)(2,1)S(1)}, u32[]{:S(2)}, u32[]{:S(2)}) collective-permute-start(bf16[128,256]{1,0:T(8,128)(2,1)S(1)} %get-tuple-element.57), channel_id=1, source_target_pairs={{0,12},{4,8},{8,4},{12,0},{16,28},{20,24},{24,20},{28,16},{1,13},{... | collective-permute-start | bytes 196616 | tf_op jit(solution)/shard_map/ppermute | solution.py:305
  28.6 4.7 %collective-permute-start.11 = (bf16[128,256]{1,0:T(8,128)(2,1)S(1)}, bf16[128,256]{1,0:T(8,128)(2,1)S(1)}, u32[]{:S(2)}, u32[]{:S(2)}) collective-permute-start(bf16[128,256]{1,0:T(8,128)(2,1)S(1)} %get-tuple-element.65), channel_id=1, source_target_pairs={{0,8},{4,12},{8,0},{12,4},{16,24},{20,28},{24,16},{28,20},{1,9},{5... | collective-permute-start | bytes 196616 | tf_op jit(solution)/shard_map/ppermute | solution.py:305
  28.9 5.6 %collective-permute-start.12 = (bf16[128,256]{1,0:T(8,128)(2,1)S(1)}, bf16[128,256]{1,0:T(8,128)(2,1)S(1)}, u32[]{:S(2)}, u32[]{:S(2)}) collective-permute-start(bf16[128,256]{1,0:T(8,128)(2,1)S(1)} %get-tuple-element.67), channel_id=1, source_target_pairs={{0,12},{4,8},{8,4},{12,0},{16,28},{20,24},{24,20},{28,16},{1,13},{... | collective-permute-start | bytes 196616 | tf_op jit(solution)/shard_map/ppermute | solution.py:305
  31.6 4.3 %collective-permute-start.13 = (bf16[128,256]{1,0:T(8,128)(2,1)S(1)}, bf16[128,256]{1,0:T(8,128)(2,1)S(1)}, u32[]{:S(2)}, u32[]{:S(2)}) collective-permute-start(bf16[128,256]{1,0:T(8,128)(2,1)S(1)} %get-tuple-element.69), channel_id=1, source_target_pairs={{0,4},{4,0},{8,12},{12,8},{16,20},{20,16},{24,28},{28,24},{1,5},{5... | collective-permute-start | bytes 196616 | tf_op jit(solution)/shard_map/ppermute | solution.py:305
  36.4 1.5 %collective-permute-start.14 = (bf16[64,1536]{1,0:T(8,128)(2,1)S(1)}, bf16[64,1536]{1,0:T(8,128)(2,1)S(1)}, u32[]{:S(2)}, u32[]{:S(2)}) collective-permute-start(bf16[64,1536]{1,0:T(8,128)(2,1)S(1)} %get-tuple-element.71), channel_id=1, source_target_pairs={{0,1},{1,0},{2,3},{3,2},{4,5},{5,4},{6,7},{7,6},{8,9},{9,8},{10,11... | collective-permute-start | bytes 589832 | tf_op jit(solution)/shard_map/ppermute | solution.py:305
  37.0 2.5 %collective-permute-start.16 = (bf16[64,2560]{1,0:T(8,128)(2,1)S(1)}, bf16[64,2560]{1,0:T(8,128)(2,1)S(1)}, u32[]{:S(2)}, u32[]{:S(2)}) collective-permute-start(bf16[64,2560]{1,0:T(8,128)(2,1)S(1)} %get-tuple-element.74), channel_id=1, source_target_pairs={{0,1},{1,0},{2,3},{3,2},{4,5},{5,4},{6,7},{7,6},{8,9},{9,8},{10,11... | collective-permute-start | bytes 983048 | tf_op jit(solution)/shard_map/ppermute | solution.py:305
  38.0 5.6 %collective-permute-start.15 = (bf16[32,1536]{1,0:T(8,128)(2,1)S(1)}, bf16[32,1536]{1,0:T(8,128)(2,1)S(1)}, u32[]{:S(2)}, u32[]{:S(2)}) collective-permute-start(bf16[32,1536]{1,0:T(8,128)(2,1)S(1)} %slice.31), channel_id=1, source_target_pairs={{0,2},{1,3},{2,0},{3,1},{4,6},{5,7},{6,4},{7,5},{8,10},{9,11},{10,... | collective-permute-start | bytes 294920 | tf_op jit(solution)/shard_map/ppermute | solution.py:305
  39.6 6.7 %collective-permute-start.17 = (bf16[32,2560]{1,0:T(8,128)(2,1)S(1)}, bf16[32,2560]{1,0:T(8,128)(2,1)S(1)}, u32[]{:S(2)}, u32[]{:S(2)}) collective-permute-start(bf16[32,2560]{1,0:T(8,128)(2,1)S(1)} %slice.30), channel_id=1, source_target_pairs={{0,2},{1,3},{2,0},{3,1},{4,6},{5,7},{6,4},{7,5},{8,10},{9,11},{10,... | collective-permute-start | bytes 491528 | tf_op jit(solution)/shard_map/ppermute | solution.py:305

commit v6 on v5

--- a/solution.py
+++ b/solution.py
@@ -55,15 +55,18 @@
     return copies
 
 
+def centered(value_ref, head, value_dim):
+    values = value_ref[:, features(head, value_dim)].astype(F32)
+    return values - jnp.mean(values, axis=1, keepdims=True)
+
+
 def first_pack_kernel(place_ref, owner_ref, decay_hbm, key_hbm, value_hbm, *refs):
-    decay_ref, key_ref, sems = refs[-3:]
-    first = refs[:-3]
+    decay_ref, key_ref, value_ref, sems = refs[-4:]
+    first = refs[:-4]
     count = len(first)
     rows, width = (first[0].shape[0] - TAIL) // 2, first[0].shape[1]
     place = place_ref[0] & (count - 1)
-    pairs = [(decay_hbm, decay_ref), (key_hbm, key_ref)]
-    for hop in range(count):
-        pairs.append((value_hbm.at[:, features(2 * (place ^ hop), width)], first[hop].at[rows : 2 * rows]))
+    pairs = [(decay_hbm, decay_ref), (key_hbm, key_ref), (value_hbm, value_ref)]
     copies = fetch(pairs, sems)
     down, across = iotas(rows)
     copies[0].wait()
@@ -84,19 +87,19 @@
     for hop in range(count):
         keys = key_ref[:, features(place ^ hop, width)].astype(F32)
         first[hop][0:rows, :] = (keys * scales[hop]).astype(BF16)
-    for copy in copies[2:]:
-        copy.wait()
+    copies[2].wait()
+    for hop in range(count):
+        values = centered(value_ref, place ^ hop, 2 * width)
+        first[hop][rows : 2 * rows, :] = values[:, :width].astype(BF16)
 
 
 def second_pack_kernel(place_ref, owner_ref, decay_hbm, query_hbm, value_hbm, *refs, owners):
-    decay_ref, query_ref, ordered, sems = refs[-4:]
-    second = refs[:-4]
+    decay_ref, query_ref, value_ref, ordered, sems = refs[-5:]
+    second = refs[:-5]
     count = len(second)
     rows, width = second[0].shape[0] // 2, second[0].shape[1]
     place = place_ref[0] & (count - 1)
-    pairs = [(decay_hbm, decay_ref), (query_hbm, query_ref)]
-    for hop in range(count):
-        pairs.append((value_hbm.at[:, features(2 * (place ^ hop) + 1, width)], second[hop].at[0:rows]))
+    pairs = [(decay_hbm, decay_ref), (query_hbm, query_ref), (value_hbm, value_ref)]
     copies = fetch(pairs, sems)
     down, across = iotas(rows)
     for copy in copies[:2]:
@@ -108,8 +111,10 @@
         queries = query_ref[:, features(head, width)].astype(F32)
         queries = by_owner(ordered, queries * jnp.exp(upto), owner_ref[0], owners)
         second[hop][rows : 2 * rows, :] = queries.astype(BF16)
-    for copy in copies[2:]:
-        copy.wait()
+    copies[2].wait()
+    for hop in range(count):
+        values = centered(value_ref, place ^ hop, 2 * width)
+        second[hop][0:rows, :] = values[:, width:].astype(BF16)
 
 
 def block_decay(message_ref):
@@ -239,9 +244,9 @@
     part = jnp.concatenate([part_ref[...] for part_ref in part_refs], axis=1)
     retained = inner_ref[:, here] + part.astype(F32)
     mean = jnp.mean(retained, axis=1, keepdims=True)
-    centered = retained - mean
-    variance = jnp.mean(centered * centered, axis=1, keepdims=True)
-    return centered * lax.rsqrt(variance + 1e-05) * swish_ref[:, here]
+    centred = retained - mean
+    variance = jnp.mean(centred * centred, axis=1, keepdims=True)
+    return centred * lax.rsqrt(variance + 1e-05) * swish_ref[:, here]
 
 
 def head_product(place_ref, rows, weight_ref, hop, group, start, tile):
@@ -366,7 +371,8 @@
         scratch_shapes=[
             pltpu.VMEM(decay.shape, F32),
             pltpu.VMEM(key.shape, BF16),
-            pltpu.SemaphoreType.DMA((2 + group,)),
+            pltpu.VMEM(value.shape, BF16),
+            pltpu.SemaphoreType.DMA((3,)),
         ],
         compiler_params=params(8),
         cost_estimate=cost(5 * 10**9, 2**24),
@@ -380,8 +386,9 @@
         scratch_shapes=[
             pltpu.VMEM(decay.shape, F32),
             pltpu.VMEM(query.shape, BF16),
+            pltpu.VMEM(value.shape, BF16),
             pltpu.VMEM((rows, key_dim), F32),
-            pltpu.SemaphoreType.DMA((2 + group,)),
+            pltpu.SemaphoreType.DMA((3,)),
         ],
         compiler_params=params(8),
         name="second_pack",

time: 47.3 us -> 47.5 us (level)
  no operation moved by 1% of the time
where the time goes in v6:
time: 47.5 us; the launch traced here: 47.3 us
  starting transfers between devices  24.8 us (52%)
  Pallas kernels  10.8 us (23%)
  waiting for transfers between devices  10.6 us (22%)
  other arithmetic  0.88 us (2%)
    ppermute x16, starting transfers between devices, swap(): return lax.ppermute(value, axis, [(i, i ^ mask) for i in range(size)])  19.7 us
    ppermute x16, waiting for transfers between devices, swap(): return lax.ppermute(value, axis, [(i, i ^ mask) for i in range(size)])  10.1 us
    ppermute x2, starting transfers between devices, shift(): lax.ppermute(value, axis, [(i, (i + by * group) % size) for i in range(si...  5.07 us
    pallas_call x3, Pallas kernels, local(): pl.pallas_call(functools.partial(add_head_kernel, hop=hop, group=group, s...  2.57 us
    pallas_call x1, Pallas kernels, local(): pl.pallas_call(functools.partial(block_kernel, owners=head), out_shape=[s...  2.4 us
    pallas_call x1, Pallas kernels, local(): pl.pallas_call(first_pack_kernel, out_shape=[shape((2 * rows + TAIL, key_...  1.37 us
    pallas_call x1, Pallas kernels, local(): pl.pallas_call(functools.partial(second_pack_kernel, owners=head), out_sh...  1.32 us
  transfers between devices with their start and end apart: 18, of which 9 were waited for; matrix products, arithmetic and copies ran while one was open for 0% of the time, Pallas kernels for 19%

profile of v6, /device:TPU:0, one launch (start us, length us, event | category | flops | bytes accessed | tf_op | source)
XLA Modules:
  0.0 47.3 jit_solution(16543426848532689236)
XLA Ops:
  0.0 1.4 %first_pack.1 = (bf16[272,256]{1,0:T(8,128)(2,1)S(1)}, bf16[272,256]{1,0:T(8,128)(2,1)S(1)}, bf16[272,256]{1,0:T(8,128)(2,1)S(1)}, bf16[272,256]{1,0:T(8,128)(2,1)S(1)}) custom-call(s32[1]{0:T(128)} %bitcast.place_ref.refs_0_, s32[1]{0:T(128)} %bitcast.1.owner_ref, f32[4,128]{1,0:T(4,128)} %decay_hbm.2, bf16[128,1024]{1,0:T(8,128)(2,1)} %refs_3_.5, ...), custom_call_target="tpu_custom_call" | custom-call | flops 5000000000 | bytes 16777216 | tf_op jit(solution)/shard_map/first_pack/pallas_call | solution.py:366
  1.4 3.0 %collective-permute-start = (bf16[272,256]{1,0:T(8,128)(2,1)S(1)}, bf16[272,256]{1,0:T(8,128)(2,1)S(1)}, u32[]{:S(2)}, u32[]{:S(2)}) collective-permute-start(bf16[272,256]{1,0:T(8,128)(2,1)S(1)} %get-tuple-element.41), channel_id=1, source_target_pairs={{0,4},{4,0},{8,12},{12,8},{16,20},{20,16},{24,28},{28,24},{1,5},{5... | collective-permute-start | bytes 417800 | tf_op jit(solution)/shard_map/ppermute | solution.py:310
  4.4 1.6 %collective-permute-start.1 = (bf16[272,256]{1,0:T(8,128)(2,1)S(1)}, bf16[272,256]{1,0:T(8,128)(2,1)S(1)}, u32[]{:S(2)}, u32[]{:S(2)}) collective-permute-start(bf16[272,256]{1,0:T(8,128)(2,1)S(1)} %get-tuple-element.42), channel_id=1, source_target_pairs={{0,8},{4,12},{8,0},{12,4},{16,24},{20,28},{24,16},{28,20},{1,9},{5... | collective-permute-start | bytes 417800 | tf_op jit(solution)/shard_map/ppermute | solution.py:310
  6.0 1.3 %second_pack.1 = (bf16[256,256]{1,0:T(8,128)(2,1)S(1)}, bf16[256,256]{1,0:T(8,128)(2,1)S(1)}, bf16[256,256]{1,0:T(8,128)(2,1)S(1)}, bf16[256,256]{1,0:T(8,128)(2,1)S(1)}) custom-call(s32[1]{0:T(128)} %bitcast.place_ref.refs_0_, s32[1]{0:T(128)} %bitcast.1.owner_ref, f32[4,128]{1,0:T(4,128)} %decay_hbm.2, bf16[128,1024]{1,0:T(8,128)(2,1)} %query_hbm.1, ...), custom_call_target="tpu_custom_call" | custom-call | tf_op jit(solution)/shard_map/second_pack/pallas_call | solution.py:381
  7.3 2.0 %collective-permute-start.4 = (bf16[256,256]{1,0:T(8,128)(2,1)S(1)}, bf16[256,256]{1,0:T(8,128)(2,1)S(1)}, u32[]{:S(2)}, u32[]{:S(2)}) collective-permute-start(bf16[256,256]{1,0:T(8,128)(2,1)S(1)} %get-tuple-element.49), channel_id=1, source_target_pairs={{0,4},{4,0},{8,12},{12,8},{16,20},{20,16},{24,28},{28,24},{1,5},{5... | collective-permute-start | bytes 393224 | tf_op jit(solution)/shard_map/ppermute | solution.py:310
  9.3 1.6 %collective-permute-start.5 = (bf16[256,256]{1,0:T(8,128)(2,1)S(1)}, bf16[256,256]{1,0:T(8,128)(2,1)S(1)}, u32[]{:S(2)}, u32[]{:S(2)}) collective-permute-start(bf16[256,256]{1,0:T(8,128)(2,1)S(1)} %get-tuple-element.50), channel_id=1, source_target_pairs={{0,8},{4,12},{8,0},{12,4},{16,24},{20,28},{24,16},{28,20},{1,9},{5... | collective-permute-start | bytes 393224 | tf_op jit(solution)/shard_map/ppermute | solution.py:310
  11.1 2.4 %collective-permute-done.2.refs_3_ = bf16[272,256]{1,0:T(8,128)(2,1)S(1)} collective-permute-done((bf16[272,256]{1,0:T(8,128)(2,1)S(1)}, bf16[272,256]{1,0:T(8,128)(2,1)S(1)}, u32[]{:S(2)}, u32[]{:S(2)}) %collective-permute-start.2) | collective-permute-done | bytes 139296 | tf_op jit(solution)/shard_map/ppermute | solution.py:310
  13.8 2.7 %collective-permute-start.3 = (bf16[256,256]{1,0:T(8,128)(2,1)S(1)}, bf16[256,256]{1,0:T(8,128)(2,1)S(1)}, u32[]{:S(2)}, u32[]{:S(2)}) collective-permute-start(bf16[256,256]{1,0:T(8,128)(2,1)S(1)} %get-tuple-element.46), channel_id=1, source_target_pairs={{0,16},{4,20},{8,24},{12,28},{16,0},{20,4},{24,8},{28,12},{1,17},{... | collective-permute-start | bytes 393224 | tf_op jit(solution)/shard_map/ppermute | solution.py:319
  16.5 2.4 %block_part.1 = (f32[128,2048]{1,0:T(8,128)S(1)}, f32[128,2048]{1,0:T(8,128)S(1)}, f32[8,128]{1,0:T(8,128)S(1)}) custom-call(s32[1]{0:T(128)} %bitcast.1.owner_ref, f32[8,256]{1,0:T(8,128)S(1)} %get-tuple-element.44.refs_0_, f32[4,128]{1,0:T(4,128)} %decay_hbm.2, bf16[128,1024]{1,0:T(8,128)(2,1)} %query_hbm.1, bf16[128,1024]{1,0:T(8,128)(2,1)} %refs_3_.5, ...), custom_call_target="tpu_custom_call" | custom-call | flops 1000000000 | bytes 4194304 | tf_op jit(solution)/shard_map/block_part/pallas_call | solution.py:409
  19.7 2.4 %collective-permute-start.10 = (bf16[256,256]{1,0:T(8,128)(2,1)S(1)}, bf16[256,256]{1,0:T(8,128)(2,1)S(1)}, u32[]{:S(2)}, u32[]{:S(2)}) collective-permute-start(bf16[256,256]{1,0:T(8,128)(2,1)S(1)} %second_state.1), channel_id=1, source_target_pairs={{0,16},{4,20},{8,24},{12,28},{16,0},{20,4},{24,8},{28,12},{1,17},{... | collective-permute-start | bytes 393224 | tf_op jit(solution)/shard_map/ppermute | solution.py:319
  22.1 0.9 %group_part.1 = (f32[512,256]{1,0:T(8,128)S(1)}, f32[512,256]{1,0:T(8,128)S(1)}, bf16[512,256]{1,0:T(8,128)(2,1)S(1)}) custom-call(s32[1]{0:T(128)} %bitcast.place_ref.refs_0_, bf16[272,256]{1,0:T(8,128)(2,1)S(1)} %get-tuple-element.40.refs_0_, bf16[272,256]{1,0:T(8,128)(2,1)S(1)} %collective-permute-done.refs_1_, ...), custom_call_target="tpu_custom_call" | custom-call | flops 1000000000 | bytes 4194304 | tf_op jit(solution)/shard_map/group_part/pallas_call | solution.py:439
  23.3 3.2 %collective-permute-start.7 = (bf16[128,256]{1,0:T(8,128)(2,1)S(1)}, bf16[128,256]{1,0:T(8,128)(2,1)S(1)}, u32[]{:S(2)}, u32[]{:S(2)}) collective-permute-start(bf16[128,256]{1,0:T(8,128)(2,1)S(1)} %get-tuple-element.55), channel_id=1, source_target_pairs={{0,4},{4,0},{8,12},{12,8},{16,20},{20,16},{24,28},{28,24},{1,5},{5... | collective-permute-start | bytes 196616 | tf_op jit(solution)/shard_map/ppermute | solution.py:310
  26.5 0.7 %collective-permute-start.8 = (bf16[128,256]{1,0:T(8,128)(2,1)S(1)}, bf16[128,256]{1,0:T(8,128)(2,1)S(1)}, u32[]{:S(2)}, u32[]{:S(2)}) collective-permute-start(bf16[128,256]{1,0:T(8,128)(2,1)S(1)} %get-tuple-element.56), channel_id=1, source_target_pairs={{0,8},{4,12},{8,0},{12,4},{16,24},{20,28},{24,16},{28,20},{1,9},{5... | collective-permute-start | bytes 196616 | tf_op jit(solution)/shard_map/ppermute | solution.py:310
  27.2 0.9 %collective-permute-start.9 = (bf16[128,256]{1,0:T(8,128)(2,1)S(1)}, bf16[128,256]{1,0:T(8,128)(2,1)S(1)}, u32[]{:S(2)}, u32[]{:S(2)}) collective-permute-start(bf16[128,256]{1,0:T(8,128)(2,1)S(1)} %get-tuple-element.57), channel_id=1, source_target_pairs={{0,12},{4,8},{8,4},{12,0},{16,28},{20,24},{24,20},{28,16},{1,13},{... | collective-permute-start | bytes 196616 | tf_op jit(solution)/shard_map/ppermute | solution.py:310
  29.1 2.7 %collective-permute-start.12 = (bf16[128,256]{1,0:T(8,128)(2,1)S(1)}, bf16[128,256]{1,0:T(8,128)(2,1)S(1)}, u32[]{:S(2)}, u32[]{:S(2)}) collective-permute-start(bf16[128,256]{1,0:T(8,128)(2,1)S(1)} %get-tuple-element.67), channel_id=1, source_target_pairs={{0,12},{4,8},{8,4},{12,0},{16,28},{20,24},{24,20},{28,16},{1,13},{... | collective-permute-start | bytes 196616 | tf_op jit(solution)/shard_map/ppermute | solution.py:310
  31.8 0.6 %collective-permute-start.13 = (bf16[128,256]{1,0:T(8,128)(2,1)S(1)}, bf16[128,256]{1,0:T(8,128)(2,1)S(1)}, u32[]{:S(2)}, u32[]{:S(2)}) collective-permute-start(bf16[128,256]{1,0:T(8,128)(2,1)S(1)} %get-tuple-element.69), channel_id=1, source_target_pairs={{0,4},{4,0},{8,12},{12,8},{16,20},{20,16},{24,28},{28,24},{1,5},{5... | collective-permute-start | bytes 196616 | tf_op jit(solution)/shard_map/ppermute | solution.py:310
  32.4 0.9 %add_head.3.refs_4_ = f32[128,4096]{1,0:T(8,128)S(1)} custom-call(s32[1]{0:T(128)} %bitcast.place_ref.refs_0_, f32[128,2048]{1,0:T(8,128)S(1)} %get-tuple-element.58.refs_1_, f32[128,2048]{1,0:T(8,128)S(1)} %get-tuple-element.59.refs_2_, bf16[2048,4096]{1,0:T(8,128)(2,1)S(1)} %bitcast.3, bf16[128,256]{1,0:T(8,128)(2,1)S(1)} %get-tuple-element.60.refs_4_, ...), custom_call_target="tpu_custom_call" | custom-call | tf_op jit(solution)/shard_map/add_head/pallas_call | solution.py:474
  33.6 0.9 %add_head.4.refs_4_ = f32[128,4096]{1,0:T(8,128)S(1)} custom-call(s32[1]{0:T(128)} %bitcast.place_ref.refs_0_, f32[128,2048]{1,0:T(8,128)S(1)} %get-tuple-element.58.refs_1_, f32[128,2048]{1,0:T(8,128)S(1)} %get-tuple-element.59.refs_2_, bf16[2048,4096]{1,0:T(8,128)(2,1)S(1)} %bitcast.3, f32[128,4096]{1,0:T(8,128)S(1)} %add_head.3.refs_4_, ...), custom_call_target="tpu_custom_call" | custom-call | tf_op jit(solution)/shard_map/add_head/pallas_call | solution.py:474
  34.7 0.9 %add_head.5.refs_4_.refs_1_ = f32[128,4096]{1,0:T(8,128)S(1)} custom-call(s32[1]{0:T(128)} %bitcast.place_ref.refs_0_, f32[128,2048]{1,0:T(8,128)S(1)} %get-tuple-element.58.refs_1_, f32[128,2048]{1,0:T(8,128)S(1)} %get-tuple-element.59.refs_2_, bf16[2048,4096]{1,0:T(8,128)(2,1)S(1)} %bitcast.3, f32[128,4096]{1,0:T(8,128)S(1)} %add_head.4.refs_4_, ...), custom_call_target="tpu_custom_call" | custom-call | tf_op jit(solution)/shard_map/add_head/pallas_call | solution.py:474
  38.1 1.6 %collective-permute-start.15 = (bf16[32,1536]{1,0:T(8,128)(2,1)S(1)}, bf16[32,1536]{1,0:T(8,128)(2,1)S(1)}, u32[]{:S(2)}, u32[]{:S(2)}) collective-permute-start(bf16[32,1536]{1,0:T(8,128)(2,1)S(1)} %slice.31), channel_id=1, source_target_pairs={{0,2},{1,3},{2,0},{3,1},{4,6},{5,7},{6,4},{7,5},{8,10},{9,11},{10,... | collective-permute-start | bytes 294920 | tf_op jit(solution)/shard_map/ppermute | solution.py:310
  39.8 0.9 %collective-permute-start.17 = (bf16[32,2560]{1,0:T(8,128)(2,1)S(1)}, bf16[32,2560]{1,0:T(8,128)(2,1)S(1)}, u32[]{:S(2)}, u32[]{:S(2)}) collective-permute-start(bf16[32,2560]{1,0:T(8,128)(2,1)S(1)} %slice.30), channel_id=1, source_target_pairs={{0,2},{1,3},{2,0},{3,1},{4,6},{5,7},{6,4},{7,5},{8,10},{9,11},{10,... | collective-permute-start | bytes 491528 | tf_op jit(solution)/shard_map/ppermute | solution.py:310
  40.7 3.1 %collective-permute-done.15 = bf16[32,1536]{1,0:T(8,128)(2,1)S(1)} collective-permute-done((bf16[32,1536]{1,0:T(8,128)(2,1)S(1)}, bf16[32,1536]{1,0:T(8,128)(2,1)S(1)}, u32[]{:S(2)}, u32[]{:S(2)}) %collective-permute-start.15) | collective-permute-done | bytes 98336 | tf_op jit(solution)/shard_map/ppermute | solution.py:310
  43.8 2.7 %collective-permute-done.17 = bf16[32,2560]{1,0:T(8,128)(2,1)S(1)} collective-permute-done((bf16[32,2560]{1,0:T(8,128)(2,1)S(1)}, bf16[32,2560]{1,0:T(8,128)(2,1)S(1)}, u32[]{:S(2)}, u32[]{:S(2)}) %collective-permute-start.17) | collective-permute-done | bytes 163872 | tf_op jit(solution)/shard_map/ppermute | solution.py:310
  46.6 0.7 %pad_maximum_fusion = bf16[32,4096]{1,0:T(8,128)(2,1)} fusion(bf16[32,2560]{1,0:T(8,128)(2,1)S(1)} %fusion, bf16[32,1536]{1,0:T(8,128)(2,1)S(1)} %fusion.1), kind=kLoop, calls=%fused_computation.5 | loop fusion | flops 524288 | bytes 524288 | tf_op jit(solution)/shard_map/concatenate | solution.py:510
  (41 shorter events, 5.9 us)
Async XLA Ops:
  1.4 9.5 %collective-permute-start = (bf16[272,256]{1,0:T(8,128)(2,1)S(1)}, bf16[272,256]{1,0:T(8,128)(2,1)S(1)}, u32[]{:S(2)}, u32[]{:S(2)}) collective-permute-start(bf16[272,256]{1,0:T(8,128)(2,1)S(1)} %get-tuple-element.41), channel_id=1, source_target_pairs={{0,4},{4,0},{8,12},{12,8},{16,20},{20,16},{24,28},{28,24},{1,5},{5... | collective-permute-start | bytes 417800 | tf_op jit(solution)/shard_map/ppermute | solution.py:310
  4.4 6.7 %collective-permute-start.1 = (bf16[272,256]{1,0:T(8,128)(2,1)S(1)}, bf16[272,256]{1,0:T(8,128)(2,1)S(1)}, u32[]{:S(2)}, u32[]{:S(2)}) collective-permute-start(bf16[272,256]{1,0:T(8,128)(2,1)S(1)} %get-tuple-element.42), channel_id=1, source_target_pairs={{0,8},{4,12},{8,0},{12,4},{16,24},{20,28},{24,16},{28,20},{1,9},{5... | collective-permute-start | bytes 417800 | tf_op jit(solution)/shard_map/ppermute | solution.py:310
  6.0 7.6 %collective-permute-start.2 = (bf16[272,256]{1,0:T(8,128)(2,1)S(1)}, bf16[272,256]{1,0:T(8,128)(2,1)S(1)}, u32[]{:S(2)}, u32[]{:S(2)}) collective-permute-start(bf16[272,256]{1,0:T(8,128)(2,1)S(1)} %get-tuple-element.43), channel_id=1, source_target_pairs={{0,12},{4,8},{8,4},{12,0},{16,28},{20,24},{24,20},{28,16},{1,13},{... | collective-permute-start | bytes 417800 | tf_op jit(solution)/shard_map/ppermute | solution.py:310
  7.3 11.6 %collective-permute-start.4 = (bf16[256,256]{1,0:T(8,128)(2,1)S(1)}, bf16[256,256]{1,0:T(8,128)(2,1)S(1)}, u32[]{:S(2)}, u32[]{:S(2)}) collective-permute-start(bf16[256,256]{1,0:T(8,128)(2,1)S(1)} %get-tuple-element.49), channel_id=1, source_target_pairs={{0,4},{4,0},{8,12},{12,8},{16,20},{20,16},{24,28},{28,24},{1,5},{5... | collective-permute-start | bytes 393224 | tf_op jit(solution)/shard_map/ppermute | solution.py:310
  9.3 9.7 %collective-permute-start.5 = (bf16[256,256]{1,0:T(8,128)(2,1)S(1)}, bf16[256,256]{1,0:T(8,128)(2,1)S(1)}, u32[]{:S(2)}, u32[]{:S(2)}) collective-permute-start(bf16[256,256]{1,0:T(8,128)(2,1)S(1)} %get-tuple-element.50), channel_id=1, source_target_pairs={{0,8},{4,12},{8,0},{12,4},{16,24},{20,28},{24,16},{28,20},{1,9},{5... | collective-permute-start | bytes 393224 | tf_op jit(solution)/shard_map/ppermute | solution.py:310
  10.8 8.5 %collective-permute-start.6 = (bf16[256,256]{1,0:T(8,128)(2,1)S(1)}, bf16[256,256]{1,0:T(8,128)(2,1)S(1)}, u32[]{:S(2)}, u32[]{:S(2)}) collective-permute-start(bf16[256,256]{1,0:T(8,128)(2,1)S(1)} %get-tuple-element.51), channel_id=1, source_target_pairs={{0,12},{4,8},{8,4},{12,0},{16,28},{20,24},{24,20},{28,16},{1,13},{... | collective-permute-start | bytes 393224 | tf_op jit(solution)/shard_map/ppermute | solution.py:310
  13.5 18.9 %slice-start = ((s8[16777216]{0:T(1024)(128)(4,1)}), s8[4194304]{0:T(1024)(128)(4,1)S(1)}, s32[]{:S(2)}) async-start(s8[16777216]{0:T(1024)(128)(4,1)} %bitcast.2), calls=%async_computation | async-start | bytes 8388608
  13.5 18.9 %slice-start.1 = ((s8[16777216]{0:T(1024)(128)(4,1)}), s8[4194304]{0:T(1024)(128)(4,1)S(1)}, s32[]{:S(2)}) async-start(s8[16777216]{0:T(1024)(128)(4,1)} %bitcast.2), calls=%async_computation.1 | async-start | bytes 8388608
  13.8 9.2 %collective-permute-start.3 = (bf16[256,256]{1,0:T(8,128)(2,1)S(1)}, bf16[256,256]{1,0:T(8,128)(2,1)S(1)}, u32[]{:S(2)}, u32[]{:S(2)}) collective-permute-start(bf16[256,256]{1,0:T(8,128)(2,1)S(1)} %get-tuple-element.46), channel_id=1, source_target_pairs={{0,16},{4,20},{8,24},{12,28},{16,0},{20,4},{24,8},{28,12},{1,17},{... | collective-permute-start | bytes 393224 | tf_op jit(solution)/shard_map/ppermute | solution.py:319
  19.4 13.0 %slice-start.2 = ((s8[16777216]{0:T(1024)(128)(4,1)}), s8[4194304]{0:T(1024)(128)(4,1)S(1)}, s32[]{:S(2)}) async-start(s8[16777216]{0:T(1024)(128)(4,1)} %bitcast.2), calls=%async_computation.2 | async-start | bytes 8388608
  19.4 13.0 %slice-start.3 = ((s8[16777216]{0:T(1024)(128)(4,1)}), s8[4194304]{0:T(1024)(128)(4,1)S(1)}, s32[]{:S(2)}) async-start(s8[16777216]{0:T(1024)(128)(4,1)} %bitcast.2), calls=%async_computation.3 | async-start | bytes 8388608
  19.7 8.9 %collective-permute-start.10 = (bf16[256,256]{1,0:T(8,128)(2,1)S(1)}, bf16[256,256]{1,0:T(8,128)(2,1)S(1)}, u32[]{:S(2)}, u32[]{:S(2)}) collective-permute-start(bf16[256,256]{1,0:T(8,128)(2,1)S(1)} %second_state.1), channel_id=1, source_target_pairs={{0,16},{4,20},{8,24},{12,28},{16,0},{20,4},{24,8},{28,12},{1,17},{... | collective-permute-start | bytes 393224 | tf_op jit(solution)/shard_map/ppermute | solution.py:319
  23.3 8.4 %collective-permute-start.7 = (bf16[128,256]{1,0:T(8,128)(2,1)S(1)}, bf16[128,256]{1,0:T(8,128)(2,1)S(1)}, u32[]{:S(2)}, u32[]{:S(2)}) collective-permute-start(bf16[128,256]{1,0:T(8,128)(2,1)S(1)} %get-tuple-element.55), channel_id=1, source_target_pairs={{0,4},{4,0},{8,12},{12,8},{16,20},{20,16},{24,28},{28,24},{1,5},{5... | collective-permute-start | bytes 196616 | tf_op jit(solution)/shard_map/ppermute | solution.py:310
  26.5 5.9 %collective-permute-start.8 = (bf16[128,256]{1,0:T(8,128)(2,1)S(1)}, bf16[128,256]{1,0:T(8,128)(2,1)S(1)}, u32[]{:S(2)}, u32[]{:S(2)}) collective-permute-start(bf16[128,256]{1,0:T(8,128)(2,1)S(1)} %get-tuple-element.56), channel_id=1, source_target_pairs={{0,8},{4,12},{8,0},{12,4},{16,24},{20,28},{24,16},{28,20},{1,9},{5... | collective-permute-start | bytes 196616 | tf_op jit(solution)/shard_map/ppermute | solution.py:310
  27.2 5.2 %collective-permute-start.9 = (bf16[128,256]{1,0:T(8,128)(2,1)S(1)}, bf16[128,256]{1,0:T(8,128)(2,1)S(1)}, u32[]{:S(2)}, u32[]{:S(2)}) collective-permute-start(bf16[128,256]{1,0:T(8,128)(2,1)S(1)} %get-tuple-element.57), channel_id=1, source_target_pairs={{0,12},{4,8},{8,4},{12,0},{16,28},{20,24},{24,20},{28,16},{1,13},{... | collective-permute-start | bytes 196616 | tf_op jit(solution)/shard_map/ppermute | solution.py:310
  28.8 4.8 %collective-permute-start.11 = (bf16[128,256]{1,0:T(8,128)(2,1)S(1)}, bf16[128,256]{1,0:T(8,128)(2,1)S(1)}, u32[]{:S(2)}, u32[]{:S(2)}) collective-permute-start(bf16[128,256]{1,0:T(8,128)(2,1)S(1)} %get-tuple-element.65), channel_id=1, source_target_pairs={{0,8},{4,12},{8,0},{12,4},{16,24},{20,28},{24,16},{28,20},{1,9},{5... | collective-permute-start | bytes 196616 | tf_op jit(solution)/shard_map/ppermute | solution.py:310
  29.1 5.6 %collective-permute-start.12 = (bf16[128,256]{1,0:T(8,128)(2,1)S(1)}, bf16[128,256]{1,0:T(8,128)(2,1)S(1)}, u32[]{:S(2)}, u32[]{:S(2)}) collective-permute-start(bf16[128,256]{1,0:T(8,128)(2,1)S(1)} %get-tuple-element.67), channel_id=1, source_target_pairs={{0,12},{4,8},{8,4},{12,0},{16,28},{20,24},{24,20},{28,16},{1,13},{... | collective-permute-start | bytes 196616 | tf_op jit(solution)/shard_map/ppermute | solution.py:310
  31.8 4.3 %collective-permute-start.13 = (bf16[128,256]{1,0:T(8,128)(2,1)S(1)}, bf16[128,256]{1,0:T(8,128)(2,1)S(1)}, u32[]{:S(2)}, u32[]{:S(2)}) collective-permute-start(bf16[128,256]{1,0:T(8,128)(2,1)S(1)} %get-tuple-element.69), channel_id=1, source_target_pairs={{0,4},{4,0},{8,12},{12,8},{16,20},{20,16},{24,28},{28,24},{1,5},{5... | collective-permute-start | bytes 196616 | tf_op jit(solution)/shard_map/ppermute | solution.py:310
  36.6 1.5 %collective-permute-start.14 = (bf16[64,1536]{1,0:T(8,128)(2,1)S(1)}, bf16[64,1536]{1,0:T(8,128)(2,1)S(1)}, u32[]{:S(2)}, u32[]{:S(2)}) collective-permute-start(bf16[64,1536]{1,0:T(8,128)(2,1)S(1)} %get-tuple-element.71), channel_id=1, source_target_pairs={{0,1},{1,0},{2,3},{3,2},{4,5},{5,4},{6,7},{7,6},{8,9},{9,8},{10,11... | collective-permute-start | bytes 589832 | tf_op jit(solution)/shard_map/ppermute | solution.py:310
  37.2 2.6 %collective-permute-start.16 = (bf16[64,2560]{1,0:T(8,128)(2,1)S(1)}, bf16[64,2560]{1,0:T(8,128)(2,1)S(1)}, u32[]{:S(2)}, u32[]{:S(2)}) collective-permute-start(bf16[64,2560]{1,0:T(8,128)(2,1)S(1)} %get-tuple-element.74), channel_id=1, source_target_pairs={{0,1},{1,0},{2,3},{3,2},{4,5},{5,4},{6,7},{7,6},{8,9},{9,8},{10,11... | collective-permute-start | bytes 983048 | tf_op jit(solution)/shard_map/ppermute | solution.py:310
  38.1 5.7 %collective-permute-start.15 = (bf16[32,1536]{1,0:T(8,128)(2,1)S(1)}, bf16[32,1536]{1,0:T(8,128)(2,1)S(1)}, u32[]{:S(2)}, u32[]{:S(2)}) collective-permute-start(bf16[32,1536]{1,0:T(8,128)(2,1)S(1)} %slice.31), channel_id=1, source_target_pairs={{0,2},{1,3},{2,0},{3,1},{4,6},{5,7},{6,4},{7,5},{8,10},{9,11},{10,... | collective-permute-start | bytes 294920 | tf_op jit(solution)/shard_map/ppermute | solution.py:310
  39.8 6.7 %collective-permute-start.17 = (bf16[32,2560]{1,0:T(8,128)(2,1)S(1)}, bf16[32,2560]{1,0:T(8,128)(2,1)S(1)}, u32[]{:S(2)}, u32[]{:S(2)}) collective-permute-start(bf16[32,2560]{1,0:T(8,128)(2,1)S(1)} %slice.30), channel_id=1, source_target_pairs={{0,2},{1,3},{2,0},{3,1},{4,6},{5,7},{6,4},{7,5},{8,10},{9,11},{10,... | collective-permute-start | bytes 491528 | tf_op jit(solution)/shard_map/ppermute | solution.py:310
